TPU v7x, 32 devices: a whole 2x2x4 slice. The times are simulated.
32 devices in a mesh: groups: 2 (over x), blk: 8 (over z, y), dp: 2 (over core).
Axes of the slice: x: 2, y: 2, z: 4, core: 2. Of those that a mesh axis runs over, the one named last changes fastest.
Arguments:
- tokens: bfloat16 [4096, 16384], P(('groups', 'blk', 'dp')), parts along dimension 0, may hold values from -6 to 6
- gain: bfloat16 [16384], replicated, may hold values from 0.29882812 to 3
- w_query: bfloat16 [16384, 1024], P('blk', 'dp')
- w_kv: bfloat16 [16384, 256], P('blk', 'dp')
- lengths: int32 [32], P('groups'), parts along dimension 0, may hold values from 1 to 1024, 2048 in all
- overlong: int32 [32], P('groups'), parts along dimension 0, may hold values 0 or 1
- assign: int32 [32], P('groups'), parts along dimension 0, may hold values from 0 to 15, as said below
Outputs:
- attended: bfloat16 [4096, 1024], P(('groups', 'blk', 'dp')), parts along dimension 0
There are 2 independent parts, one for each index of `groups`. A program takes and returns all parts, laid end to end along the dimension named above; an argument that names none is the same for every part. Nothing has to cross between parts.
Inputs may be any that keep to these rules, and one draw needn't show every extreme that they name: `assign`: each aligned run of 2 entries holds the numbers of the row blocks of that same run, each once.
All inputs are finite; a program needn't handle non-finite values.
Results may differ from a plain program's by a relative error of at most 0.0024.
The roundings to bfloat16 on the way count: a program that leaves them out, or rounds other values in their place, can miss the bound.
Values may be sent and summed in bfloat16 or wider, within the bound.
No kernel may reach another device: no remote copies, remote signals or barrier semaphores. Data moves between devices by JAX's collectives and lax.ppermute only.
A program may use at most 128 MiB of HBM per device.

v0:
```python
import jax
import jax.numpy as jnp
from jax import lax
from jax.sharding import PartitionSpec as P

HEAD = 128
BLOCK = 128


def partner_2(block, axis, apart):
    count = lax.axis_size(axis)
    route = []
    for low in range(count):
        high = low | 1 << apart
        if high != low and high < count:
            route += [(low, high), (high, low)]
    return lax.ppermute(block, axis, route)


def rollout_info(positions, lengths, overlong):
    ends = jnp.cumsum(lengths)
    starts = ends - lengths
    which = jnp.sum((ends[None, :] <= positions[:, None]).astype(jnp.int32), axis=1)
    match = jnp.arange(lengths.shape[0], dtype=jnp.int32)[None, :] == which[:, None]
    offset = positions - jnp.sum(jnp.where(match, starts[None, :], 0), axis=1)
    masked = jnp.sum(jnp.where(match, overlong[None, :], 0), axis=1)
    return (which, offset, masked)


def rotate(vectors, offset):
    half = vectors.shape[-1] // 2
    freqs = jnp.power(
        jnp.float32(500000.0), -jnp.arange(half, dtype=jnp.float32) * 2.0 / vectors.shape[-1]
    )
    angle = offset.astype(jnp.float32)[:, None] * freqs[None, :]
    cosine = jnp.cos(angle)[:, None, :]
    sine = jnp.sin(angle)[:, None, :]
    first = vectors[..., :half]
    second = vectors[..., half:]
    return jnp.concatenate(
        [first * cosine - second * sine, second * cosine + first * sine], axis=-1
    )


def normalize(tokens, gain):
    widened = tokens.astype(jnp.float32)
    factor = lax.rsqrt(jnp.mean(widened * widened, axis=1, keepdims=True) + 1e-05)
    return (widened * factor * gain.astype(jnp.float32)[None, :]).astype(jnp.bfloat16)


def attend_rows(query, row_places, heads, keyval, key_places, lengths, overlong):
    rows = row_places.shape[0]
    which, offset, masked = rollout_info(row_places, lengths, overlong)
    query_which = jnp.repeat(which, heads)
    query_place = jnp.repeat(row_places, heads)
    ends = jnp.cumsum(lengths)
    pair_vals = lax.all_gather(keyval, "blk", axis=0, tiled=True)
    key_place = lax.all_gather(key_places, "blk", axis=0, tiled=True)
    largest = jnp.full((rows * heads,), -1e30, jnp.float32)
    key_which = jnp.sum((ends[None, :] <= key_place[:, None]).astype(jnp.int32), axis=1)
    scores = lax.dot_general(
        query, pair_vals[:, :HEAD], (((1,), (1,)), ((), ())), preferred_element_type=jnp.float32
    ) * HEAD ** (-0.5)
    valid = (query_which[:, None] == key_which[None, :]) & (
        key_place[None, :] <= query_place[:, None]
    )
    newest = jnp.maximum(largest, jnp.max(jnp.where(valid, scores, -1e30), axis=1))
    weights = jnp.where(valid, jnp.exp(scores - newest[:, None]), 0.0)
    total = jnp.sum(weights, axis=1)
    summed = jnp.dot(
        weights.astype(jnp.bfloat16), pair_vals[:, HEAD:], preferred_element_type=jnp.float32
    )
    largest, total, summed = (newest, total, summed)
    out = (summed / total[:, None]).reshape(rows, heads * HEAD)
    return jnp.where(masked[:, None] == 1, 0.0, out).astype(jnp.bfloat16)


def on_device(tokens, gain, w_query, w_kv, lengths, overlong, assign):
    count = tokens.shape[0]
    pair_count = 2 * count
    side = lax.axis_index("dp")
    device = lax.axis_index(("blk", "dp"))
    pair_base = (device - side) * count
    partner = partner_2(tokens, "dp", 0)
    paired = jnp.where(
        side == 0,
        jnp.concatenate([tokens, partner], axis=0),
        jnp.concatenate([partner, tokens], axis=0),
    )
    pair_rows = pair_base + jnp.arange(pair_count, dtype=jnp.int32)
    which, offset, masked = rollout_info(pair_rows, lengths, overlong)
    normed = normalize(paired, gain)
    heads_here = w_query.shape[1] // HEAD
    proj_query = jnp.dot(
        normed,
        lax.all_gather(w_query, "blk", axis=0, tiled=True),
        preferred_element_type=jnp.float32,
    )
    proj_kv = jnp.dot(
        normed, lax.all_gather(w_kv, "blk", axis=0, tiled=True), preferred_element_type=jnp.float32
    )
    query = rotate(proj_query.reshape(pair_count, heads_here, HEAD), offset).astype(jnp.bfloat16)
    turned = rotate(proj_kv.reshape(pair_count, 1, HEAD), offset).reshape(pair_count, HEAD)
    mine_kv = jnp.where(side == 0, turned, proj_kv).astype(jnp.bfloat16)
    other_kv = partner_2(mine_kv, "dp", 0)
    keyval = jnp.where(
        side == 0,
        jnp.concatenate([mine_kv, other_kv], axis=1),
        jnp.concatenate([other_kv, mine_kv], axis=1),
    )
    run_blocks = pair_count // BLOCK
    first_block = pair_base // BLOCK
    slot_blocks = lax.dynamic_slice_in_dim(assign, first_block, run_blocks) - first_block
    picked = ((slot_blocks * BLOCK)[:, None] + jnp.arange(BLOCK, dtype=jnp.int32)[None, :]).reshape(
        pair_count
    )
    out = attend_rows(
        query.reshape(pair_count * heads_here, HEAD),
        pair_rows,
        heads_here,
        keyval,
        pair_rows,
        lengths,
        overlong,
    )
    ordered = jnp.take(out, picked, axis=0)
    result = lax.all_to_all(ordered, "dp", split_axis=0, concat_axis=1, tiled=True)
    return result


def solution(mesh):
    placed = (
        P(("groups", "blk", "dp"), None),
        P(),
        P("blk", "dp"),
        P("blk", "dp"),
        P("groups"),
        P("groups"),
        P("groups"),
    )
    return jax.shard_map(
        on_device,
        mesh=mesh,
        in_specs=placed,
        out_specs=P(("groups", "blk", "dp"), None),
        check_vma=False,
    )
```

profile of v0, /device:TPU:0, one launch (start us, length us, event | category | flops | bytes accessed | tf_op | source)
XLA Modules:
  0.0 375.7 jit_solution(8824840267091017882)
XLA Ops:
  6.5 0.7 all-gather.7.cloned.1.call-update
  7.3 0.7 all-gather.5.cloned.1.call-update
  8.1 0.5 collective-permute-start
  8.6 0.7 copy.14
  9.7 0.7 sub.38
  10.7 0.8 convert_element_type.38
  11.4 22.1 %all-gather = s32[8,1,256]{2,1,0:T(1,128)S(1)} all-gather(s32[1,1,256]{2,1,0:T(1,128)S(1)} %bitcast.29), channel_id=1, replica_groups=mesh['groups'=2,'blk'=8,'dp'=2] {'blk'}, dimensions={0}, use_global_device_ids=true | all-gather | bytes 9216 | tf_op jit(solution)/shard_map/all_gather | solution.py:58
  33.5 0.7 subtract_multiply_fusion
  34.3 0.7 select_reduce_fusion.2
  35.2 0.5 multiply_cosine_fusion
  35.8 7.5 %fusion = f32[256]{0:T(256)S(1)} fusion(bf16[128,16384]{1,0:T(8,128)(2,1)} %param.7, bf16[128,16384]{1,0:T(8,128)(2,1)} %collective-permute-done, pred[]{:T(512)S(6)} %eq.60), kind=kLoop, calls=%fused_computation.3 | loop fusion | flops 50331392 | bytes 8389633 | tf_op jit(solution)/shard_map/reduce_sum | solution.py:47
  43.3 42.3 %all-gather.7.cloned.1.call-done = bf16[16384,128]{1,0:T(8,128)(2,1)} async-done(((bf16[2048,128]{1,0:T(8,128)(2,1)}), bf16[16384,128]{1,0:T(8,128)(2,1)}) %all-gather.7.cloned.1.call-update) | async-done | bytes 4194320 | tf_op jit(solution)/shard_map/all_gather | solution.py:100
  85.6 9.3 %fusion.7 = f32[256,128]{0,1:T(8,128)S(1)} fusion(bf16[16384,128]{1,0:T(8,128)(2,1)} %all-gather.7.cloned.1.call-done, f32[16384]{0:T(1024)S(1)} %convert_element_type.38, f32[256]{0:T(256)S(1)} %add_rsqrt_fusion, bf16[128,16384]{1,0:T(8,128)(2,1)} %collective-permute-done, bf16[128,16384]{1,0:T(8,128)(2,1)} %param.7, pred[]{:T(512)S(6)} %eq.60), kind=kOutput, calls=%fused_computation.13 | convolution fusion | flops 1128267776 | bytes 12780545 | tf_op jit(solution)/shard_map/dot_general | solution.py:99
  95.4 1.2 collective-permute-done.1
  96.6 0.7 maximum_select_fusion.1
  97.3 216.4 %all-gather.5.cloned.1.call-done = bf16[16384,512]{1,0:T(8,128)(2,1)} async-done(((bf16[2048,512]{1,0:T(8,128)(2,1)}), bf16[16384,512]{1,0:T(8,128)(2,1)}) %all-gather.5.cloned.1.call-update) | async-done | bytes 16777232 | tf_op jit(solution)/shard_map/all_gather | solution.py:96
  313.7 13.2 %fusion.9 = f32[256,512]{1,0:T(8,128)S(1)} fusion(bf16[16384,512]{1,0:T(8,128)(2,1)} %all-gather.5.cloned.1.call-done, f32[16384]{0:T(1024)S(1)} %convert_element_type.38, f32[256]{0:T(256)S(1)} %add_rsqrt_fusion, bf16[128,16384]{1,0:T(8,128)(2,1)} %collective-permute-done, bf16[128,16384]{1,0:T(8,128)(2,1)} %param.7, pred[]{:T(512)S(6)} %eq.60), kind=kOutput, calls=%fused_computation.14 | convolution fusion | flops 4349493248 | bytes 25756672 | tf_op jit(solution)/shard_map/dot_general | solution.py:94
  327.6 25.9 %all-gather.9.cloned.1.call-done = bf16[2048,256]{0,1:T(8,128)(2,1)} async-done(((bf16[256,256]{0,1:T(8,128)(2,1)}), bf16[2048,256]{0,1:T(8,128)(2,1)}) %all-gather.9.cloned.1.call-update) | async-done | bytes 1048592 | tf_op jit(solution)/shard_map/all_gather | solution.py:57
  353.5 3.6 select_reduce_fusion
  357.1 3.4 fusion.3
  360.5 2.4 fusion.11
  363.2 1.2 gather_fusion
  364.5 3.9 %all_to_all.16 = bf16[2,128,512]{2,1,0:T(8,128)(2,1)S(1)} all-to-all(bf16[2,128,512]{2,1,0:T(8,128)(2,1)S(1)} %broadcast_select_fusion), channel_id=1, replica_groups=mesh['groups'=2,'blk'=8,'dp'=2] {'dp'}, dimensions={0} | all-to-all | bytes 524288 | tf_op jit(solution)/shard_map/all_to_all | solution.py:127
  368.4 0.7 copy.16
  (33 shorter events, 2.5 us)
Async XLA Ops:
  6.5 79.1 %all-gather.7.cloned.1.call-start = ((), (), s32[]{:S(2)}) async-start(), calls=%async_computation.2 | async-start | bytes 4718592 | tf_op jit(solution)/shard_map/all_gather | solution.py:100
  7.3 306.4 %all-gather.5.cloned.1.call-start = ((), (), s32[]{:S(2)}) async-start(), calls=%async_computation.1 | async-start | bytes 18874368 | tf_op jit(solution)/shard_map/all_gather | solution.py:96
  8.0 345.5 %all-gather.9.cloned.1.call-start = ((), (), s32[]{:S(2)}) async-start(), calls=%async_computation.3 | async-start | bytes 1179648 | tf_op jit(solution)/shard_map/all_gather | solution.py:57
  8.1 27.7 %collective-permute-start = (bf16[128,16384]{1,0:T(8,128)(2,1)}, bf16[128,16384]{1,0:T(8,128)(2,1)}, u32[]{:S(2)}, u32[]{:S(2)}) collective-permute-start(bf16[128,16384]{1,0:T(8,128)(2,1)} %param.7), channel_id=1, source_target_pairs={{0,1},{1,0},{2,3},{3,2},{4,5},{5,4},{6,7},{7,6},{8,9},{9,8},{10,11... | collective-permute-start | bytes 12582920 | tf_op jit(solution)/shard_map/ppermute | solution.py:17
  95.3 1.3 collective-permute-start.1
  357.1 3.5 copy-start
Sparse Core Ops, SparseCore 0:
  9.5 76.1 all-gather.6
  87.8 225.8 all-gather.4
  315.7 37.7 all-gather.8
where the time goes:
time: 376 us
  waiting for transfers between devices  287 us (76%)
  matrix products  28.4 us (8%)
  blocking collectives  26 us (7%)
  other arithmetic  16.7 us (4%)
  between operations  13.3 us (4%)
    all_gather x1, waiting for transfers between devices, on_device(): lax.all_gather(w_query, 'blk', axis=0, tiled=True)  216 us
    all_gather x1, waiting for transfers between devices, on_device(): lax.all_gather(w_kv, 'blk', axis=0, tiled=True)  42.3 us
    all_gather x1, waiting for transfers between devices, attend_rows(): pair_vals = lax.all_gather(keyval, 'blk', axis=0, tiled=True)  25.9 us
    all_gather x1, blocking collectives, attend_rows(): key_place = lax.all_gather(key_places, 'blk', axis=0, tiled=True)  22.1 us
    dot_general x1, matrix products, on_device(): jnp.dot(normed, lax.all_gather(w_query, 'blk', axis=0, tiled=True), prefe...  13.2 us
    dot_general x1, matrix products, on_device(): jnp.dot(normed, lax.all_gather(w_kv, 'blk', axis=0, tiled=True), preferre...  9.27 us
    reduce_sum x1, other arithmetic, normalize(): jnp.mean(widened * widened, axis=1, keepdims=True) + 1e-05  7.54 us
  transfers between devices with their start and end apart: 5, of which 4 were waited for; matrix products, arithmetic and copies ran while one was open for 10% of the time, Pallas kernels for 0%

commit v1 on v0

v1 whole, which is shorter than its diff:
```python
import functools

import jax
import jax.numpy as jnp
from jax import lax
from jax.sharding import Mesh
from jax.sharding import PartitionSpec as P

HEAD = 128
BLOCK = 128
CHUNK_HEADS = (2, 1, 1)


def rollout_info(positions, lengths, overlong):
    ends = jnp.cumsum(lengths)
    starts = ends - lengths
    which = jnp.sum((ends[None, :] <= positions[:, None]).astype(jnp.int32), axis=1)
    match = jnp.arange(lengths.shape[0], dtype=jnp.int32)[None, :] == which[:, None]
    offset = positions - jnp.sum(jnp.where(match, starts[None, :], 0), axis=1)
    masked = jnp.sum(jnp.where(match, overlong[None, :], 0), axis=1)
    return (which, offset, masked)


def angles(offset):
    half = HEAD // 2
    freqs = jnp.power(
        jnp.float32(500000.0), -jnp.arange(half, dtype=jnp.float32) * 2.0 / HEAD
    )
    angle = offset.astype(jnp.float32)[:, None] * freqs[None, :]
    return jnp.cos(angle), jnp.sin(angle)


def rotate(vectors, cosine, sine):
    half = HEAD // 2
    first = vectors[:, :half]
    second = vectors[:, half:]
    return jnp.concatenate(
        [first * cosine - second * sine, second * cosine + first * sine], axis=-1
    )


def shift_square(block, dx, dy, groups, ys):
    route = [
        (x * ys + y, (x + dx) % groups * ys + (y + dy) % ys)
        for x in range(groups)
        for y in range(ys)
    ]
    return lax.ppermute(block, ("groups", "y"), route)


def swap_core(block):
    return lax.ppermute(block, "dp", [(0, 1), (1, 0)])


def gather_line(block, zs):
    z = lax.axis_index("z")
    down, up = [block], [block]
    for step in range(1, zs):
        down.append(lax.ppermute(down[-1], "z", [(i, i - 1) for i in range(1, zs - step + 1)]))
        up.append(lax.ppermute(up[-1], "z", [(i, i + 1) for i in range(step - 1, zs - 1)]))
    return [block] + [jnp.where(z >= s, up[s], down[zs - s]) for s in range(1, zs)]


def on_device(groups, zs, ys, tokens, gain, w_query, w_kv, lengths, overlong, assign):
    count = tokens.shape[0]
    pair = 2 * count
    x, z, y, side = (lax.axis_index(name) for name in ("groups", "z", "y", "dp"))
    blk = z * ys + y
    part_rows = w_query.shape[0] // groups
    heads_here = w_query.shape[1] // HEAD
    offsets = [(dx, dy) for dx in range(groups) for dy in range(ys)]

    mine_q = lax.dynamic_slice_in_dim(w_query, x * part_rows, part_rows, 0)
    mine_kv = lax.dynamic_slice_in_dim(w_kv, x * part_rows, part_rows, 0)
    chunks = [mine_kv]
    at = 0
    for heads in CHUNK_HEADS:
        chunks.append(mine_q[:, at * HEAD : (at + heads) * HEAD])
        at += heads
    weights = [jnp.concatenate(gather_line(chunk, zs), axis=0) for chunk in chunks]

    factor = lax.rsqrt(
        jnp.mean(jnp.square(tokens.astype(jnp.float32)), axis=1, keepdims=True) + 1e-05
    )

    def columns_of(dx, dy):
        pieces = []
        for s in range(zs):
            start = (((z - s) % zs * ys + (y + dy) % ys) * groups + (x + dx) % groups) * part_rows
            part = lax.dynamic_slice_in_dim(tokens, start, part_rows, 1).astype(jnp.float32)
            scale = lax.dynamic_slice_in_dim(gain, start, part_rows, 0).astype(jnp.float32)
            pieces.append((part * factor * scale[None, :]).astype(jnp.bfloat16))
        return jnp.concatenate(pieces, axis=1)

    pieces = [shift_square(columns_of(dx, dy), dx, dy, groups, ys) if dx or dy else columns_of(0, 0) for dx, dy in offsets]
    others = [swap_core(piece) for piece in pieces]
    rows_of = [
        jnp.where(side == 0, jnp.concatenate([a, b], axis=0), jnp.concatenate([b, a], axis=0))
        for a, b in zip(pieces, others)
    ]

    def project(weight):
        total = None
        for (dx, dy), rows in zip(offsets, rows_of):
            partial = jnp.dot(rows, weight, preferred_element_type=jnp.float32)
            if dx or dy:
                partial = shift_square(partial, -dx, -dy, groups, ys)
            total = partial if total is None else total + partial
        return total

    pair_base = blk * pair
    pair_rows = pair_base + jnp.arange(pair, dtype=jnp.int32)
    which, offset, masked = rollout_info(pair_rows, lengths, overlong)
    cosine, sine = angles(offset)

    proj = project(weights[0])
    kept = jnp.where(side == 0, rotate(proj, cosine, sine), proj).astype(jnp.bfloat16)
    along = [kept] + [
        lax.ppermute(kept, "z", [(i, (i + s) % zs) for i in range(zs)]) for s in range(1, zs)
    ]
    along = jnp.concatenate(along, axis=0)
    halves = [along] + [
        lax.ppermute(along, "y", [(i, (i + s) % ys) for i in range(ys)]) for s in range(1, ys)
    ]
    here = jnp.concatenate(halves, axis=0)
    there = swap_core(here)
    key = jnp.where(side == 0, here, there)
    value = jnp.where(side == 0, there, here)
    key_blk = jnp.stack([(z - s) % zs * ys + (y - t) % ys for t in range(ys) for s in range(zs)])
    key_place = (
        key_blk[:, None] * pair + jnp.arange(pair, dtype=jnp.int32)[None, :]
    ).reshape(-1)
    ends = jnp.cumsum(lengths)
    key_which = jnp.sum((ends[None, :] <= key_place[:, None]).astype(jnp.int32), axis=1)
    valid = (which[:, None] == key_which[None, :]) & (key_place[None, :] <= pair_rows[:, None])

    def attend(query):
        scores = lax.dot_general(
            query, key, (((1,), (1,)), ((), ())), preferred_element_type=jnp.float32
        ) * HEAD ** (-0.5)
        newest = jnp.max(jnp.where(valid, scores, -1e30), axis=1)
        weight = jnp.where(valid, jnp.exp(scores - newest[:, None]), 0.0)
        total = jnp.sum(weight, axis=1)
        summed = jnp.dot(weight.astype(jnp.bfloat16), value, preferred_element_type=jnp.float32)
        out = summed / total[:, None]
        return jnp.where(masked[:, None] == 1, 0.0, out).astype(jnp.bfloat16)

    first = pair_base // BLOCK
    slots = lax.dynamic_slice_in_dim(assign, first, 2) - first
    own_slot = lax.dynamic_index_in_dim(slots, side, keepdims=False)
    other_slot = lax.dynamic_index_in_dim(slots, 1 - side, keepdims=False)
    kept_out, got_out = [], []
    for heads, weight in zip(CHUNK_HEADS, weights[1:]):
        proj = project(weight)
        outs = []
        for head in range(heads):
            query = rotate(proj[:, head * HEAD : (head + 1) * HEAD], cosine, sine)
            outs.append(attend(query.astype(jnp.bfloat16)))
        outs = jnp.concatenate(outs, axis=1)
        kept_out.append(lax.dynamic_slice_in_dim(outs, own_slot * BLOCK, BLOCK, 0))
        got_out.append(swap_core(lax.dynamic_slice_in_dim(outs, other_slot * BLOCK, BLOCK, 0)))
    kept_out = jnp.concatenate(kept_out, axis=1)
    got_out = jnp.concatenate(got_out, axis=1)
    return jnp.where(
        side == 0,
        jnp.concatenate([kept_out, got_out], axis=1),
        jnp.concatenate([got_out, kept_out], axis=1),
    )


def solution(mesh):
    groups, blks, cores = (mesh.shape[name] for name in ("groups", "blk", "dp"))
    ys = 2
    zs = blks // ys
    fine = Mesh(mesh.devices.reshape(groups, zs, ys, cores), ("groups", "z", "y", "dp"))
    placed = (
        P(("groups", "z", "y", "dp"), None),
        P(),
        P(("z", "y"), "dp"),
        P(("z", "y"), "dp"),
        P("groups"),
        P("groups"),
        P("groups"),
    )
    return jax.shard_map(
        functools.partial(on_device, groups, zs, ys),
        mesh=fine,
        in_specs=placed,
        out_specs=P(("groups", "z", "y", "dp"), None),
        check_vma=False,
    )
```

time: 376 us -> 227 us (0.60)
  waiting for transfers between devices: 287 us -> 84.7 us
  starting transfers between devices: 0.67 us -> 75.6 us
  blocking collectives: 26 us -> 0 us
  other arithmetic: 16.7 us -> 32 us
  between operations: 13.3 us -> 2.5 us
  matrix products: 28.4 us -> 24.5 us
    all_gather x3 -> x0, waiting for transfers between devices: 285 us -> none  [the longest x1 216 us: on_device(): lax.all_gather(w_query, 'blk', axis=0, tiled=True)]
    ppermute x2 -> x51, waiting for transfers between devices: 1.23 us -> 84.7 us  [the longest x15 36.5 us: shift_square(): return lax.ppermute(block, ('groups', 'y'), route)]
    ppermute x2 -> x51, starting transfers between devices: 0.59 us -> 75.6 us  [the longest x12 37.4 us: gather_line(): lax.ppermute(up[-1], 'z', [(i, i + 1) for i in range(step - 1, zs - 1)])]
    all_gather x1 -> x0, blocking collectives: 22.1 us -> none  [attend_rows(): key_place = lax.all_gather(key_places, 'blk', axis=0, tiled=True)]
    select_n x3 -> x18, other arithmetic: 0.79 us -> 19.6 us  [the longest x4 14.3 us: on_device(): jnp.where(side == 0, jnp.concatenate([a, b], axis=0), jnp.concatenate([b,...]
    reduce_sum x3, other arithmetic: 11.1 us -> 4.4 us  [the longest x1 3.1 us: on_device(): jnp.mean(jnp.square(tokens.astype(jnp.float32)), axis=1, keepdims=True)]
    all_to_all x1 -> x0, blocking collectives: 3.94 us -> none  [on_device(): lax.all_to_all(ordered, 'dp', split_axis=0, concat_axis=1, tiled=True)]
    dot_general x4 -> x24, matrix products: 28.4 us -> 24.5 us  [the longest x16 17.9 us: project(): partial = jnp.dot(rows, weight, preferred_element_type=jnp.float32)]
  transfers between devices with their start and end apart: 5 -> 51, of which waited for: 4 -> 13; matrix products, arithmetic and copies ran while one was open for 10% -> 21% of each run, Pallas kernels for 0% -> 0%
where the time goes in v1:
time: 227 us; the launch traced here: 225 us
  waiting for transfers between devices  84.7 us (37%)
  starting transfers between devices  75.6 us (33%)
  other arithmetic  32 us (14%)
  matrix products  24.5 us (11%)
  local copies, waits for them, and re-layouts  6.11 us (3%)
  between operations  2.5 us (1%)
    ppermute x12, starting transfers between devices, gather_line(): lax.ppermute(up[-1], 'z', [(i, i + 1) for i in range(step - 1, zs - 1)])  37.4 us
    ppermute x15, waiting for transfers between devices, shift_square(): return lax.ppermute(block, ('groups', 'y'), route)  36.5 us
    ppermute x12, waiting for transfers between devices, gather_line(): lax.ppermute(down[-1], 'z', [(i, i - 1) for i in range(1, zs - step + 1)])  31.1 us
    ppermute x15, starting transfers between devices, shift_square(): return lax.ppermute(block, ('groups', 'y'), route)  21.2 us
    dot_general x16, matrix products, project(): partial = jnp.dot(rows, weight, preferred_element_type=jnp.float32)  17.9 us
    ppermute x12, starting transfers between devices, gather_line(): lax.ppermute(down[-1], 'z', [(i, i - 1) for i in range(1, zs - step + 1)])  15.6 us
    select_n x4, other arithmetic, on_device(): jnp.where(side == 0, jnp.concatenate([a, b], axis=0), jnp.concatenate([b,...  14.3 us
    ppermute x1, waiting for transfers between devices, on_device(): lax.ppermute(along, 'y', [(i, (i + s) % ys) for i in range(ys)])  11.7 us
  transfers between devices with their start and end apart: 51, of which 13 were waited for; matrix products, arithmetic and copies ran while one was open for 21% of the time, Pallas kernels for 0%

profile of v1, /device:TPU:0, one launch (start us, length us, event | category | flops | bytes accessed | tf_op | source)
XLA Modules:
  0.0 225.5 jit_solution(6391364126100853277)
XLA Ops:
  2.4 6.3 %collective-permute-start.16 = (bf16[1024,128]{1,0:T(8,128)(2,1)S(1)}, bf16[1024,128]{1,0:T(8,128)(2,1)}, u32[]{:S(2)}, u32[]{:S(2)}) collective-permute-start(bf16[1024,128]{1,0:T(8,128)(2,1)S(1)} %constant_dynamic-slice_fusion.3), channel_id=1, source_target_pairs={{0,4},{4,8},{8,12},{1,5},{5,9},{9,13},{2,6},{6,10},{10,14},{3,7},{... | collective-permute-start | bytes 786440 | tf_op jit(solution)/shard_map/ppermute | solution.py:60
  11.7 5.3 %collective-permute-start.30 = (bf16[1024,128]{1,0:T(8,128)(2,1)S(1)}, bf16[1024,128]{1,0:T(8,128)(2,1)}, u32[]{:S(2)}, u32[]{:S(2)}) collective-permute-start(bf16[1024,128]{1,0:T(8,128)(2,1)S(1)} %get-tuple-element.33), channel_id=1, source_target_pairs={{0,4},{4,8},{8,12},{1,5},{5,9},{9,13},{2,6},{6,10},{10,14},{3,7},{... | collective-permute-start | bytes 786440 | tf_op jit(solution)/shard_map/ppermute | solution.py:60
  18.5 3.1 %multiply_reduce_fusion = f32[128]{0:T(128)S(1)} fusion(bf16[128,16384]{1,0:T(8,128)(2,1)} %param.7), kind=kLoop, calls=%fused_computation | loop fusion | flops 6291328 | bytes 4194816 | tf_op jit(solution)/shard_map/reduce_sum | solution.py:83
  22.4 2.4 %multiply_convert_fusion.11 = (bf16[128,1024]{1,0:T(8,128)(2,1)S(1)}, bf16[128,1024]{1,0:T(8,128)(2,1)S(1)}, bf16[128,1024]{1,0:T(8,128)(2,1)S(1)}, bf16[128,102...) fusion(f32[1024]{0:T(1024)S(1)} %get-tuple-element.53, ...), kind=kLoop, calls=%fused_computation.65 | loop fusion | flops 4194304 | bytes 4227616 | tf_op jit(solution)/shard_map/convert_element_type | solution.py:92
  29.2 5.3 %collective-permute-start.39 = (bf16[1024,128]{1,0:T(8,128)(2,1)}, bf16[1024,128]{1,0:T(8,128)(2,1)}, u32[]{:S(2)}, u32[]{:S(2)}) collective-permute-start(bf16[1024,128]{1,0:T(8,128)(2,1)} %get-tuple-element.34), channel_id=1, source_target_pairs={{0,4},{4,8},{8,12},{1,5},{5,9},{9,13},{2,6},{6,10},{10,14},{3,7},{... | collective-permute-start | bytes 786440 | tf_op jit(solution)/shard_map/ppermute | solution.py:60
  47.3 3.0 %collective-permute-done.32 = bf16[1024,128]{1,0:T(8,128)(2,1)} collective-permute-done((bf16[1024,128]{1,0:T(8,128)(2,1)}, bf16[1024,128]{1,0:T(8,128)(2,1)}, u32[]{:S(2)}, u32[]{:S(2)}) %collective-permute-start.32) | collective-permute-done | bytes 262176 | tf_op jit(solution)/shard_map/ppermute | solution.py:59
  51.5 13.6 %collective-permute-start.1 = (bf16[1024,256]{1,0:T(8,128)(2,1)S(1)}, bf16[1024,256]{1,0:T(8,128)(2,1)S(1)}, u32[]{:S(2)}, u32[]{:S(2)}) collective-permute-start(bf16[1024,256]{1,0:T(8,128)(2,1)S(1)} %constant_dynamic-slice_fusion), channel_id=1, source_target_pairs={{0,4},{4,8},{8,12},{1,5},{5,9},{9,13},{2,6},{6,10},{10,14},{3,7},{... | collective-permute-start | bytes 1572872 | tf_op jit(solution)/shard_map/ppermute | solution.py:60
  69.0 9.9 %collective-permute-done.2 = bf16[1024,256]{1,0:T(8,128)(2,1)S(1)} collective-permute-done((bf16[1024,256]{1,0:T(8,128)(2,1)S(1)}, bf16[1024,256]{1,0:T(8,128)(2,1)S(1)}, u32[]{:S(2)}, u32[]{:S(2)}) %collective-permute-start.2) | collective-permute-done | bytes 524320 | tf_op jit(solution)/shard_map/ppermute | solution.py:59
  85.0 7.2 %collective-permute-done.42 = bf16[1024,128]{1,0:T(8,128)(2,1)S(1)} collective-permute-done((bf16[1024,128]{1,0:T(8,128)(2,1)S(1)}, bf16[1024,128]{1,0:T(8,128)(2,1)S(1)}, u32[]{:S(2)}, u32[]{:S(2)}) %collective-permute-start.42) | collective-permute-done | bytes 262176 | tf_op jit(solution)/shard_map/ppermute | solution.py:59
  96.2 11.0 %collective-permute-done.3 = bf16[1024,256]{1,0:T(8,128)(2,1)S(1)} collective-permute-done((bf16[1024,256]{1,0:T(8,128)(2,1)S(1)}, bf16[1024,256]{1,0:T(8,128)(2,1)S(1)}, u32[]{:S(2)}, u32[]{:S(2)}) %collective-permute-start.3) | collective-permute-done | bytes 524320 | tf_op jit(solution)/shard_map/ppermute | solution.py:59
  109.5 13.0 %collective-permute-done.13 = bf16[128,4096]{1,0:T(8,128)(2,1)S(1)} collective-permute-done((bf16[128,4096]{1,0:T(8,128)(2,1)S(1)}, bf16[128,4096]{1,0:T(8,128)(2,1)S(1)}, u32[]{:S(2)}, u32[]{:S(2)}) %collective-permute-start.13) | collective-permute-done | bytes 1048608 | tf_op jit(solution)/shard_map/ppermute | solution.py:48
  122.5 12.7 %maximum_select_fusion = bf16[256,4096]{1,0:T(8,128)(2,1)S(1)} fusion(bf16[128,4096]{1,0:T(8,128)(2,1)S(1)} %collective-permute-done, bf16[128,1024]{1,0:T(8,128)(2,1)S(1)} %get-tuple-element.27, bf16[128,1024]{1,0:T(8,128)(2,1)S(1)} %get-tuple-element.28, bf16[128,1024]{1,0:T(8,128)(2,1)S(1)} %get-tuple-element.29, ...), kind=kLoop, calls=%fused_computation.5 | loop fusion | flops 22020096 | bytes 4194305 | tf_op jit(solution)/shard_map/jit(_where)/select_n | solution.py:98
  135.3 1.8 fusion.92
  137.9 7.0 %collective-permute-done.7 = bf16[128,4096]{1,0:T(8,128)(2,1)S(1)} collective-permute-done((bf16[128,4096]{1,0:T(8,128)(2,1)S(1)}, bf16[128,4096]{1,0:T(8,128)(2,1)S(1)}, u32[]{:S(2)}, u32[]{:S(2)}) %collective-permute-start.7) | collective-permute-done | bytes 1048608 | tf_op jit(solution)/shard_map/ppermute | solution.py:48
  147.6 1.8 fusion.90
  151.6 1.8 fusion.89
  170.3 2.4 %collective-permute-start.38 = (f32[256,128]{0,1:T(8,128)S(1)}, f32[256,128]{0,1:T(8,128)S(1)}, u32[]{:S(2)}, u32[]{:S(2)}) collective-permute-start(f32[256,128]{0,1:T(8,128)S(1)} %fusion.93), channel_id=1, source_target_pairs={{0,18},{2,16},{16,2},{18,0},{1,19},{3,17},{17,3},{19,1},{4,22},{6,... | collective-permute-start | bytes 393224 | tf_op jit(solution)/shard_map/ppermute | solution.py:48
  173.7 10.2 %collective-permute-done.38 = f32[256,128]{0,1:T(8,128)S(1)} collective-permute-done((f32[256,128]{0,1:T(8,128)S(1)}, f32[256,128]{0,1:T(8,128)S(1)}, u32[]{:S(2)}, u32[]{:S(2)}) %collective-permute-start.38) | collective-permute-done | bytes 131104 | tf_op jit(solution)/shard_map/ppermute | solution.py:48
  184.0 2.5 %collective-permute-start.47 = (f32[256,128]{0,1:T(8,128)S(1)}, f32[256,128]{0,1:T(8,128)S(1)}, u32[]{:S(2)}, u32[]{:S(2)}) collective-permute-start(f32[256,128]{0,1:T(8,128)S(1)} %fusion.89), channel_id=1, source_target_pairs={{0,18},{2,16},{16,2},{18,0},{1,19},{3,17},{17,3},{19,1},{4,22},{6,... | collective-permute-start | bytes 393224 | tf_op jit(solution)/shard_map/ppermute | solution.py:48
  186.5 4.1 %collective-permute-done.26 = bf16[256,128]{0,1:T(8,128)(2,1)S(1)} collective-permute-done((bf16[256,128]{0,1:T(8,128)(2,1)S(1)}, bf16[256,128]{0,1:T(8,128)(2,1)S(1)}, u32[]{:S(2)}, u32[]{:S(2)}) %collective-permute-start.26) | collective-permute-done | bytes 65568 | tf_op jit(solution)/shard_map/ppermute | solution.py:119
  192.8 2.5 %collective-permute-start.15 = (f32[256,256]{0,1:T(8,128)S(1)}, f32[256,256]{0,1:T(8,128)S(1)}, u32[]{:S(2)}, u32[]{:S(2)}) collective-permute-start(f32[256,256]{0,1:T(8,128)S(1)} %fusion.107), channel_id=1, source_target_pairs={{0,18},{2,16},{16,2},{18,0},{1,19},{3,17},{17,3},{19,1},{4,22},{6,... | collective-permute-start | bytes 786440 | tf_op jit(solution)/shard_map/ppermute | solution.py:48
  195.3 11.7 %collective-permute-done.28 = bf16[1024,128]{0,1:T(8,128)(2,1)S(1)} collective-permute-done((bf16[1024,128]{0,1:T(8,128)(2,1)S(1)}, bf16[1024,128]{0,1:T(8,128)(2,1)S(1)}, u32[]{:S(2)}, u32[]{:S(2)}) %collective-permute-start.28) | collective-permute-done | bytes 262176 | tf_op jit(solution)/shard_map/ppermute | solution.py:123
  208.8 5.4 %collective-permute-done.9 = f32[256,256]{0,1:T(8,128)S(1)} collective-permute-done((f32[256,256]{0,1:T(8,128)S(1)}, f32[256,256]{0,1:T(8,128)S(1)}, u32[]{:S(2)}, u32[]{:S(2)}) %collective-permute-start.9) | collective-permute-done | bytes 262176 | tf_op jit(solution)/shard_map/ppermute | solution.py:48
  216.6 1.8 fusion.6
  (198 shorter events, 77.2 us)
Async XLA Ops:
  1.1 28.1 %collective-permute-start.17 = (bf16[1024,128]{1,0:T(8,128)(2,1)S(1)}, bf16[1024,128]{1,0:T(8,128)(2,1)}, u32[]{:S(2)}, u32[]{:S(2)}) collective-permute-start(bf16[1024,128]{1,0:T(8,128)(2,1)S(1)} %constant_dynamic-slice_fusion.3), channel_id=1, source_target_pairs={{4,0},{8,4},{12,8},{5,1},{9,5},{13,9},{6,2},{10,6},{14,10},{7,3},{... | collective-permute-start | bytes 786440 | tf_op jit(solution)/shard_map/ppermute | solution.py:59
  2.4 32.0 %collective-permute-start.16 = (bf16[1024,128]{1,0:T(8,128)(2,1)S(1)}, bf16[1024,128]{1,0:T(8,128)(2,1)}, u32[]{:S(2)}, u32[]{:S(2)}) collective-permute-start(bf16[1024,128]{1,0:T(8,128)(2,1)S(1)} %constant_dynamic-slice_fusion.3), channel_id=1, source_target_pairs={{0,4},{4,8},{8,12},{1,5},{5,9},{9,13},{2,6},{6,10},{10,14},{3,7},{... | collective-permute-start | bytes 786440 | tf_op jit(solution)/shard_map/ppermute | solution.py:60
  10.4 25.3 %collective-permute-start.31 = (bf16[1024,128]{1,0:T(8,128)(2,1)S(1)}, bf16[1024,128]{1,0:T(8,128)(2,1)}, u32[]{:S(2)}, u32[]{:S(2)}) collective-permute-start(bf16[1024,128]{1,0:T(8,128)(2,1)S(1)} %get-tuple-element.33), channel_id=1, source_target_pairs={{4,0},{8,4},{12,8},{5,1},{9,5},{13,9},{6,2},{10,6},{14,10},{7,3},{... | collective-permute-start | bytes 786440 | tf_op jit(solution)/shard_map/ppermute | solution.py:59
  11.7 26.5 %collective-permute-start.30 = (bf16[1024,128]{1,0:T(8,128)(2,1)S(1)}, bf16[1024,128]{1,0:T(8,128)(2,1)}, u32[]{:S(2)}, u32[]{:S(2)}) collective-permute-start(bf16[1024,128]{1,0:T(8,128)(2,1)S(1)} %get-tuple-element.33), channel_id=1, source_target_pairs={{0,4},{4,8},{8,12},{1,5},{5,9},{9,13},{2,6},{6,10},{10,14},{3,7},{... | collective-permute-start | bytes 786440 | tf_op jit(solution)/shard_map/ppermute | solution.py:60
  17.0 22.6 %collective-permute-start.40 = (bf16[1024,128]{1,0:T(8,128)(2,1)}, bf16[1024,128]{1,0:T(8,128)(2,1)}, u32[]{:S(2)}, u32[]{:S(2)}) collective-permute-start(bf16[1024,128]{1,0:T(8,128)(2,1)} %get-tuple-element.34), channel_id=1, source_target_pairs={{4,0},{8,4},{12,8},{5,1},{9,5},{13,9},{6,2},{10,6},{14,10},{7,3},{... | collective-permute-start | bytes 786440 | tf_op jit(solution)/shard_map/ppermute | solution.py:59
  42.8 23.3 %collective-permute-start.41 = (bf16[1024,128]{1,0:T(8,128)(2,1)}, bf16[1024,128]{1,0:T(8,128)(2,1)S(1)}, u32[]{:S(2)}, u32[]{:S(2)}) collective-permute-start(bf16[1024,128]{1,0:T(8,128)(2,1)} %collective-permute-done.40), channel_id=1, source_target_pairs={{4,0},{8,4},{5,1},{9,5},{6,2},{10,6},{7,3},{11,7},{20,16},{24,20},... | collective-permute-start | bytes 786440 | tf_op jit(solution)/shard_map/ppermute | solution.py:59
  44.3 22.6 %collective-permute-start.43 = (bf16[1024,128]{1,0:T(8,128)(2,1)}, bf16[1024,128]{1,0:T(8,128)(2,1)S(1)}, u32[]{:S(2)}, u32[]{:S(2)}) collective-permute-start(bf16[1024,128]{1,0:T(8,128)(2,1)} %collective-permute-done.39), channel_id=1, source_target_pairs={{4,8},{8,12},{5,9},{9,13},{6,10},{10,14},{7,11},{11,15},{20,24},{2... | collective-permute-start | bytes 786440 | tf_op jit(solution)/shard_map/ppermute | solution.py:60
  45.0 23.2 %collective-permute-start.19 = (bf16[1024,128]{1,0:T(8,128)(2,1)}, bf16[1024,128]{1,0:T(8,128)(2,1)S(1)}, u32[]{:S(2)}, u32[]{:S(2)}) collective-permute-start(bf16[1024,128]{1,0:T(8,128)(2,1)} %collective-permute-done.18), channel_id=1, source_target_pairs={{4,0},{5,1},{6,2},{7,3},{20,16},{21,17},{22,18},{23,19}} | collective-permute-start | bytes 786440 | tf_op jit(solution)/shard_map/ppermute | solution.py:59
  50.3 28.6 %collective-permute-start.2 = (bf16[1024,256]{1,0:T(8,128)(2,1)S(1)}, bf16[1024,256]{1,0:T(8,128)(2,1)S(1)}, u32[]{:S(2)}, u32[]{:S(2)}) collective-permute-start(bf16[1024,256]{1,0:T(8,128)(2,1)S(1)} %constant_dynamic-slice_fusion), channel_id=1, source_target_pairs={{4,0},{8,4},{12,8},{5,1},{9,5},{13,9},{6,2},{10,6},{14,10},{7,3},{... | collective-permute-start | bytes 1572872 | tf_op jit(solution)/shard_map/ppermute | solution.py:59
  51.5 28.8 %collective-permute-start.1 = (bf16[1024,256]{1,0:T(8,128)(2,1)S(1)}, bf16[1024,256]{1,0:T(8,128)(2,1)S(1)}, u32[]{:S(2)}, u32[]{:S(2)}) collective-permute-start(bf16[1024,256]{1,0:T(8,128)(2,1)S(1)} %constant_dynamic-slice_fusion), channel_id=1, source_target_pairs={{0,4},{4,8},{8,12},{1,5},{5,9},{9,13},{2,6},{6,10},{10,14},{3,7},{... | collective-permute-start | bytes 1572872 | tf_op jit(solution)/shard_map/ppermute | solution.py:60
  66.9 15.1 %collective-permute-start.33 = (bf16[1024,128]{1,0:T(8,128)(2,1)}, bf16[1024,128]{1,0:T(8,128)(2,1)S(1)}, u32[]{:S(2)}, u32[]{:S(2)}) collective-permute-start(bf16[1024,128]{1,0:T(8,128)(2,1)} %collective-permute-done.32), channel_id=1, source_target_pairs={{4,0},{5,1},{6,2},{7,3},{20,16},{21,17},{22,18},{23,19}} | collective-permute-start | bytes 786440 | tf_op jit(solution)/shard_map/ppermute | solution.py:59
  78.9 29.7 %collective-permute-start.10 = (bf16[128,4096]{1,0:T(8,128)(2,1)S(1)}, bf16[128,4096]{1,0:T(8,128)(2,1)S(1)}, u32[]{:S(2)}, u32[]{:S(2)}) collective-permute-start(bf16[128,4096]{1,0:T(8,128)(2,1)S(1)} %pad_maximum_fusion.3), channel_id=1, source_target_pairs={{0,16},{2,18},{16,0},{18,2},{1,17},{3,19},{17,1},{19,3},{4,20},{6,... | collective-permute-start | bytes 3145736 | tf_op jit(solution)/shard_map/ppermute | solution.py:48
  80.4 29.1 %collective-permute-start = (bf16[128,4096]{1,0:T(8,128)(2,1)S(1)}, bf16[128,4096]{1,0:T(8,128)(2,1)S(1)}, u32[]{:S(2)}, u32[]{:S(2)}) collective-permute-start(bf16[128,4096]{1,0:T(8,128)(2,1)S(1)} %copy-done.4), channel_id=1, source_target_pairs={{0,1},{1,0},{2,3},{3,2},{4,5},{5,4},{6,7},{7,6},{8,9},{9,8},{10,11... | collective-permute-start | bytes 3145736 | tf_op jit(solution)/shard_map/ppermute | solution.py:52
  80.4 42.1 %collective-permute-start.13 = (bf16[128,4096]{1,0:T(8,128)(2,1)S(1)}, bf16[128,4096]{1,0:T(8,128)(2,1)S(1)}, u32[]{:S(2)}, u32[]{:S(2)}) collective-permute-start(bf16[128,4096]{1,0:T(8,128)(2,1)S(1)} %copy-done.3), channel_id=1, source_target_pairs={{0,18},{2,16},{16,2},{18,0},{1,19},{3,17},{17,3},{19,1},{4,22},{6,... | collective-permute-start | bytes 3145736 | tf_op jit(solution)/shard_map/ppermute | solution.py:48
  107.2 37.6 %collective-permute-start.7 = (bf16[128,4096]{1,0:T(8,128)(2,1)S(1)}, bf16[128,4096]{1,0:T(8,128)(2,1)S(1)}, u32[]{:S(2)}, u32[]{:S(2)}) collective-permute-start(bf16[128,4096]{1,0:T(8,128)(2,1)S(1)} %copy-done.2), channel_id=1, source_target_pairs={{0,2},{2,0},{16,18},{18,16},{1,3},{3,1},{17,19},{19,17},{4,6},{6,4... | collective-permute-start | bytes 3145736 | tf_op jit(solution)/shard_map/ppermute | solution.py:48
  107.3 38.6 %collective-permute-start.4 = (bf16[1024,256]{1,0:T(8,128)(2,1)S(1)}, bf16[1024,256]{1,0:T(8,128)(2,1)S(1)}, u32[]{:S(2)}, u32[]{:S(2)}) collective-permute-start(bf16[1024,256]{1,0:T(8,128)(2,1)S(1)} %collective-permute-done.3), channel_id=1, source_target_pairs={{4,0},{5,1},{6,2},{7,3},{20,16},{21,17},{22,18},{23,19}} | collective-permute-start | bytes 1572872 | tf_op jit(solution)/shard_map/ppermute | solution.py:59
  108.6 37.3 %collective-permute-start.6 = (bf16[1024,256]{1,0:T(8,128)(2,1)S(1)}, bf16[1024,256]{1,0:T(8,128)(2,1)S(1)}, u32[]{:S(2)}, u32[]{:S(2)}) collective-permute-start(bf16[1024,256]{1,0:T(8,128)(2,1)S(1)} %collective-permute-done.5), channel_id=1, source_target_pairs={{8,12},{9,13},{10,14},{11,15},{24,28},{25,29},{26,30},{27,31}} | collective-permute-start | bytes 1572872 | tf_op jit(solution)/shard_map/ppermute | solution.py:60
  109.5 37.6 %collective-permute-start.11 = (bf16[128,4096]{1,0:T(8,128)(2,1)S(1)}, bf16[128,4096]{1,0:T(8,128)(2,1)S(1)}, u32[]{:S(2)}, u32[]{:S(2)}) collective-permute-start(bf16[128,4096]{1,0:T(8,128)(2,1)S(1)} %collective-permute-done.10), channel_id=1, source_target_pairs={{0,1},{1,0},{2,3},{3,2},{4,5},{5,4},{6,7},{7,6},{8,9},{9,8},{10,11... | collective-permute-start | bytes 3145736 | tf_op jit(solution)/shard_map/ppermute | solution.py:52
  122.5 28.6 %collective-permute-start.14 = (bf16[128,4096]{1,0:T(8,128)(2,1)S(1)}, bf16[128,4096]{1,0:T(8,128)(2,1)S(1)}, u32[]{:S(2)}, u32[]{:S(2)}) collective-permute-start(bf16[128,4096]{1,0:T(8,128)(2,1)S(1)} %collective-permute-done.13), channel_id=1, source_target_pairs={{0,1},{1,0},{2,3},{3,2},{4,5},{5,4},{6,7},{7,6},{8,9},{9,8},{10,11... | collective-permute-start | bytes 3145736 | tf_op jit(solution)/shard_map/ppermute | solution.py:52
  167.3 25.5 %collective-permute-start.46 = (f32[256,128]{0,1:T(8,128)S(1)}, f32[256,128]{0,1:T(8,128)S(1)}, u32[]{:S(2)}, u32[]{:S(2)}) collective-permute-start(f32[256,128]{0,1:T(8,128)S(1)} %fusion.90), channel_id=1, source_target_pairs={{0,16},{2,18},{16,0},{18,2},{1,17},{3,19},{17,1},{19,3},{4,20},{6,... | collective-permute-start | bytes 393224 | tf_op jit(solution)/shard_map/ppermute | solution.py:48
  167.9 40.9 %collective-permute-start.12 = (f32[256,256]{0,1:T(8,128)S(1)}, f32[256,256]{0,1:T(8,128)S(1)}, u32[]{:S(2)}, u32[]{:S(2)}) collective-permute-start(f32[256,256]{0,1:T(8,128)S(1)} %fusion.106), channel_id=1, source_target_pairs={{0,16},{2,18},{16,0},{18,2},{1,17},{3,19},{17,1},{19,3},{4,20},{6,... | collective-permute-start | bytes 786440 | tf_op jit(solution)/shard_map/ppermute | solution.py:48
  184.0 24.6 %collective-permute-start.47 = (f32[256,128]{0,1:T(8,128)S(1)}, f32[256,128]{0,1:T(8,128)S(1)}, u32[]{:S(2)}, u32[]{:S(2)}) collective-permute-start(f32[256,128]{0,1:T(8,128)S(1)} %fusion.89), channel_id=1, source_target_pairs={{0,18},{2,16},{16,2},{18,0},{1,19},{3,17},{17,3},{19,1},{4,22},{6,... | collective-permute-start | bytes 393224 | tf_op jit(solution)/shard_map/ppermute | solution.py:48
  190.7 18.0 %collective-permute-start.45 = (f32[256,128]{0,1:T(8,128)S(1)}, f32[256,128]{0,1:T(8,128)S(1)}, u32[]{:S(2)}, u32[]{:S(2)}) collective-permute-start(f32[256,128]{0,1:T(8,128)S(1)} %fusion.91), channel_id=1, source_target_pairs={{0,2},{2,0},{16,18},{18,16},{1,3},{3,1},{17,19},{19,17},{4,6},{6,4... | collective-permute-start | bytes 393224 | tf_op jit(solution)/shard_map/ppermute | solution.py:48
  192.8 15.9 %collective-permute-start.15 = (f32[256,256]{0,1:T(8,128)S(1)}, f32[256,256]{0,1:T(8,128)S(1)}, u32[]{:S(2)}, u32[]{:S(2)}) collective-permute-start(f32[256,256]{0,1:T(8,128)S(1)} %fusion.107), channel_id=1, source_target_pairs={{0,18},{2,16},{16,2},{18,0},{1,19},{3,17},{17,3},{19,1},{4,22},{6,... | collective-permute-start | bytes 786440 | tf_op jit(solution)/shard_map/ppermute | solution.py:48
  (38 other events, 431.1 us)

commit v2 on v1

v2 whole, which is shorter than its diff:
```python
import functools

import jax
import jax.numpy as jnp
from jax import lax
from jax.experimental import pallas as pl
from jax.experimental.pallas import tpu as pltpu
from jax.sharding import Mesh
from jax.sharding import PartitionSpec as P

HEAD = 128
BLOCK = 128
CHUNK_HEADS = (1, 2, 1)
VMEM = 48 * 1024 * 1024


def rollout_info(positions, lengths, overlong):
    ends = jnp.cumsum(lengths)
    starts = ends - lengths
    which = jnp.sum((ends[None, :] <= positions[:, None]).astype(jnp.int32), axis=1)
    match = jnp.arange(lengths.shape[0], dtype=jnp.int32)[None, :] == which[:, None]
    offset = positions - jnp.sum(jnp.where(match, starts[None, :], 0), axis=1)
    masked = jnp.sum(jnp.where(match, overlong[None, :], 0), axis=1)
    return (which, offset, masked)


def rotation(offset):
    half = HEAD // 2
    freqs = jnp.power(
        jnp.float32(500000.0), -jnp.arange(half, dtype=jnp.float32) * 2.0 / HEAD
    )
    angle = offset.astype(jnp.float32)[:, None] * freqs[None, :]
    cosine, sine = jnp.cos(angle), jnp.sin(angle)
    return jnp.concatenate([cosine, cosine], axis=1), jnp.concatenate([-sine, sine], axis=1)


def shift_square(block, dx, dy, groups, ys):
    route = [
        (x * ys + y, (x + dx) % groups * ys + (y + dy) % ys)
        for x in range(groups)
        for y in range(ys)
    ]
    return lax.ppermute(block, ("groups", "y"), route)


def swap_core(block):
    return lax.ppermute(block, "dp", [(0, 1), (1, 0)])


def gather_line(block, zs):
    down, up = [block], [block]
    for step in range(1, zs):
        down.append(lax.ppermute(down[-1], "z", [(i, i - 1) for i in range(1, zs - step + 1)]))
        up.append(lax.ppermute(up[-1], "z", [(i, i + 1) for i in range(step - 1, zs - 1)]))
    return down, up


def norm_kernel(zs, ys, groups, width, place, tokens, gain, *outs):
    x, z, y = place[0], place[1], place[2]
    rows, columns = tokens.shape
    step = min(columns, 1024)
    squares = jnp.zeros((rows, step), jnp.float32)
    for at in range(0, columns, step):
        part = tokens[:, at : at + step].astype(jnp.float32)
        squares += part * part
    factor = lax.rsqrt(jnp.sum(squares, axis=1, keepdims=True) / columns + 1e-05)
    for peer, out in enumerate(outs):
        dx, dy = peer // ys, peer % ys
        for s in range(zs):
            blk = lax.rem(z + (zs - s), zs) * ys + lax.rem(y + dy, ys)
            start = pl.multiple_of((blk * groups + lax.rem(x + dx, groups)) * width, width)
            part = tokens[:, pl.ds(start, width)].astype(jnp.float32)
            scale = gain[:, pl.ds(start, width)]
            out[:, s * width : (s + 1) * width] = (part * factor * scale).astype(jnp.bfloat16)


def norm_pieces(tokens, gain, place, zs, ys, groups, width):
    count, columns = tokens.shape
    rows = min(count, 32)
    peers = groups * ys
    return pl.pallas_call(
        functools.partial(norm_kernel, zs, ys, groups, width),
        grid=(count // rows,),
        in_specs=[
            pl.BlockSpec(memory_space=pltpu.SMEM),
            pl.BlockSpec((rows, columns), lambda i: (i, 0)),
            pl.BlockSpec((1, columns), lambda i: (0, 0)),
        ],
        out_specs=[pl.BlockSpec((rows, zs * width), lambda i: (i, 0))] * peers,
        out_shape=[jax.ShapeDtypeStruct((count, zs * width), jnp.bfloat16)] * peers,
        compiler_params=pltpu.CompilerParams(vmem_limit_bytes=VMEM),
        cost_estimate=pl.CostEstimate(
            flops=5 * count * columns, bytes_accessed=4 * count * columns, transcendentals=count
        ),
        name="norm",
    )(place, tokens, gain.astype(jnp.float32)[None, :])


def project_kernel(zs, peers, place, *refs):
    mine, others = refs[:peers], refs[peers : 2 * peers]
    weights = refs[2 * peers : 2 * peers + 2 * zs - 1]
    own, down, up = weights[0], weights[1:zs], weights[zs:]
    outs = refs[2 * peers + 2 * zs - 1 :]
    z, side = place[1], place[3]
    count = mine[0].shape[0]
    width = own.shape[0]
    total = None
    for s in range(zs):
        columns = slice(s * width, (s + 1) * width)
        rows = jnp.concatenate([ref[:, columns] for ref in mine + others], axis=0)
        weight = own[...] if s == 0 else jnp.where(z >= s, up[s - 1][...], down[zs - s - 1][...])
        product = jnp.dot(rows, weight, preferred_element_type=jnp.float32)
        total = product if total is None else total + product
    for peer, out in enumerate(outs):
        here = pl.multiple_of(side * count, count)
        there = pl.multiple_of((1 - side) * count, count)
        out[pl.ds(here, count), :] = total[peer * count : (peer + 1) * count]
        out[pl.ds(there, count), :] = total[(peers + peer) * count : (peers + peer + 1) * count]


def project(pieces, others, down, up, place, zs):
    peers = len(pieces)
    count = pieces[0].shape[0]
    width, columns = down[0].shape
    operands = [place, *pieces, *others, *down, *up[1:]]
    return pl.pallas_call(
        functools.partial(project_kernel, zs, peers),
        in_specs=[pl.BlockSpec(memory_space=pltpu.SMEM)]
        + [pl.BlockSpec(memory_space=pltpu.VMEM)] * (len(operands) - 1),
        out_specs=[pl.BlockSpec(memory_space=pltpu.VMEM)] * peers,
        out_shape=[jax.ShapeDtypeStruct((2 * count, columns), jnp.float32)] * peers,
        compiler_params=pltpu.CompilerParams(vmem_limit_bytes=VMEM),
        cost_estimate=pl.CostEstimate(
            flops=4 * peers * count * zs * width * columns,
            bytes_accessed=4 * peers * count * zs * width,
            transcendentals=0,
        ),
        name="project",
    )(*operands)


def attend_kernel(heads, peers, first, place, *refs):
    partials = refs[:peers]
    cosine, sine, query_info, key_info, here, there, kept, sent = refs[peers:]
    side, own_slot, other_slot = place[3], place[4], place[5]
    key = jnp.where(side == 0, here[...], there[...])
    value = jnp.where(side == 0, there[...], here[...])
    which, position, masked = query_info[:, 0:1], query_info[:, 1:2], query_info[:, 2:3]
    valid = (which == key_info[0:1, :]) & (key_info[1:2, :] <= position)
    for head in range(heads):
        columns = slice((first + head) * HEAD, (first + head + 1) * HEAD)
        proj = partials[0][:, columns]
        for other in partials[1:]:
            proj = proj + other[:, columns]
        turned = proj * cosine[...] + pltpu.roll(proj, HEAD // 2, 1) * sine[...]
        scores = lax.dot_general(
            turned.astype(jnp.bfloat16),
            key,
            (((1,), (1,)), ((), ())),
            preferred_element_type=jnp.float32,
        ) * HEAD ** (-0.5)
        largest = jnp.max(jnp.where(valid, scores, -1e30), axis=1, keepdims=True)
        weights = jnp.where(valid, jnp.exp(scores - largest), 0.0)
        total = jnp.sum(weights, axis=1, keepdims=True)
        summed = jnp.dot(weights.astype(jnp.bfloat16), value, preferred_element_type=jnp.float32)
        out = jnp.where(masked == 1, 0.0, summed / total).astype(jnp.bfloat16)
        low, high = out[:BLOCK], out[BLOCK:]
        into = slice(head * HEAD, (head + 1) * HEAD)
        kept[:, into] = jnp.where(own_slot == 0, low, high)
        sent[:, into] = jnp.where(other_slot == 0, low, high)


def attend(heads, first, partials, cosine, sine, query_info, key_info, here, there, place):
    rows, keys = cosine.shape[0], here.shape[0]
    operands = [place, *partials, cosine, sine, query_info, key_info, here, there]
    return pl.pallas_call(
        functools.partial(attend_kernel, heads, len(partials), first),
        in_specs=[pl.BlockSpec(memory_space=pltpu.SMEM)]
        + [pl.BlockSpec(memory_space=pltpu.VMEM)] * (len(operands) - 1),
        out_specs=[pl.BlockSpec(memory_space=pltpu.VMEM)] * 2,
        out_shape=[jax.ShapeDtypeStruct((BLOCK, heads * HEAD), jnp.bfloat16)] * 2,
        compiler_params=pltpu.CompilerParams(vmem_limit_bytes=VMEM),
        cost_estimate=pl.CostEstimate(
            flops=4 * heads * rows * keys * HEAD,
            bytes_accessed=4 * keys * HEAD + 20 * rows * heads * HEAD,
            transcendentals=heads * rows * keys,
        ),
        name="attend",
    )(*operands)


def on_device(groups, zs, ys, tokens, gain, w_query, w_kv, lengths, overlong, assign):
    count = tokens.shape[0]
    pair = 2 * count
    x, z, y, side = (lax.axis_index(name) for name in ("groups", "z", "y", "dp"))
    blk = z * ys + y
    width = w_query.shape[0] // groups
    peers = [(dx, dy) for dx in range(groups) for dy in range(ys)]
    pair_base = blk * pair
    block_base = pair_base // BLOCK
    slots = lax.dynamic_slice_in_dim(assign, block_base, 2) - block_base
    own_slot = lax.dynamic_index_in_dim(slots, side, keepdims=False)
    other_slot = lax.dynamic_index_in_dim(slots, 1 - side, keepdims=False)
    place = jnp.stack([x, z, y, side, own_slot, other_slot]).astype(jnp.int32)

    mine_q = lax.dynamic_slice_in_dim(w_query, x * width, width, 0)
    mine_kv = lax.dynamic_slice_in_dim(w_kv, x * width, width, 0)
    chunks, at = [], 0
    for heads in CHUNK_HEADS:
        chunk = mine_q[:, at * HEAD : (at + heads) * HEAD]
        chunks.append(jnp.concatenate([mine_kv, chunk], axis=1) if at == 0 else chunk)
        at += heads

    normed = norm_pieces(tokens, gain, place, zs, ys, groups, width)
    normed, chunks[1:] = lax.optimization_barrier((normed, chunks[1:]))
    weights = [gather_line(chunk, zs) for chunk in chunks]
    pieces = [
        shift_square(piece, dx, dy, groups, ys) if dx or dy else piece
        for (dx, dy), piece in zip(peers, normed)
    ]
    others = [swap_core(piece) for piece in pieces]

    def partial_sums(chunk):
        down, up = weights[chunk]
        sums = project(pieces, others, down, up, place, zs)
        return [
            shift_square(part, -dx, -dy, groups, ys) if dx or dy else part
            for (dx, dy), part in zip(peers, sums)
        ]

    pair_rows = pair_base + jnp.arange(pair, dtype=jnp.int32)
    which, offset, masked = rollout_info(pair_rows, lengths, overlong)
    cosine, sine = rotation(offset)
    query_info = jnp.stack([which, pair_rows, masked], axis=1)
    key_blk = jnp.stack([(z - s) % zs * ys + (y - t) % ys for t in range(ys) for s in range(zs)])
    key_place = (
        key_blk[:, None] * pair + jnp.arange(pair, dtype=jnp.int32)[None, :]
    ).reshape(-1)
    ends = jnp.cumsum(lengths)
    key_which = jnp.sum((ends[None, :] <= key_place[:, None]).astype(jnp.int32), axis=1)
    key_info = jnp.stack([key_which, key_place], axis=0)

    partials = partial_sums(0)
    proj = sum(part[:, :HEAD] for part in partials)
    turned = proj * cosine + jnp.roll(proj, HEAD // 2, axis=1) * sine
    mine = jnp.where(side == 0, turned, proj).astype(jnp.bfloat16)
    along = [mine] + [
        lax.ppermute(mine, "z", [(i, (i + s) % zs) for i in range(zs)]) for s in range(1, zs)
    ]
    along = jnp.concatenate(along, axis=0)
    here = [along] + [
        lax.ppermute(along, "y", [(i, (i + s) % ys) for i in range(ys)]) for s in range(1, ys)
    ]
    here = jnp.concatenate(here, axis=0)
    there = swap_core(here)

    kept, got = [], []
    for chunk, heads in enumerate(CHUNK_HEADS):
        if chunk:
            partials = partial_sums(chunk)
        own, other = attend(
            heads, 0 if chunk else 1, partials, cosine, sine, query_info, key_info, here, there, place
        )
        kept.append(own)
        got.append(swap_core(other))
    kept = jnp.concatenate(kept, axis=1)
    got = jnp.concatenate(got, axis=1)
    return jnp.where(
        side == 0,
        jnp.concatenate([kept, got], axis=1),
        jnp.concatenate([got, kept], axis=1),
    )


def solution(mesh):
    groups, blks, cores = (mesh.shape[name] for name in ("groups", "blk", "dp"))
    ys = 2
    zs = blks // ys
    fine = Mesh(mesh.devices.reshape(groups, zs, ys, cores), ("groups", "z", "y", "dp"))
    placed = (
        P(("groups", "z", "y", "dp"), None),
        P(),
        P(("z", "y"), "dp"),
        P(("z", "y"), "dp"),
        P("groups"),
        P("groups"),
        P("groups"),
    )
    return jax.shard_map(
        functools.partial(on_device, groups, zs, ys),
        mesh=fine,
        in_specs=placed,
        out_specs=P(("groups", "z", "y", "dp"), None),
        check_vma=False,
    )
```

time: 227 us -> 185 us (0.81)
  Pallas kernels: 0 us -> 33.2 us
  other arithmetic: 32 us -> 4.65 us
  matrix products: 24.5 us -> 0 us
  starting transfers between devices: 75.6 us -> 55.9 us
  waiting for transfers between devices: 84.7 us -> 76.1 us
  local copies, waits for them, and re-layouts: 6.11 us -> 13.1 us
    pallas_call x0 -> x7, Pallas kernels: none -> 33.2 us  [the longest x3 19.4 us: project(): pl.pallas_call(functools.partial(project_kernel, zs, peers), in_specs=[pl...]
    dot_general x24 -> x0, matrix products: 24.5 us -> none  [the longest x16 17.9 us: project(): partial = jnp.dot(rows, weight, preferred_element_type=jnp.float32)]
    select_n x18 -> x1, other arithmetic: 19.6 us -> 0.73 us  [on_device(): jnp.where(side == 0, jnp.concatenate([kept, got], axis=1), jnp.concatenat...]
    ppermute x12 -> x9, starting transfers between devices: 37.4 us -> 19.4 us  [gather_line(): lax.ppermute(up[-1], 'z', [(i, i + 1) for i in range(step - 1, zs - 1)])]
    ppermute x12 -> x9, waiting for transfers between devices: 0.03 us -> 9.83 us  [gather_line(): lax.ppermute(up[-1], 'z', [(i, i + 1) for i in range(step - 1, zs - 1)])]
    ppermute x15 -> x12, waiting for transfers between devices: 36.5 us -> 29.4 us  [shift_square(): return lax.ppermute(block, ('groups', 'y'), route)]
    unnamed x32 -> x80, local copies, waits for them, and re-layouts: 1.56 us -> 8.51 us
    ppermute x1, waiting for transfers between devices: 11.7 us -> 4.8 us  [on_device(): lax.ppermute(along, 'y', [(i, (i + s) % ys) for i in range(ys)])]
  transfers between devices with their start and end apart: 51 -> 42, of which waited for: 13 -> 13; matrix products, arithmetic and copies ran while one was open for 21% -> 4% of each run, Pallas kernels for 0% -> 18%
where the time goes in v2:
time: 185 us; the launch traced here: 184 us
  waiting for transfers between devices  76.1 us (41%)
  starting transfers between devices  55.9 us (30%)
  Pallas kernels  33.2 us (18%)
  local copies, waits for them, and re-layouts  13.1 us (7%)
  other arithmetic  4.65 us (3%)
    ppermute x9, waiting for transfers between devices, gather_line(): lax.ppermute(down[-1], 'z', [(i, i - 1) for i in range(1, zs - step + 1)])  31 us
    ppermute x12, waiting for transfers between devices, shift_square(): return lax.ppermute(block, ('groups', 'y'), route)  29.4 us
    ppermute x9, starting transfers between devices, gather_line(): lax.ppermute(up[-1], 'z', [(i, i + 1) for i in range(step - 1, zs - 1)])  19.4 us
    pallas_call x3, Pallas kernels, project(): pl.pallas_call(functools.partial(project_kernel, zs, peers), in_specs=[pl...  19.4 us
    ppermute x12, starting transfers between devices, shift_square(): return lax.ppermute(block, ('groups', 'y'), route)  15.7 us
    ppermute x9, starting transfers between devices, gather_line(): lax.ppermute(down[-1], 'z', [(i, i - 1) for i in range(1, zs - step + 1)])  11.6 us
    ppermute x9, waiting for transfers between devices, gather_line(): lax.ppermute(up[-1], 'z', [(i, i + 1) for i in range(step - 1, zs - 1)])  9.83 us
    pallas_call x3, Pallas kernels, attend(): pl.pallas_call(functools.partial(attend_kernel, heads, len(partials), fir...  8.96 us
  transfers between devices with their start and end apart: 42, of which 13 were waited for; matrix products, arithmetic and copies ran while one was open for 4% of the time, Pallas kernels for 18%

profile of v2, /device:TPU:0, one launch (start us, length us, event | category | flops | bytes accessed | tf_op | source)
XLA Modules:
  0.0 183.7 jit_solution(15625482689589734183)
XLA Ops:
  7.5 4.9 %norm.1 = (bf16[128,4096]{1,0:T(8,128)(2,1)S(1)}, bf16[128,4096]{1,0:T(8,128)(2,1)S(1)}, bf16[128,4096]{1,0:T(8,128)(2,1)}, bf16[128,4096]{1,0:T(8,128)(2,1)}) custom-call(s32[6]{0:T(128)S(1)} %stack.62.place, bf16[128,16384]{1,0:T(8,128)(2,1)} %tokens.1, f32[1,16384]{1,0:T(1,128)S(1)} %bitcast.24), custom_call_target="tpu_custom_call" | custom-call | flops 10485760 | bytes 8388608 | tf_op jit(solution)/shard_map/norm/pallas_call | solution.py:81
  12.4 3.0 %collective-permute-start = (bf16[128,4096]{1,0:T(8,128)(2,1)S(1)}, bf16[128,4096]{1,0:T(8,128)(2,1)S(1)}, u32[]{:S(2)}, u32[]{:S(2)}) collective-permute-start(bf16[128,4096]{1,0:T(8,128)(2,1)S(1)} %get-tuple-element.38), channel_id=1, source_target_pairs={{0,2},{2,0},{16,18},{18,16},{1,3},{3,1},{17,19},{19,17},{4,6},{6,4... | collective-permute-start | bytes 3145736 | tf_op jit(solution)/shard_map/ppermute | solution.py:43
  16.9 3.3 %collective-permute-done.7.refs_9_ = bf16[1024,256]{1,0:T(8,128)(2,1)} collective-permute-done((bf16[1024,256]{1,0:T(8,128)(2,1)}, bf16[1024,256]{1,0:T(8,128)(2,1)}, u32[]{:S(2)}, u32[]{:S(2)}) %collective-permute-start.7) | collective-permute-done | bytes 524320 | tf_op jit(solution)/shard_map/ppermute | solution.py:53
  20.2 4.4 %collective-permute-start.10 = (bf16[1024,256]{1,0:T(8,128)(2,1)}, bf16[1024,256]{1,0:T(8,128)(2,1)}, u32[]{:S(2)}, u32[]{:S(2)}) collective-permute-start(bf16[1024,256]{1,0:T(8,128)(2,1)} %pad_maximum_fusion.refs_8_), channel_id=1, source_target_pairs={{0,4},{4,8},{8,12},{1,5},{5,9},{9,13},{2,6},{6,10},{10,14},{3,7},{... | collective-permute-start | bytes 1572872 | tf_op jit(solution)/shard_map/ppermute | solution.py:54
  24.6 9.8 %collective-permute-done.10.refs_12_ = bf16[1024,256]{1,0:T(8,128)(2,1)} collective-permute-done((bf16[1024,256]{1,0:T(8,128)(2,1)}, bf16[1024,256]{1,0:T(8,128)(2,1)}, u32[]{:S(2)}, u32[]{:S(2)}) %collective-permute-start.10) | collective-permute-done | bytes 524320 | tf_op jit(solution)/shard_map/ppermute | solution.py:54
  35.7 2.8 %collective-permute-done.refs_1_ = bf16[128,4096]{1,0:T(8,128)(2,1)S(1)} collective-permute-done((bf16[128,4096]{1,0:T(8,128)(2,1)S(1)}, bf16[128,4096]{1,0:T(8,128)(2,1)S(1)}, u32[]{:S(2)}, u32[]{:S(2)}) %collective-permute-start) | collective-permute-done | bytes 1048608 | tf_op jit(solution)/shard_map/ppermute | solution.py:43
  41.8 20.7 %collective-permute-done.2.refs_3_ = bf16[128,4096]{1,0:T(8,128)(2,1)} collective-permute-done((bf16[128,4096]{1,0:T(8,128)(2,1)}, bf16[128,4096]{1,0:T(8,128)(2,1)}, u32[]{:S(2)}, u32[]{:S(2)}) %collective-permute-start.2) | collective-permute-done | bytes 1048608 | tf_op jit(solution)/shard_map/ppermute | solution.py:43
  65.8 13.3 %collective-permute-done.9.refs_11_ = bf16[1024,256]{1,0:T(8,128)(2,1)S(1)} collective-permute-done((bf16[1024,256]{1,0:T(8,128)(2,1)}, bf16[1024,256]{1,0:T(8,128)(2,1)S(1)}, u32[]{:S(2)}, u32[]{:S(2)}) %collective-permute-start.9) | collective-permute-done | bytes 524320 | tf_op jit(solution)/shard_map/ppermute | solution.py:53
  80.4 4.6 %collective-permute-start.33 = (bf16[1024,128]{1,0:T(8,128)(2,1)S(1)}, bf16[1024,128]{1,0:T(8,128)(2,1)S(1)}, u32[]{:S(2)}, u32[]{:S(2)}) collective-permute-start(bf16[1024,128]{1,0:T(8,128)(2,1)S(1)} %get-tuple-element.52.refs_8_), channel_id=1, source_target_pairs={{0,4},{4,8},{8,12},{1,5},{5,9},{9,13},{2,6},{6,10},{10,14},{3,7},{... | collective-permute-start | bytes 786440 | tf_op jit(solution)/shard_map/ppermute | solution.py:54
  86.4 5.4 %collective-permute-start.24 = (bf16[1024,256]{1,0:T(8,128)(2,1)S(1)}, bf16[1024,256]{1,0:T(8,128)(2,1)}, u32[]{:S(2)}, u32[]{:S(2)}) collective-permute-start(bf16[1024,256]{1,0:T(8,128)(2,1)S(1)} %dynamic-slice.refs_8_), channel_id=1, source_target_pairs={{0,4},{4,8},{8,12},{1,5},{5,9},{9,13},{2,6},{6,10},{10,14},{3,7},{... | collective-permute-start | bytes 1572872 | tf_op jit(solution)/shard_map/ppermute | solution.py:54
  92.8 7.0 %project.3 = (f32[256,256]{1,0:T(8,128)S(1)}, f32[256,256]{1,0:T(8,128)}, f32[256,256]{1,0:T(8,128)}, f32[256,256]{1,0:T(8,128)}) custom-call(s32[6]{0:T(128)S(1)} %stack.62.place, bf16[128,4096]{1,0:T(8,128)(2,1)S(1)} %get-tuple-element.37.refs_0_, bf16[128,4096]{1,0:T(8,128)(2,1)} %copy-done.1, bf16[128,4096]{1,0:T(8,128)(2,1)} %collective-permute-done.1.refs_2_, ...), custom_call_target="tpu_custom_call" | custom-call | flops 2147483648 | bytes 8388608 | tf_op jit(solution)/shard_map/project/pallas_call | solution.py:126
  100.5 1.7 collective-permute-start.13
  111.9 2.1 %collective-permute-done.15.refs_3_ = f32[256,256]{1,0:T(8,128)S(1)} collective-permute-done((f32[256,256]{1,0:T(8,128)}, f32[256,256]{1,0:T(8,128)S(1)}, u32[]{:S(2)}, u32[]{:S(2)}) %collective-permute-start.15) | collective-permute-done | bytes 262176 | tf_op jit(solution)/shard_map/ppermute | solution.py:43
  115.3 3.9 %collective-permute-start.16 = (bf16[256,128]{1,0:T(8,128)(2,1)S(1)}, bf16[256,128]{1,0:T(8,128)(2,1)S(1)}, u32[]{:S(2)}, u32[]{:S(2)}) collective-permute-start(bf16[256,128]{1,0:T(8,128)(2,1)S(1)} %get-tuple-element.64), channel_id=1, source_target_pairs={{0,4},{4,8},{8,12},{12,0},{1,5},{5,9},{9,13},{13,1},{2,6},{6,10},{... | collective-permute-start | bytes 196616 | tf_op jit(solution)/shard_map/ppermute | solution.py:248
  119.3 2.4 %collective-permute-start.18 = (bf16[256,128]{1,0:T(8,128)(2,1)S(1)}, bf16[256,128]{1,0:T(8,128)(2,1)S(1)}, u32[]{:S(2)}, u32[]{:S(2)}) collective-permute-start(bf16[256,128]{1,0:T(8,128)(2,1)S(1)} %get-tuple-element.64), channel_id=1, source_target_pairs={{0,12},{4,0},{8,4},{12,8},{1,13},{5,1},{9,5},{13,9},{2,14},{6,2},{... | collective-permute-start | bytes 196616 | tf_op jit(solution)/shard_map/ppermute | solution.py:248
  121.7 6.4 %collective-permute-done.22.refs_10_ = bf16[1024,256]{1,0:T(8,128)(2,1)S(1)} collective-permute-done((bf16[1024,256]{1,0:T(8,128)(2,1)}, bf16[1024,256]{1,0:T(8,128)(2,1)S(1)}, u32[]{:S(2)}, u32[]{:S(2)}) %collective-permute-start.22) | collective-permute-done | bytes 524320 | tf_op jit(solution)/shard_map/ppermute | solution.py:53
  132.4 1.6 collective-permute-start.19
  134.0 4.8 %collective-permute-done.19 = bf16[1024,128]{1,0:T(8,128)(2,1)S(1)} collective-permute-done((bf16[1024,128]{1,0:T(8,128)(2,1)S(1)}, bf16[1024,128]{1,0:T(8,128)(2,1)S(1)}, u32[]{:S(2)}, u32[]{:S(2)}) %collective-permute-start.19) | collective-permute-done | bytes 262176 | tf_op jit(solution)/shard_map/ppermute | solution.py:252
  139.0 8.0 %collective-permute-done.23.refs_11_ = bf16[1024,256]{1,0:T(8,128)(2,1)S(1)} collective-permute-done((bf16[1024,256]{1,0:T(8,128)(2,1)S(1)}, bf16[1024,256]{1,0:T(8,128)(2,1)S(1)}, u32[]{:S(2)}, u32[]{:S(2)}) %collective-permute-start.23) | collective-permute-done | bytes 524320 | tf_op jit(solution)/shard_map/ppermute | solution.py:53
  146.9 6.5 %project.4 = (f32[256,256]{1,0:T(8,128)S(1)}, f32[256,256]{1,0:T(8,128)S(1)}, f32[256,256]{1,0:T(8,128)}, f32[256,256]{1,0:T(8,128)}) custom-call(s32[6]{0:T(128)S(1)} %copy-done.22, bf16[128,4096]{1,0:T(8,128)(2,1)S(1)} %get-tuple-element.37.refs_0_, bf16[128,4096]{1,0:T(8,128)(2,1)} %copy-done.1, bf16[128,4096]{1,0:T(8,128)(2,1)} %collective-permute-done.1.refs_2_, ...), custom_call_target="tpu_custom_call" | custom-call | flops 2147483648 | bytes 8388608 | tf_op jit(solution)/shard_map/project/pallas_call | solution.py:126
  157.2 5.9 %project.5 = (f32[256,128]{1,0:T(8,128)S(1)}, f32[256,128]{1,0:T(8,128)}, f32[256,128]{1,0:T(8,128)}, f32[256,128]{1,0:T(8,128)}) custom-call(s32[6]{0:T(128)S(1)} %copy-done.22, bf16[128,4096]{1,0:T(8,128)(2,1)S(1)} %get-tuple-element.37.refs_0_, bf16[128,4096]{1,0:T(8,128)(2,1)S(1)} %copy-done.2, bf16[128,4096]{1,0:T(8,128)(2,1)} %collective-permute-done.1.refs_2_, ...), custom_call_target="tpu_custom_call" | custom-call | flops 1073741824 | bytes 8388608 | tf_op jit(solution)/shard_map/project/pallas_call | solution.py:126
  171.9 2.2 %attend.3 = (bf16[128,128]{1,0:T(8,128)(2,1)S(1)}, bf16[128,128]{1,0:T(8,128)(2,1)S(1)}) custom-call(s32[6]{0:T(128)S(1)} %copy-done.23, f32[256,256]{1,0:T(8,128)S(1)} %copy-done.4, f32[256,256]{1,0:T(8,128)S(1)} %copy-done.6, f32[256,256]{1,0:T(8,128)S(1)} %copy-done.8, f32[256,256]{1,0:T(8,128)S(1)} %copy-done.10, ...), custom_call_target="tpu_custom_call" | custom-call | flops 268435456 | bytes 1703936 | tf_op jit(solution)/shard_map/attend/pallas_call | solution.py:176
  174.3 3.9 %attend.4 = (bf16[128,256]{1,0:T(8,128)(2,1)S(1)}, bf16[128,256]{1,0:T(8,128)(2,1)S(1)}) custom-call(s32[6]{0:T(128)S(1)} %copy-done.23, f32[256,256]{1,0:T(8,128)S(1)} %copy-done.16, f32[256,256]{1,0:T(8,128)S(1)} %copy-done.18, f32[256,256]{1,0:T(8,128)} %collective-permute-done.28.refs_2_, f32[256,256]{1,0:T(8,128)} %collective-permute-done.29.refs_3_, ...), custom_call_target="tpu_custom_call" | custom-call | flops 536870912 | bytes 2359296 | tf_op jit(solution)/shard_map/attend/pallas_call | solution.py:176
  178.8 2.8 %attend.5 = (bf16[128,128]{1,0:T(8,128)(2,1)S(1)}, bf16[128,128]{1,0:T(8,128)(2,1)S(1)}) custom-call(s32[6]{0:T(128)S(1)} %copy-done.23, f32[256,128]{1,0:T(8,128)S(1)} %copy-done.20, f32[256,128]{1,0:T(8,128)} %collective-permute-done.36.refs_1_, f32[256,128]{1,0:T(8,128)} %collective-permute-done.37.refs_2_, f32[256,128]{1,0:T(8,128)} %collective-permute-done.38.refs_3_, ...), custom_call_target="tpu_custom_call" | custom-call | flops 268435456 | bytes 1703936 | tf_op jit(solution)/shard_map/attend/pallas_call | solution.py:176
  (182 shorter events, 51.6 us)
Async XLA Ops:
  3.0 17.2 %collective-permute-start.7 = (bf16[1024,256]{1,0:T(8,128)(2,1)}, bf16[1024,256]{1,0:T(8,128)(2,1)}, u32[]{:S(2)}, u32[]{:S(2)}) collective-permute-start(bf16[1024,256]{1,0:T(8,128)(2,1)} %pad_maximum_fusion.refs_8_), channel_id=1, source_target_pairs={{4,0},{8,4},{12,8},{5,1},{9,5},{13,9},{6,2},{10,6},{14,10},{7,3},{... | collective-permute-start | bytes 1572872 | tf_op jit(solution)/shard_map/ppermute | solution.py:53
  12.4 26.1 %collective-permute-start = (bf16[128,4096]{1,0:T(8,128)(2,1)S(1)}, bf16[128,4096]{1,0:T(8,128)(2,1)S(1)}, u32[]{:S(2)}, u32[]{:S(2)}) collective-permute-start(bf16[128,4096]{1,0:T(8,128)(2,1)S(1)} %get-tuple-element.38), channel_id=1, source_target_pairs={{0,2},{2,0},{16,18},{18,16},{1,3},{3,1},{17,19},{19,17},{4,6},{6,4... | collective-permute-start | bytes 3145736 | tf_op jit(solution)/shard_map/ppermute | solution.py:43
  15.4 26.4 %collective-permute-start.1 = (bf16[128,4096]{1,0:T(8,128)(2,1)}, bf16[128,4096]{1,0:T(8,128)(2,1)}, u32[]{:S(2)}, u32[]{:S(2)}) collective-permute-start(bf16[128,4096]{1,0:T(8,128)(2,1)} %get-tuple-element.39), channel_id=1, source_target_pairs={{0,16},{2,18},{16,0},{18,2},{1,17},{3,19},{17,1},{19,3},{4,20},{6,... | collective-permute-start | bytes 3145736 | tf_op jit(solution)/shard_map/ppermute | solution.py:43
  16.9 45.6 %collective-permute-start.2 = (bf16[128,4096]{1,0:T(8,128)(2,1)}, bf16[128,4096]{1,0:T(8,128)(2,1)}, u32[]{:S(2)}, u32[]{:S(2)}) collective-permute-start(bf16[128,4096]{1,0:T(8,128)(2,1)} %get-tuple-element.40), channel_id=1, source_target_pairs={{0,18},{2,16},{16,2},{18,0},{1,19},{3,17},{17,3},{19,1},{4,22},{6,... | collective-permute-start | bytes 3145736 | tf_op jit(solution)/shard_map/ppermute | solution.py:43
  16.9 45.6 %collective-permute-start.3 = (bf16[128,4096]{1,0:T(8,128)(2,1)S(1)}, bf16[128,4096]{1,0:T(8,128)(2,1)}, u32[]{:S(2)}, u32[]{:S(2)}) collective-permute-start(bf16[128,4096]{1,0:T(8,128)(2,1)S(1)} %get-tuple-element.37.refs_0_), channel_id=1, source_target_pairs={{0,1},{1,0},{2,3},{3,2},{4,5},{5,4},{6,7},{7,6},{8,9},{9,8},{10,11... | collective-permute-start | bytes 3145736 | tf_op jit(solution)/shard_map/ppermute | solution.py:47
  34.4 28.7 %collective-permute-start.8 = (bf16[1024,256]{1,0:T(8,128)(2,1)}, bf16[1024,256]{1,0:T(8,128)(2,1)}, u32[]{:S(2)}, u32[]{:S(2)}) collective-permute-start(bf16[1024,256]{1,0:T(8,128)(2,1)} %collective-permute-done.7.refs_9_), channel_id=1, source_target_pairs={{4,0},{8,4},{5,1},{9,5},{6,2},{10,6},{7,3},{11,7},{20,16},{24,20},... | collective-permute-start | bytes 1572872 | tf_op jit(solution)/shard_map/ppermute | solution.py:53
  38.5 25.9 %collective-permute-start.11 = (bf16[1024,256]{1,0:T(8,128)(2,1)}, bf16[1024,256]{1,0:T(8,128)(2,1)}, u32[]{:S(2)}, u32[]{:S(2)}) collective-permute-start(bf16[1024,256]{1,0:T(8,128)(2,1)} %collective-permute-done.10.refs_12_), channel_id=1, source_target_pairs={{4,8},{8,12},{5,9},{9,13},{6,10},{10,14},{7,11},{11,15},{20,24},{2... | collective-permute-start | bytes 1572872 | tf_op jit(solution)/shard_map/ppermute | solution.py:54
  41.8 43.3 %collective-permute-start.4 = (bf16[128,4096]{1,0:T(8,128)(2,1)S(1)}, bf16[128,4096]{1,0:T(8,128)(2,1)S(1)}, u32[]{:S(2)}, u32[]{:S(2)}) collective-permute-start(bf16[128,4096]{1,0:T(8,128)(2,1)S(1)} %collective-permute-done.refs_1_), channel_id=1, source_target_pairs={{0,1},{1,0},{2,3},{3,2},{4,5},{5,4},{6,7},{7,6},{8,9},{9,8},{10,11... | collective-permute-start | bytes 3145736 | tf_op jit(solution)/shard_map/ppermute | solution.py:47
  62.5 23.9 %collective-permute-start.5 = (bf16[128,4096]{1,0:T(8,128)(2,1)}, bf16[128,4096]{1,0:T(8,128)(2,1)S(1)}, u32[]{:S(2)}, u32[]{:S(2)}) collective-permute-start(bf16[128,4096]{1,0:T(8,128)(2,1)} %collective-permute-done.1.refs_2_), channel_id=1, source_target_pairs={{0,1},{1,0},{2,3},{3,2},{4,5},{5,4},{6,7},{7,6},{8,9},{9,8},{10,11... | collective-permute-start | bytes 3145736 | tf_op jit(solution)/shard_map/ppermute | solution.py:47
  62.5 29.3 %collective-permute-start.6 = (bf16[128,4096]{1,0:T(8,128)(2,1)}, bf16[128,4096]{1,0:T(8,128)(2,1)S(1)}, u32[]{:S(2)}, u32[]{:S(2)}) collective-permute-start(bf16[128,4096]{1,0:T(8,128)(2,1)} %collective-permute-done.2.refs_3_), channel_id=1, source_target_pairs={{0,1},{1,0},{2,3},{3,2},{4,5},{5,4},{6,7},{7,6},{8,9},{9,8},{10,11... | collective-permute-start | bytes 3145736 | tf_op jit(solution)/shard_map/ppermute | solution.py:47
  63.1 16.0 %collective-permute-start.9 = (bf16[1024,256]{1,0:T(8,128)(2,1)}, bf16[1024,256]{1,0:T(8,128)(2,1)S(1)}, u32[]{:S(2)}, u32[]{:S(2)}) collective-permute-start(bf16[1024,256]{1,0:T(8,128)(2,1)} %collective-permute-done.8.refs_10_), channel_id=1, source_target_pairs={{4,0},{5,1},{6,2},{7,3},{20,16},{21,17},{22,18},{23,19}} | collective-permute-start | bytes 1572872 | tf_op jit(solution)/shard_map/ppermute | solution.py:53
  64.4 16.0 %collective-permute-start.12 = (bf16[1024,256]{1,0:T(8,128)(2,1)}, bf16[1024,256]{1,0:T(8,128)(2,1)S(1)}, u32[]{:S(2)}, u32[]{:S(2)}) collective-permute-start(bf16[1024,256]{1,0:T(8,128)(2,1)} %collective-permute-done.11.refs_13_), channel_id=1, source_target_pairs={{8,12},{9,13},{10,14},{11,15},{24,28},{25,29},{26,30},{27,31}} | collective-permute-start | bytes 1572872 | tf_op jit(solution)/shard_map/ppermute | solution.py:54
  79.1 23.1 %collective-permute-start.30 = (bf16[1024,128]{1,0:T(8,128)(2,1)S(1)}, bf16[1024,128]{1,0:T(8,128)(2,1)S(1)}, u32[]{:S(2)}, u32[]{:S(2)}) collective-permute-start(bf16[1024,128]{1,0:T(8,128)(2,1)S(1)} %get-tuple-element.52.refs_8_), channel_id=1, source_target_pairs={{4,0},{8,4},{12,8},{5,1},{9,5},{13,9},{6,2},{10,6},{14,10},{7,3},{... | collective-permute-start | bytes 786440 | tf_op jit(solution)/shard_map/ppermute | solution.py:53
  80.4 23.3 %collective-permute-start.33 = (bf16[1024,128]{1,0:T(8,128)(2,1)S(1)}, bf16[1024,128]{1,0:T(8,128)(2,1)S(1)}, u32[]{:S(2)}, u32[]{:S(2)}) collective-permute-start(bf16[1024,128]{1,0:T(8,128)(2,1)S(1)} %get-tuple-element.52.refs_8_), channel_id=1, source_target_pairs={{0,4},{4,8},{8,12},{1,5},{5,9},{9,13},{2,6},{6,10},{10,14},{3,7},{... | collective-permute-start | bytes 786440 | tf_op jit(solution)/shard_map/ppermute | solution.py:54
  85.1 20.5 %collective-permute-start.21 = (bf16[1024,256]{1,0:T(8,128)(2,1)S(1)}, bf16[1024,256]{1,0:T(8,128)(2,1)}, u32[]{:S(2)}, u32[]{:S(2)}) collective-permute-start(bf16[1024,256]{1,0:T(8,128)(2,1)S(1)} %dynamic-slice.refs_8_), channel_id=1, source_target_pairs={{4,0},{8,4},{12,8},{5,1},{9,5},{13,9},{6,2},{10,6},{14,10},{7,3},{... | collective-permute-start | bytes 1572872 | tf_op jit(solution)/shard_map/ppermute | solution.py:53
  86.4 20.5 %collective-permute-start.24 = (bf16[1024,256]{1,0:T(8,128)(2,1)S(1)}, bf16[1024,256]{1,0:T(8,128)(2,1)}, u32[]{:S(2)}, u32[]{:S(2)}) collective-permute-start(bf16[1024,256]{1,0:T(8,128)(2,1)S(1)} %dynamic-slice.refs_8_), channel_id=1, source_target_pairs={{0,4},{4,8},{8,12},{1,5},{5,9},{9,13},{2,6},{6,10},{10,14},{3,7},{... | collective-permute-start | bytes 1572872 | tf_op jit(solution)/shard_map/ppermute | solution.py:54
  108.8 19.4 %collective-permute-start.22 = (bf16[1024,256]{1,0:T(8,128)(2,1)}, bf16[1024,256]{1,0:T(8,128)(2,1)S(1)}, u32[]{:S(2)}, u32[]{:S(2)}) collective-permute-start(bf16[1024,256]{1,0:T(8,128)(2,1)} %collective-permute-done.21.refs_9_), channel_id=1, source_target_pairs={{4,0},{8,4},{5,1},{9,5},{6,2},{10,6},{7,3},{11,7},{20,16},{24,20},... | collective-permute-start | bytes 1572872 | tf_op jit(solution)/shard_map/ppermute | solution.py:53
  111.2 18.3 %collective-permute-start.25 = (bf16[1024,256]{1,0:T(8,128)(2,1)}, bf16[1024,256]{1,0:T(8,128)(2,1)S(1)}, u32[]{:S(2)}, u32[]{:S(2)}) collective-permute-start(bf16[1024,256]{1,0:T(8,128)(2,1)} %collective-permute-done.24.refs_12_), channel_id=1, source_target_pairs={{4,8},{8,12},{5,9},{9,13},{6,10},{10,14},{7,11},{11,15},{20,24},{2... | collective-permute-start | bytes 1572872 | tf_op jit(solution)/shard_map/ppermute | solution.py:54
  128.1 28.3 %collective-permute-start.32 = (bf16[1024,128]{1,0:T(8,128)(2,1)S(1)}, bf16[1024,128]{1,0:T(8,128)(2,1)S(1)}, u32[]{:S(2)}, u32[]{:S(2)}) collective-permute-start(bf16[1024,128]{1,0:T(8,128)(2,1)S(1)} %collective-permute-done.31.refs_10_), channel_id=1, source_target_pairs={{4,0},{5,1},{6,2},{7,3},{20,16},{21,17},{22,18},{23,19}} | collective-permute-start | bytes 786440 | tf_op jit(solution)/shard_map/ppermute | solution.py:53
  129.4 27.7 %collective-permute-start.35 = (bf16[1024,128]{1,0:T(8,128)(2,1)S(1)}, bf16[1024,128]{1,0:T(8,128)(2,1)S(1)}, u32[]{:S(2)}, u32[]{:S(2)}) collective-permute-start(bf16[1024,128]{1,0:T(8,128)(2,1)S(1)} %collective-permute-done.34.refs_13_), channel_id=1, source_target_pairs={{8,12},{9,13},{10,14},{11,15},{24,28},{25,29},{26,30},{27,31}} | collective-permute-start | bytes 786440 | tf_op jit(solution)/shard_map/ppermute | solution.py:54
  130.1 16.8 %collective-permute-start.23 = (bf16[1024,256]{1,0:T(8,128)(2,1)S(1)}, bf16[1024,256]{1,0:T(8,128)(2,1)S(1)}, u32[]{:S(2)}, u32[]{:S(2)}) collective-permute-start(bf16[1024,256]{1,0:T(8,128)(2,1)S(1)} %collective-permute-done.22.refs_10_), channel_id=1, source_target_pairs={{4,0},{5,1},{6,2},{7,3},{20,16},{21,17},{22,18},{23,19}} | collective-permute-start | bytes 1572872 | tf_op jit(solution)/shard_map/ppermute | solution.py:53
  138.9 28.3 %collective-permute-start.20 = (bf16[2048,128]{1,0:T(8,128)(2,1)S(1)}, bf16[2048,128]{1,0:T(8,128)(2,1)S(1)}, u32[]{:S(2)}, u32[]{:S(2)}) collective-permute-start(bf16[2048,128]{1,0:T(8,128)(2,1)S(1)} %constant_dynamic-update-slice_fusion.refs_8_), channel_id=1, source_target_pairs={{0,1},{1,0},{2,3},{3,2},{4,5},{5,4},{6,7},{7,6},{8,9},{9,8},{10,11... | collective-permute-start | bytes 1572872 | tf_op jit(solution)/shard_map/ppermute | solution.py:47
  155.1 19.1 %collective-permute-start.28 = (f32[256,256]{1,0:T(8,128)}, f32[256,256]{1,0:T(8,128)}, u32[]{:S(2)}, u32[]{:S(2)}) collective-permute-start(f32[256,256]{1,0:T(8,128)} %get-tuple-element.49), channel_id=1, source_target_pairs={{0,16},{2,18},{16,0},{18,2},{1,17},{3,19},{17,1},{19,3},{4,20},{6,... | collective-permute-start | bytes 786440 | tf_op jit(solution)/shard_map/ppermute | solution.py:43
  156.4 17.9 %collective-permute-start.29 = (f32[256,256]{1,0:T(8,128)}, f32[256,256]{1,0:T(8,128)}, u32[]{:S(2)}, u32[]{:S(2)}) collective-permute-start(f32[256,256]{1,0:T(8,128)} %get-tuple-element.50), channel_id=1, source_target_pairs={{0,18},{2,16},{16,2},{18,0},{1,19},{3,17},{17,3},{19,1},{4,22},{6,... | collective-permute-start | bytes 786440 | tf_op jit(solution)/shard_map/ppermute | solution.py:43
  (52 other events, 639.3 us)

commit v3 on v2

v3 whole, which is shorter than its diff:
```python
import functools

import jax
import jax.numpy as jnp
from jax import lax
from jax.experimental import pallas as pl
from jax.experimental.pallas import tpu as pltpu
from jax.sharding import Mesh
from jax.sharding import PartitionSpec as P

HEAD = 128
BLOCK = 128
CHUNK_HEADS = (2, 2)
MIB = 1024 * 1024
COST = pl.CostEstimate(flops=1, bytes_accessed=1, transcendentals=0)


def rollout_info(positions, lengths, overlong):
    ends = jnp.cumsum(lengths)
    starts = ends - lengths
    which = jnp.sum((ends[None, :] <= positions[:, None]).astype(jnp.int32), axis=1)
    match = jnp.arange(lengths.shape[0], dtype=jnp.int32)[None, :] == which[:, None]
    offset = positions - jnp.sum(jnp.where(match, starts[None, :], 0), axis=1)
    masked = jnp.sum(jnp.where(match, overlong[None, :], 0), axis=1)
    return (which, offset, masked)


def rotation(offset):
    half = HEAD // 2
    freqs = jnp.power(
        jnp.float32(500000.0), -jnp.arange(half, dtype=jnp.float32) * 2.0 / HEAD
    )
    angle = offset.astype(jnp.float32)[:, None] * freqs[None, :]
    cosine, sine = jnp.cos(angle), jnp.sin(angle)
    return jnp.concatenate([cosine, cosine], axis=1), jnp.concatenate([-sine, sine], axis=1)


def shift_square(block, dx, dy, groups, ys):
    route = [
        (x * ys + y, (x + dx) % groups * ys + (y + dy) % ys)
        for x in range(groups)
        for y in range(ys)
    ]
    return lax.ppermute(block, ("groups", "y"), route)


def swap_core(block):
    return lax.ppermute(block, "dp", [(0, 1), (1, 0)])


def after(block, *done):
    return lax.optimization_barrier((block, *done))[0]


def hop_down(block, step, zs):
    with jax.named_scope("hop%d_down" % step):
        return lax.ppermute(block, "z", [(i, i - 1) for i in range(1, zs - step + 1)])


def hop_up(block, step, zs):
    with jax.named_scope("hop%d_up" % step):
        return lax.ppermute(block, "z", [(i, i + 1) for i in range(step - 1, zs - 1)])


def hop_ends(block, zs):
    with jax.named_scope("hop_ends"):
        return lax.ppermute(block, "z", [(1, 0), (zs - 2, zs - 1)])


def nearest(z, place, zs):
    low = jnp.minimum(z, zs - 1 - z)
    step = (place + 1) // 2
    inner = z - step if place % 2 else z + step
    return jnp.where(place <= 2 * low, inner, jnp.where(2 * z < zs, place, zs - 1 - place))


def ways(place, zs):
    if place == 0:
        return [(None, "own", 0)]
    step = (place + 1) // 2
    inner = [(None, "up" if place % 2 else "down", step)] if place <= zs - 2 else []
    ends = [z for z in range(zs // 2) if 2 * z < place]
    return (
        inner
        + [(z, "down", place - z) for z in ends]
        + [(zs - 1 - z, "up", place - z) for z in ends]
    )


def norm_kernel(zs, ys, groups, width, tokens, gain, out):
    z = lax.axis_index("z")
    rows, columns = tokens.shape
    step = min(columns, 1024)
    squares = jnp.zeros((rows, step), jnp.float32)
    for at in range(0, columns, step):
        part = tokens[:, at : at + step].astype(jnp.float32)
        squares += part * part
    factor = lax.rsqrt(jnp.sum(squares, axis=1, keepdims=True) / columns + 1e-05)
    for s in range(zs):
        into = slice(s * width, (s + 1) * width)
        for peer in range(groups * ys):
            x, y = peer // ys, peer % ys
            blk = nearest(z, s, zs) * ys + y
            start = pl.multiple_of((blk * groups + x) * width, width)
            part = tokens[:, pl.ds(start, width)].astype(jnp.float32)
            scale = gain[:, pl.ds(start, width)]
            out[peer, :, into] = (part * factor * scale).astype(jnp.bfloat16)


def norm_pieces(tokens, gain, zs, ys, groups, width):
    count, columns = tokens.shape
    rows = min(count, 32)
    shape = (groups * ys, count, zs * width)
    return pl.pallas_call(
        functools.partial(norm_kernel, zs, ys, groups, width),
        grid=(count // rows,),
        in_specs=[
            pl.BlockSpec((rows, columns), lambda i: (i, 0)),
            pl.BlockSpec((1, columns), lambda i: (0, 0)),
        ],
        out_specs=pl.BlockSpec((shape[0], rows, shape[2]), lambda i: (0, i, 0)),
        out_shape=jax.ShapeDtypeStruct(shape, jnp.bfloat16),
        compiler_params=pltpu.CompilerParams(vmem_limit_bytes=24 * MIB),
        cost_estimate=COST,
        name="norm",
    )(tokens, gain.astype(jnp.float32)[None, :])


def peer_order(ys, groups, peers):
    x, y = lax.axis_index("groups"), lax.axis_index("y")
    return [
        lax.rem(x + (groups - peer // ys), groups) * ys + lax.rem(y + (ys - peer % ys), ys)
        for peer in range(peers)
    ]


def collect_kernel(zs, ys, groups, names, cuts, *refs):
    mine, others = refs[:2]
    weights, outs = dict(zip(names, refs[2:])), refs[2 + len(names) :]
    z = lax.axis_index("z")
    base, size = cuts[0][0], sum(size for _, size in cuts)
    peers, _, columns = mine.shape
    width = columns // zs
    index = peer_order(ys, groups, peers)
    total = None
    for place in range(zs):
        into = slice(place * width, (place + 1) * width)
        rows = jnp.concatenate([ref[i, :, into] for ref in (mine, others) for i in index], axis=0)
        weight = None
        for who, way, hops in ways(place, zs):
            if (way, hops) in weights:
                read = weights[way, hops][:, base : base + size]
                if weight is None:
                    weight = read if who is None else jnp.where(z == who, read, jnp.zeros_like(read))
                else:
                    weight = jnp.where(z == who, read, weight)
        product = jnp.dot(rows, weight, preferred_element_type=jnp.float32)
        total = product if total is None else total + product
    for (first, size), out in zip(cuts, outs):
        out[...] = total[:, first - base : first - base + size]


def collect(mine, others, pieces, cuts, zs, ys, groups):
    rows = 2 * mine.shape[0] * mine.shape[1]
    operands = [mine, others, *pieces.values()]
    return pl.pallas_call(
        functools.partial(collect_kernel, zs, ys, groups, list(pieces), cuts),
        in_specs=[pl.BlockSpec(memory_space=pltpu.VMEM)] * len(operands),
        out_specs=[pl.BlockSpec(memory_space=pltpu.VMEM)] * len(cuts),
        out_shape=[jax.ShapeDtypeStruct((rows, size), jnp.float32) for _, size in cuts],
        compiler_params=pltpu.CompilerParams(vmem_limit_bytes=40 * MIB),
        cost_estimate=COST,
        name="collect",
    )(*operands)


def finish_kernel(ys, groups, cuts, mine, others, last, sums, *outs):
    side = lax.axis_index("dp")
    peers, count = mine.shape[:2]
    index = peer_order(ys, groups, peers)
    rows = jnp.concatenate([ref[i] for ref in (mine, others) for i in index], axis=0)
    total = sums[...] + jnp.dot(rows, last[...], preferred_element_type=jnp.float32)
    here = pl.multiple_of(side * count, count)
    there = pl.multiple_of((1 - side) * count, count)
    for at, out in enumerate(outs):
        first, size = cuts[at // peers]
        peer = at % peers
        part = total[:, first : first + size]
        out[pl.ds(here, count), :] = part[peer * count : (peer + 1) * count]
        out[pl.ds(there, count), :] = part[(peers + peer) * count : (peers + peer + 1) * count]


def finish(mine, others, last, sums, cuts, ys, groups):
    peers, count, columns = mine.shape
    width = last.shape[0]
    tokens = pl.BlockSpec((peers, count, width), lambda i: (0, 0, columns // width - 1))
    sizes = [size for _, size in cuts for _ in range(peers)]
    outs = pl.pallas_call(
        functools.partial(finish_kernel, ys, groups, cuts),
        grid=(1,),
        in_specs=[
            tokens,
            tokens,
            pl.BlockSpec(last.shape, lambda i: (0, 0)),
            pl.BlockSpec(sums.shape, lambda i: (0, 0)),
        ],
        out_specs=[pl.BlockSpec((2 * count, size), lambda i: (0, 0)) for size in sizes],
        out_shape=[jax.ShapeDtypeStruct((2 * count, size), jnp.float32) for size in sizes],
        compiler_params=pltpu.CompilerParams(vmem_limit_bytes=32 * MIB),
        cost_estimate=COST,
        name="finish",
    )(mine, others, last, sums)
    return [outs[at * peers : (at + 1) * peers] for at in range(len(cuts))]


def attend_kernel(peers, window, place, *refs):
    partials = refs[:peers]
    cosine, sine, query_info, which_key, here, there, kept, sent = refs[peers:]
    side, own_slot, other_slot, first = place[0], place[1], place[2], place[3]
    rows = cosine.shape[0]
    spots = [place[4 + i] for i in range(window // rows)]
    here, there = (
        jnp.concatenate([ref[pl.ds(pl.multiple_of(at, rows), rows), :] for at in spots], axis=0)
        for ref in (here, there)
    )
    key = jnp.where(side == 0, here, there)
    value = jnp.where(side == 0, there, here)
    which, position, masked = query_info[:, 0:1], query_info[:, 1:2], query_info[:, 2:3]
    key_position = first + lax.broadcasted_iota(jnp.int32, (1, window), 1)
    valid = (which == which_key[...]) & (key_position <= position)
    proj = partials[0][...]
    for other in partials[1:]:
        proj = proj + other[...]
    turned = proj * cosine[...] + pltpu.roll(proj, HEAD // 2, 1) * sine[...]
    scores = lax.dot_general(
        turned.astype(jnp.bfloat16), key, (((1,), (1,)), ((), ())), preferred_element_type=jnp.float32
    ) * HEAD ** (-0.5)
    largest = jnp.max(jnp.where(valid, scores, -1e30), axis=1, keepdims=True)
    weights = jnp.where(valid, jnp.exp(scores - largest), 0.0)
    total = jnp.sum(weights, axis=1, keepdims=True)
    summed = jnp.dot(weights.astype(jnp.bfloat16), value, preferred_element_type=jnp.float32)
    out = jnp.where(masked == 1, 0.0, summed / total).astype(jnp.bfloat16)
    low, high = out[:BLOCK], out[BLOCK:]
    kept[...] = jnp.where(own_slot == 0, low, high)
    sent[...] = jnp.where(other_slot == 0, low, high)


def attend(partials, cosine, sine, query_info, which_key, here, there, place):
    rows, window = cosine.shape[0], which_key.shape[1]
    heads = partials[0].shape[1] // HEAD
    fixed = [cosine, sine, query_info, which_key, here, there]
    return pl.pallas_call(
        functools.partial(attend_kernel, len(partials), window),
        grid=(heads,),
        in_specs=[pl.BlockSpec(memory_space=pltpu.SMEM)]
        + [pl.BlockSpec((rows, HEAD), lambda h: (0, h))] * len(partials)
        + [pl.BlockSpec(array.shape, lambda h: (0, 0)) for array in fixed],
        out_specs=[pl.BlockSpec((BLOCK, HEAD), lambda h: (0, h))] * 2,
        out_shape=[jax.ShapeDtypeStruct((BLOCK, heads * HEAD), jnp.bfloat16)] * 2,
        compiler_params=pltpu.CompilerParams(vmem_limit_bytes=16 * MIB + 24 * rows * window),
        cost_estimate=COST,
        name="attend",
    )(place, *partials, *fixed)


def on_device(groups, zs, ys, tokens, gain, w_query, w_kv, lengths, overlong, assign):
    count = tokens.shape[0]
    pair = 2 * count
    x, z, y, side = (lax.axis_index(name) for name in ("groups", "z", "y", "dp"))
    blk = z * ys + y
    width = w_query.shape[0] // groups
    peers = [(dx, dy) for dx in range(groups) for dy in range(ys)]
    pair_base = blk * pair
    block_base = pair_base // BLOCK
    slots = lax.dynamic_slice_in_dim(assign, block_base, 2) - block_base
    own_slot = lax.dynamic_index_in_dim(slots, side, keepdims=False)
    other_slot = lax.dynamic_index_in_dim(slots, 1 - side, keepdims=False)
    tokens_all = zs * ys * pair
    window = min(tokens_all // 2 + pair, tokens_all)
    first_key = jnp.maximum(pair_base - tokens_all // 2, 0)
    key_blk = first_key // pair + jnp.arange(window // pair, dtype=jnp.int32)
    spot = (blk % ys + ys - key_blk % ys) % ys * zs + (z + zs - key_blk // ys) % zs
    place = jnp.concatenate(
        [jnp.stack([side, own_slot, other_slot, first_key]).astype(jnp.int32), spot * pair]
    )

    own = jnp.concatenate(
        [
            lax.dynamic_slice_in_dim(w_kv, x * width, width, 0),
            lax.dynamic_slice_in_dim(w_query, x * width, width, 0),
        ],
        axis=1,
    )
    normed = norm_pieces(tokens, gain, zs, ys, groups, width)
    mine = lax.all_to_all(normed, ("groups", "y"), 0, 0, tiled=True)
    pieces = {("own", 0): own}
    came = [after(own, normed), after(own, normed)]
    for step in range(1, zs - 1):
        came = [hop_down(came[0], step, zs), hop_up(came[1], step, zs)]
        pieces["down", step], pieces["up", step] = came
    done = (mine, *came)
    others = swap_core(after(mine, *done))
    came = [after(came[0], *done), after(came[1], *done)]
    cuts, first = [(0, HEAD)], HEAD
    for heads in CHUNK_HEADS:
        cuts.append((first, heads * HEAD))
        first += heads * HEAD
    last = [
        hop_ends(jnp.where(z == 1, came[0][:, a : a + n], came[1][:, a : a + n]), zs)
        for a, n in cuts
    ]
    sums = [
        *collect(mine, others, pieces, cuts[:1], zs, ys, groups),
        *collect(mine, others, pieces, cuts[1:], zs, ys, groups),
    ]

    def partial_sums(part):
        inner = [(0, cuts[part][1])]
        (parts,) = finish(mine, others, last[part], sums[part], inner, ys, groups)
        return [
            shift_square(part_of, -dx, -dy, groups, ys) if dx or dy else part_of
            for (dx, dy), part_of in zip(peers, parts)
        ]

    pair_rows = pair_base + jnp.arange(pair, dtype=jnp.int32)
    which, offset, masked = rollout_info(pair_rows, lengths, overlong)
    cosine, sine = rotation(offset)
    query_info = jnp.stack([which, pair_rows, masked], axis=1)
    key_place = first_key + jnp.arange(window, dtype=jnp.int32)
    ends = jnp.cumsum(lengths)
    which_key = jnp.sum((ends[:, None] <= key_place[None, :]).astype(jnp.int32), axis=0)[None, :]

    proj = sum(partial_sums(0))
    turned = proj * cosine + jnp.roll(proj, HEAD // 2, axis=1) * sine
    kept_kv = jnp.where(side == 0, turned, proj).astype(jnp.bfloat16)
    kept_kv, last[1] = lax.optimization_barrier((kept_kv, last[1]))
    along = [
        lax.ppermute(kept_kv, "z", [(i, (i + n) % zs) for i in range(zs)]) for n in range(1, zs)
    ]
    along, last[2] = lax.optimization_barrier((along, last[2]))
    along = jnp.concatenate([kept_kv, *along], axis=0)
    beside = lax.ppermute(along, "y", [(i, (i + 1) % ys) for i in range(ys)])
    here = jnp.concatenate([along, beside], axis=0)
    there = swap_core(here)

    kept, got = [], []
    for part in range(1, len(cuts)):
        partials = partial_sums(part)
        owned, other = attend(partials, cosine, sine, query_info, which_key, here, there, place)
        kept.append(owned)
        got.append(swap_core(other))
    kept = jnp.concatenate(kept, axis=1)
    got = jnp.concatenate(got, axis=1)
    return jnp.where(
        side == 0,
        jnp.concatenate([kept, got], axis=1),
        jnp.concatenate([got, kept], axis=1),
    )


def solution(mesh):
    groups, blks, cores = (mesh.shape[name] for name in ("groups", "blk", "dp"))
    ys = 2
    zs = blks // ys
    fine = Mesh(mesh.devices.reshape(groups, zs, ys, cores), ("groups", "z", "y", "dp"))
    placed = (
        P(("groups", "z", "y", "dp"), None),
        P(),
        P(("z", "y"), "dp"),
        P(("z", "y"), "dp"),
        P("groups"),
        P("groups"),
        P("groups"),
    )
    return jax.shard_map(
        functools.partial(on_device, groups, zs, ys),
        mesh=fine,
        in_specs=placed,
        out_specs=P(("groups", "z", "y", "dp"), None),
        check_vma=False,
    )
```

time: 185 us -> 171 us (0.924)
  starting transfers between devices: 55.9 us -> 37.9 us
  local copies, waits for them, and re-layouts: 13.1 us -> 16.3 us
  other arithmetic: 4.65 us -> 7.81 us
    ppermute x12 -> x9, waiting for transfers between devices: 29.4 us -> 1.92 us  [shift_square(): return lax.ppermute(block, ('groups', 'y'), route)]
    ppermute x22 -> x11, waiting for transfers between devices: 45.6 us -> 69.2 us  [the longest x2 53.6 us: hop_down(): lax.ppermute(block, 'z', [(i, i - 1) for i in range(1, zs - step + 1)])]
    ppermute x22 -> x11, starting transfers between devices: 39 us -> 20.5 us  [the longest x2 7.09 us: hop_up(): lax.ppermute(block, 'z', [(i, i + 1) for i in range(step - 1, zs - 1)])]
    unnamed x80 -> x50, local copies, waits for them, and re-layouts: 8.51 us -> 14 us
    all_to_all x0 -> x1, starting transfers between devices: none -> 5.29 us  [on_device(): mine = lax.all_to_all(normed, ('groups', 'y'), 0, 0, tiled=True)]
    ppermute x12 -> x9, starting transfers between devices: 15.7 us -> 11.9 us  [shift_square(): return lax.ppermute(block, ('groups', 'y'), route)]
    select_n x0 -> x2, other arithmetic: none -> 3.41 us  [on_device(): jnp.where(z == 1, came[0][:, a:a + n], came[1][:, a:a + n])]
    ppermute x8 -> x4, waiting for transfers between devices: 1.16 us -> 4.04 us  [swap_core(): return lax.ppermute(block, 'dp', [(0, 1), (1, 0)])]
  transfers between devices with their start and end apart: 42 -> 25, of which waited for: 13 -> 8; matrix products, arithmetic and copies ran while one was open for 4% -> 5% of each run, Pallas kernels for 18% -> 17%
where the time goes in v3:
time: 171 us
  waiting for transfers between devices  75.2 us (44%)
  starting transfers between devices  37.9 us (22%)
  Pallas kernels  32.8 us (19%)
  local copies, waits for them, and re-layouts  16.3 us (10%)
  other arithmetic  7.81 us (5%)
    ppermute x2, waiting for transfers between devices, hop_down(): lax.ppermute(block, 'z', [(i, i - 1) for i in range(1, zs - step + 1)])  53.6 us
    pallas_call x2, Pallas kernels, collect(): pl.pallas_call(functools.partial(collect_kernel, zs, ys, groups, list(pie...  15.1 us
    unnamed x50, local copies, waits for them, and re-layouts  14 us
    ppermute x9, starting transfers between devices, shift_square(): return lax.ppermute(block, ('groups', 'y'), route)  11.9 us
    ppermute x3, waiting for transfers between devices, hop_ends(): return lax.ppermute(block, 'z', [(1, 0), (zs - 2, zs - 1)])  10.7 us
    pallas_call x3, Pallas kernels, finish(): pl.pallas_call(functools.partial(finish_kernel, ys, groups, cuts), grid=(...  8.32 us
    pallas_call x2, Pallas kernels, attend(): pl.pallas_call(functools.partial(attend_kernel, len(partials), window), g...  7.3 us
    ppermute x2, starting transfers between devices, hop_up(): lax.ppermute(block, 'z', [(i, i + 1) for i in range(step - 1, zs - 1)])  7.09 us
  transfers between devices with their start and end apart: 25, of which 8 were waited for; matrix products, arithmetic and copies ran while one was open for 5% of the time, Pallas kernels for 17%

profile of v3, /device:TPU:0, one launch (start us, length us, event | category | flops | bytes accessed | tf_op | source)
XLA Modules:
  0.0 170.5 jit_solution(5313920551744377477)
XLA Ops:
  0.9 2.2 %copy-done.6 = bf16[128,16384]{1,0:T(8,128)(2,1)S(1)} copy-done((bf16[128,16384]{1,0:T(8,128)(2,1)S(1)}, bf16[128,16384]{1,0:T(8,128)(2,1)}, u32[]{:S(2)}) %copy-start.6) | copy-done | bytes 4194328
  3.1 2.1 %norm.1 = bf16[4,128,4096]{2,1,0:T(8,128)(2,1)S(1)} custom-call(bf16[128,16384]{1,0:T(8,128)(2,1)S(1)} %copy-done.6, f32[1,16384]{1,0:T(1,128)S(1)} %bitcast.6), custom_call_target="tpu_custom_call" | custom-call | flops 1 | bytes 1 | tf_op jit(solution)/shard_map/norm/pallas_call | solution.py:114
  5.2 2.0 %copy-done.1 = bf16[4,128,4096]{2,1,0:T(8,128)(2,1)} copy-done((bf16[4,128,4096]{2,1,0:T(8,128)(2,1)}, bf16[4,128,4096]{2,1,0:T(8,128)(2,1)S(1)}, u32[]{:S(2)}) %copy-start.1) | copy-done | bytes 4194328
  7.2 5.3 %all-to-all-start = ((bf16[4,128,4096]{2,1,0:T(8,128)(2,1)}), bf16[4,128,4096]{2,1,0:T(8,128)(2,1)}, u32[]{:S(2)}, u32[]{:S(2)}) async-start(bf16[4,128,4096]{2,1,0:T(8,128)(2,1)} %copy-done.1), calls=%async_computation | async-start | bytes 8388608 | tf_op jit(solution)/shard_map/all_to_all | solution.py:295
  14.1 5.4 %collective-permute-start.2 = (bf16[1024,640]{1,0:T(8,128)(2,1)S(1)}, bf16[1024,640]{1,0:T(8,128)(2,1)S(1)}, u32[]{:S(2)}, u32[]{:S(2)}) collective-permute-start(bf16[1024,640]{1,0:T(8,128)(2,1)S(1)} %pad_maximum_fusion.refs_2_), channel_id=1, source_target_pairs={{0,4},{4,8},{8,12},{1,5},{5,9},{9,13},{2,6},{6,10},{10,14},{3,7},{... | collective-permute-start | bytes 3932168 | tf_op jit(solution)/shard_map/hop1_up/ppermute | solution.py:62
  19.5 26.8 %collective-permute-done.refs_3_ = bf16[1024,640]{1,0:T(8,128)(2,1)S(1)} collective-permute-done((bf16[1024,640]{1,0:T(8,128)(2,1)S(1)}, bf16[1024,640]{1,0:T(8,128)(2,1)S(1)}, u32[]{:S(2)}, u32[]{:S(2)}) %collective-permute-start) | collective-permute-done | bytes 1310752 | tf_op jit(solution)/shard_map/hop1_down/ppermute | solution.py:57
  48.6 1.7 %collective-permute-start.3 = (bf16[1024,640]{1,0:T(8,128)(2,1)S(1)}, bf16[1024,640]{1,0:T(8,128)(2,1)}, u32[]{:S(2)}, u32[]{:S(2)}) collective-permute-start(bf16[1024,640]{1,0:T(8,128)(2,1)S(1)} %collective-permute-done.2.refs_4_), channel_id=1, source_target_pairs={{4,8},{8,12},{5,9},{9,13},{6,10},{10,14},{7,11},{11,15},{20,24},{2... | collective-permute-start | bytes 3932168 | tf_op jit(solution)/shard_map/hop2_up/ppermute | solution.py:62
  51.4 26.9 %collective-permute-done.1.refs_5_ = bf16[1024,640]{1,0:T(8,128)(2,1)} collective-permute-done((bf16[1024,640]{1,0:T(8,128)(2,1)S(1)}, bf16[1024,640]{1,0:T(8,128)(2,1)}, u32[]{:S(2)}, u32[]{:S(2)}) %collective-permute-start.1) | collective-permute-done | bytes 1310752 | tf_op jit(solution)/shard_map/hop2_down/ppermute | solution.py:57
  79.4 1.8 %slice_select_fusion.2 = bf16[1024,128]{1,0:T(8,128)(2,1)} fusion(bf16[1024,640]{1,0:T(8,128)(2,1)} %collective-permute-done.3.refs_6_, bf16[1024,640]{1,0:T(8,128)(2,1)} %collective-permute-done.1.refs_5_, pred[]{:T(512)S(6)} %eq.29), kind=kLoop, calls=%fused_computation.5 | loop fusion | flops 131072 | bytes 786433 | tf_op jit(solution)/shard_map/jit(_where)/select_n | solution.py:309
  83.0 2.8 %collective-permute-done.4.refs_1_.others = bf16[4,128,4096]{2,1,0:T(8,128)(2,1)} collective-permute-done((bf16[4,128,4096]{2,1,0:T(8,128)(2,1)}, bf16[4,128,4096]{2,1,0:T(8,128)(2,1)}, u32[]{:S(2)}, u32[]{:S(2)}) %collective-permute-start.4) | collective-permute-done | bytes 4194336 | tf_op jit(solution)/shard_map/ppermute | solution.py:48
  88.4 6.5 %collect.2.sums = f32[1024,128]{1,0:T(8,128)S(1)} custom-call(bf16[4,128,4096]{2,1,0:T(8,128)(2,1)} %all-to-all-done.refs_0_.mine, bf16[4,128,4096]{2,1,0:T(8,128)(2,1)} %collective-permute-done.4.refs_1_.others, bf16[1024,640]{1,0:T(8,128)(2,1)S(1)} %pad_maximum_fusion.refs_2_, bf16[1024,640]{1,0:T(8,128)(2,1)S(1)} %copy-done.3, ...), custom_call_target="tpu_custom_call" | custom-call | flops 1 | bytes 1 | tf_op jit(solution)/shard_map/collect/pallas_call | solution.py:166
  95.0 2.3 %finish.3 = (f32[256,128]{1,0:T(8,128)S(1)}, f32[256,128]{1,0:T(8,128)S(1)}, f32[256,128]{1,0:T(8,128)S(1)}, f32[256,128]{1,0:T(8,128)S(1)}) custom-call(bf16[4,128,4096]{2,1,0:T(8,128)(2,1)} %all-to-all-done.refs_0_.mine, bf16[4,128,4096]{2,1,0:T(8,128)(2,1)} %collective-permute-done.4.refs_1_.others, bf16[1024,128]{1,0:T(8,128)(2,1)} %collective-permute-done.5.last, ...), custom_call_target="tpu_custom_call" | custom-call | flops 1 | bytes 1 | tf_op jit(solution)/shard_map/finish/pallas_call | solution.py:198
  105.1 8.6 %collect.3 = (f32[1024,256]{1,0:T(8,128)S(1)}, f32[1024,256]{1,0:T(8,128)S(1)}) custom-call(bf16[4,128,4096]{2,1,0:T(8,128)(2,1)} %all-to-all-done.refs_0_.mine, bf16[4,128,4096]{2,1,0:T(8,128)(2,1)} %collective-permute-done.4.refs_1_.others, bf16[1024,640]{1,0:T(8,128)(2,1)S(1)} %pad_maximum_fusion.refs_2_, bf16[1024,640]{1,0:T(8,128)(2,1)S(1)} %copy-done.3, ...), custom_call_target="tpu_custom_call" | custom-call | flops 1 | bytes 1 | tf_op jit(solution)/shard_map/collect/pallas_call | solution.py:166
  114.1 7.1 %collective-permute-done.9.last = bf16[1024,256]{1,0:T(8,128)(2,1)S(1)} collective-permute-done((bf16[1024,256]{1,0:T(8,128)(2,1)S(1)}, bf16[1024,256]{1,0:T(8,128)(2,1)S(1)}, u32[]{:S(2)}, u32[]{:S(2)}) %collective-permute-start.9) | collective-permute-done | bytes 524320 | tf_op jit(solution)/shard_map/hop_ends/ppermute | solution.py:67
  121.2 5.0 %collective-permute-start.14 = (bf16[256,128]{1,0:T(8,128)(2,1)S(1)}, bf16[256,128]{1,0:T(8,128)(2,1)S(1)}, u32[]{:S(2)}, u32[]{:S(2)}) collective-permute-start(bf16[256,128]{1,0:T(8,128)(2,1)S(1)} %get-tuple-element.47), channel_id=1, source_target_pairs={{0,8},{4,12},{8,0},{12,4},{1,9},{5,13},{9,1},{13,5},{2,10},{6,14},... | collective-permute-start | bytes 196616 | tf_op jit(solution)/shard_map/ppermute | solution.py:338
  126.6 3.0 %finish.4 = (f32[256,256]{1,0:T(8,128)S(1)}, f32[256,256]{1,0:T(8,128)S(1)}, f32[256,256]{1,0:T(8,128)S(1)}, f32[256,256]{1,0:T(8,128)}) custom-call(bf16[4,128,4096]{2,1,0:T(8,128)(2,1)} %all-to-all-done.refs_0_.mine, bf16[4,128,4096]{2,1,0:T(8,128)(2,1)} %collective-permute-done.4.refs_1_.others, bf16[1024,256]{1,0:T(8,128)(2,1)S(1)} %collective-permute-done.9.last, ...), custom_call_target="tpu_custom_call" | custom-call | flops 1 | bytes 1 | tf_op jit(solution)/shard_map/finish/pallas_call | solution.py:198
  130.9 3.6 %collective-permute-done.16.last = bf16[1024,256]{1,0:T(8,128)(2,1)S(1)} collective-permute-done((bf16[1024,256]{1,0:T(8,128)(2,1)S(1)}, bf16[1024,256]{1,0:T(8,128)(2,1)S(1)}, u32[]{:S(2)}, u32[]{:S(2)}) %collective-permute-start.16) | collective-permute-done | bytes 524320 | tf_op jit(solution)/shard_map/hop_ends/ppermute | solution.py:67
  137.5 4.9 %collective-permute-done.17 = bf16[1024,128]{1,0:T(8,128)(2,1)S(1)} collective-permute-done((bf16[1024,128]{1,0:T(8,128)(2,1)S(1)}, bf16[1024,128]{1,0:T(8,128)(2,1)S(1)}, u32[]{:S(2)}, u32[]{:S(2)}) %collective-permute-start.17) | collective-permute-done | bytes 262176 | tf_op jit(solution)/shard_map/ppermute | solution.py:342
  142.6 2.1 %collective-permute-start.12 = (f32[256,256]{1,0:T(8,128)}, f32[256,256]{1,0:T(8,128)}, u32[]{:S(2)}, u32[]{:S(2)}) collective-permute-start(f32[256,256]{1,0:T(8,128)} %get-tuple-element.46), channel_id=1, source_target_pairs={{0,18},{2,16},{16,2},{18,0},{1,19},{3,17},{17,3},{19,1},{4,22},{6,... | collective-permute-start | bytes 786440 | tf_op jit(solution)/shard_map/ppermute | solution.py:44
  144.7 3.1 %finish.5 = (f32[256,256]{1,0:T(8,128)S(1)}, f32[256,256]{1,0:T(8,128)}, f32[256,256]{1,0:T(8,128)}, f32[256,256]{1,0:T(8,128)}) custom-call(bf16[4,128,4096]{2,1,0:T(8,128)(2,1)} %all-to-all-done.refs_0_.mine, bf16[4,128,4096]{2,1,0:T(8,128)(2,1)} %collective-permute-done.4.refs_1_.others, bf16[1024,256]{1,0:T(8,128)(2,1)S(1)} %collective-permute-done.16.last, ...), custom_call_target="tpu_custom_call" | custom-call | flops 1 | bytes 1 | tf_op jit(solution)/shard_map/finish/pallas_call | solution.py:198
  151.3 2.1 %collective-permute-start.21 = (f32[256,256]{1,0:T(8,128)}, f32[256,256]{1,0:T(8,128)}, u32[]{:S(2)}, u32[]{:S(2)}) collective-permute-start(f32[256,256]{1,0:T(8,128)} %get-tuple-element.57), channel_id=1, source_target_pairs={{0,18},{2,16},{16,2},{18,0},{1,19},{3,17},{17,3},{19,1},{4,22},{6,... | collective-permute-start | bytes 786440 | tf_op jit(solution)/shard_map/ppermute | solution.py:44
  159.1 3.6 %attend.2 = (bf16[128,256]{1,0:T(8,128)(2,1)S(1)}, bf16[128,256]{1,0:T(8,128)(2,1)S(1)}) custom-call(s32[9]{0:T(128)S(1)} %concatenate.33.place, f32[256,256]{1,0:T(8,128)S(1)} %copy-done.8, f32[256,256]{1,0:T(8,128)S(1)} %copy-done.10, f32[256,256]{1,0:T(8,128)S(1)} %copy-done.12, f32[256,256]{1,0:T(8,128)} %collective-permute-done.12.refs_3_, ...), custom_call_target="tpu_custom_call" | custom-call | flops 1 | bytes 1 | tf_op jit(solution)/shard_map/attend/pallas_call | solution.py:252
  162.8 1.9 %collective-permute-done.21.refs_3_ = f32[256,256]{1,0:T(8,128)} collective-permute-done((f32[256,256]{1,0:T(8,128)}, f32[256,256]{1,0:T(8,128)}, u32[]{:S(2)}, u32[]{:S(2)}) %collective-permute-start.21) | collective-permute-done | bytes 262176 | tf_op jit(solution)/shard_map/ppermute | solution.py:44
  164.7 3.7 %attend.3 = (bf16[128,256]{1,0:T(8,128)(2,1)S(1)}, bf16[128,256]{1,0:T(8,128)(2,1)S(1)}) custom-call(s32[9]{0:T(128)S(1)} %concatenate.33.place, f32[256,256]{1,0:T(8,128)S(1)} %copy-done.14, f32[256,256]{1,0:T(8,128)} %collective-permute-done.19.refs_1_, f32[256,256]{1,0:T(8,128)} %collective-permute-done.20.refs_2_, ...), custom_call_target="tpu_custom_call" | custom-call | flops 1 | bytes 1 | tf_op jit(solution)/shard_map/attend/pallas_call | solution.py:252
  (116 shorter events, 35.7 us)
Async XLA Ops:
  7.2 71.1 %all-to-all-start = ((bf16[4,128,4096]{2,1,0:T(8,128)(2,1)}), bf16[4,128,4096]{2,1,0:T(8,128)(2,1)}, u32[]{:S(2)}, u32[]{:S(2)}) async-start(bf16[4,128,4096]{2,1,0:T(8,128)(2,1)} %copy-done.1), calls=%async_computation | async-start | bytes 8388608 | tf_op jit(solution)/shard_map/all_to_all | solution.py:295
  12.8 33.4 %collective-permute-start = (bf16[1024,640]{1,0:T(8,128)(2,1)S(1)}, bf16[1024,640]{1,0:T(8,128)(2,1)S(1)}, u32[]{:S(2)}, u32[]{:S(2)}) collective-permute-start(bf16[1024,640]{1,0:T(8,128)(2,1)S(1)} %pad_maximum_fusion.refs_2_), channel_id=1, source_target_pairs={{4,0},{8,4},{12,8},{5,1},{9,5},{13,9},{6,2},{10,6},{14,10},{7,3},{... | collective-permute-start | bytes 3932168 | tf_op jit(solution)/shard_map/hop1_down/ppermute | solution.py:57
  14.1 34.5 %collective-permute-start.2 = (bf16[1024,640]{1,0:T(8,128)(2,1)S(1)}, bf16[1024,640]{1,0:T(8,128)(2,1)S(1)}, u32[]{:S(2)}, u32[]{:S(2)}) collective-permute-start(bf16[1024,640]{1,0:T(8,128)(2,1)S(1)} %pad_maximum_fusion.refs_2_), channel_id=1, source_target_pairs={{0,4},{4,8},{8,12},{1,5},{5,9},{9,13},{2,6},{6,10},{10,14},{3,7},{... | collective-permute-start | bytes 3932168 | tf_op jit(solution)/shard_map/hop1_up/ppermute | solution.py:62
  46.2 32.1 %collective-permute-start.1 = (bf16[1024,640]{1,0:T(8,128)(2,1)S(1)}, bf16[1024,640]{1,0:T(8,128)(2,1)}, u32[]{:S(2)}, u32[]{:S(2)}) collective-permute-start(bf16[1024,640]{1,0:T(8,128)(2,1)S(1)} %collective-permute-done.refs_3_), channel_id=1, source_target_pairs={{4,0},{8,4},{5,1},{9,5},{6,2},{10,6},{7,3},{11,7},{20,16},{24,20},... | collective-permute-start | bytes 3932168 | tf_op jit(solution)/shard_map/hop2_down/ppermute | solution.py:57
  48.6 29.7 %collective-permute-start.3 = (bf16[1024,640]{1,0:T(8,128)(2,1)S(1)}, bf16[1024,640]{1,0:T(8,128)(2,1)}, u32[]{:S(2)}, u32[]{:S(2)}) collective-permute-start(bf16[1024,640]{1,0:T(8,128)(2,1)S(1)} %collective-permute-done.2.refs_4_), channel_id=1, source_target_pairs={{4,8},{8,12},{5,9},{9,13},{6,10},{10,14},{7,11},{11,15},{20,24},{2... | collective-permute-start | bytes 3932168 | tf_op jit(solution)/shard_map/hop2_up/ppermute | solution.py:62
  78.3 7.5 %collective-permute-start.4 = (bf16[4,128,4096]{2,1,0:T(8,128)(2,1)}, bf16[4,128,4096]{2,1,0:T(8,128)(2,1)}, u32[]{:S(2)}, u32[]{:S(2)}) collective-permute-start(bf16[4,128,4096]{2,1,0:T(8,128)(2,1)} %all-to-all-done.refs_0_.mine), channel_id=1, source_target_pairs={{0,1},{1,0},{2,3},{3,2},{4,5},{5,4},{6,7},{7,6},{8,9},{9,8},{10,11... | collective-permute-start | bytes 12582920 | tf_op jit(solution)/shard_map/ppermute | solution.py:48
  81.2 13.8 %collective-permute-start.5 = (bf16[1024,128]{1,0:T(8,128)(2,1)}, bf16[1024,128]{1,0:T(8,128)(2,1)}, u32[]{:S(2)}, u32[]{:S(2)}) collective-permute-start(bf16[1024,128]{1,0:T(8,128)(2,1)} %slice_select_fusion.2), channel_id=1, source_target_pairs={{4,0},{8,12},{5,1},{9,13},{6,2},{10,14},{7,3},{11,15},{20,16},{24,... | collective-permute-start | bytes 786440 | tf_op jit(solution)/shard_map/hop_ends/ppermute | solution.py:67
  97.3 16.4 %collective-permute-start.6 = (f32[256,128]{1,0:T(8,128)S(1)}, f32[256,128]{1,0:T(8,128)S(1)}, u32[]{:S(2)}, u32[]{:S(2)}) collective-permute-start(f32[256,128]{1,0:T(8,128)S(1)} %get-tuple-element.38), channel_id=1, source_target_pairs={{0,2},{2,0},{16,18},{18,16},{1,3},{3,1},{17,19},{19,17},{4,6},{6,4... | collective-permute-start | bytes 393224 | tf_op jit(solution)/shard_map/ppermute | solution.py:44
  98.7 15.0 %collective-permute-start.7 = (f32[256,128]{1,0:T(8,128)S(1)}, f32[256,128]{1,0:T(8,128)S(1)}, u32[]{:S(2)}, u32[]{:S(2)}) collective-permute-start(f32[256,128]{1,0:T(8,128)S(1)} %get-tuple-element.39), channel_id=1, source_target_pairs={{0,16},{2,18},{16,0},{18,2},{1,17},{3,19},{17,1},{19,3},{4,20},{6,... | collective-permute-start | bytes 393224 | tf_op jit(solution)/shard_map/ppermute | solution.py:44
  100.2 13.6 %collective-permute-start.8 = (f32[256,128]{1,0:T(8,128)S(1)}, f32[256,128]{1,0:T(8,128)S(1)}, u32[]{:S(2)}, u32[]{:S(2)}) collective-permute-start(f32[256,128]{1,0:T(8,128)S(1)} %get-tuple-element.40), channel_id=1, source_target_pairs={{0,18},{2,16},{16,2},{18,0},{1,19},{3,17},{17,3},{19,1},{4,22},{6,... | collective-permute-start | bytes 393224 | tf_op jit(solution)/shard_map/ppermute | solution.py:44
  102.5 18.7 %collective-permute-start.9 = (bf16[1024,256]{1,0:T(8,128)(2,1)S(1)}, bf16[1024,256]{1,0:T(8,128)(2,1)S(1)}, u32[]{:S(2)}, u32[]{:S(2)}) collective-permute-start(bf16[1024,256]{1,0:T(8,128)(2,1)S(1)} %get-tuple-element.66), channel_id=1, source_target_pairs={{4,0},{8,12},{5,1},{9,13},{6,2},{10,14},{7,3},{11,15},{20,16},{24,... | collective-permute-start | bytes 1572872 | tf_op jit(solution)/shard_map/hop_ends/ppermute | solution.py:67
  103.8 30.7 %collective-permute-start.16 = (bf16[1024,256]{1,0:T(8,128)(2,1)S(1)}, bf16[1024,256]{1,0:T(8,128)(2,1)S(1)}, u32[]{:S(2)}, u32[]{:S(2)}) collective-permute-start(bf16[1024,256]{1,0:T(8,128)(2,1)S(1)} %get-tuple-element.65), channel_id=1, source_target_pairs={{4,0},{8,12},{5,1},{9,13},{6,2},{10,14},{7,3},{11,15},{20,16},{24,... | collective-permute-start | bytes 1572872 | tf_op jit(solution)/shard_map/hop_ends/ppermute | solution.py:67
  121.2 14.7 %collective-permute-start.13 = (bf16[256,128]{1,0:T(8,128)(2,1)S(1)}, bf16[256,128]{1,0:T(8,128)(2,1)S(1)}, u32[]{:S(2)}, u32[]{:S(2)}) collective-permute-start(bf16[256,128]{1,0:T(8,128)(2,1)S(1)} %get-tuple-element.47), channel_id=1, source_target_pairs={{0,4},{4,8},{8,12},{12,0},{1,5},{5,9},{9,13},{13,1},{2,6},{6,10},{... | collective-permute-start | bytes 196616 | tf_op jit(solution)/shard_map/ppermute | solution.py:338
  121.2 14.7 %collective-permute-start.14 = (bf16[256,128]{1,0:T(8,128)(2,1)S(1)}, bf16[256,128]{1,0:T(8,128)(2,1)S(1)}, u32[]{:S(2)}, u32[]{:S(2)}) collective-permute-start(bf16[256,128]{1,0:T(8,128)(2,1)S(1)} %get-tuple-element.47), channel_id=1, source_target_pairs={{0,8},{4,12},{8,0},{12,4},{1,9},{5,13},{9,1},{13,5},{2,10},{6,14},... | collective-permute-start | bytes 196616 | tf_op jit(solution)/shard_map/ppermute | solution.py:338
  126.2 9.7 %collective-permute-start.15 = (bf16[256,128]{1,0:T(8,128)(2,1)S(1)}, bf16[256,128]{1,0:T(8,128)(2,1)S(1)}, u32[]{:S(2)}, u32[]{:S(2)}) collective-permute-start(bf16[256,128]{1,0:T(8,128)(2,1)S(1)} %get-tuple-element.47), channel_id=1, source_target_pairs={{0,12},{4,0},{8,4},{12,8},{1,13},{5,1},{9,5},{13,9},{2,14},{6,2},{... | collective-permute-start | bytes 196616 | tf_op jit(solution)/shard_map/ppermute | solution.py:338
  129.6 19.5 %collective-permute-start.10 = (f32[256,256]{1,0:T(8,128)S(1)}, f32[256,256]{1,0:T(8,128)S(1)}, u32[]{:S(2)}, u32[]{:S(2)}) collective-permute-start(f32[256,256]{1,0:T(8,128)S(1)} %get-tuple-element.44), channel_id=1, source_target_pairs={{0,2},{2,0},{16,18},{18,16},{1,3},{3,1},{17,19},{19,17},{4,6},{6,4... | collective-permute-start | bytes 786440 | tf_op jit(solution)/shard_map/ppermute | solution.py:44
  134.5 16.1 %collective-permute-start.11 = (f32[256,256]{1,0:T(8,128)S(1)}, f32[256,256]{1,0:T(8,128)S(1)}, u32[]{:S(2)}, u32[]{:S(2)}) collective-permute-start(f32[256,256]{1,0:T(8,128)S(1)} %get-tuple-element.45), channel_id=1, source_target_pairs={{0,16},{2,18},{16,0},{18,2},{1,17},{3,19},{17,1},{19,3},{4,20},{6,... | collective-permute-start | bytes 786440 | tf_op jit(solution)/shard_map/ppermute | solution.py:44
  135.9 6.4 %collective-permute-start.17 = (bf16[1024,128]{1,0:T(8,128)(2,1)S(1)}, bf16[1024,128]{1,0:T(8,128)(2,1)S(1)}, u32[]{:S(2)}, u32[]{:S(2)}) collective-permute-start(bf16[1024,128]{1,0:T(8,128)(2,1)S(1)} %pad_maximum_fusion.1), channel_id=1, source_target_pairs={{0,2},{2,0},{1,3},{3,1},{4,6},{6,4},{5,7},{7,5},{8,10},{10,8},{9,1... | collective-permute-start | bytes 786440 | tf_op jit(solution)/shard_map/ppermute | solution.py:342
  142.4 13.9 %collective-permute-start.18 = (bf16[2048,128]{1,0:T(8,128)(2,1)S(1)}, bf16[2048,128]{1,0:T(8,128)(2,1)S(1)}, u32[]{:S(2)}, u32[]{:S(2)}) collective-permute-start(bf16[2048,128]{1,0:T(8,128)(2,1)S(1)} %constant_dynamic-update-slice_fusion.refs_8_), channel_id=1, source_target_pairs={{0,1},{1,0},{2,3},{3,2},{4,5},{5,4},{6,7},{7,6},{8,9},{9,8},{10,11... | collective-permute-start | bytes 1572872 | tf_op jit(solution)/shard_map/ppermute | solution.py:48
  142.6 13.7 %collective-permute-start.12 = (f32[256,256]{1,0:T(8,128)}, f32[256,256]{1,0:T(8,128)}, u32[]{:S(2)}, u32[]{:S(2)}) collective-permute-start(f32[256,256]{1,0:T(8,128)} %get-tuple-element.46), channel_id=1, source_target_pairs={{0,18},{2,16},{16,2},{18,0},{1,19},{3,17},{17,3},{19,1},{4,22},{6,... | collective-permute-start | bytes 786440 | tf_op jit(solution)/shard_map/ppermute | solution.py:44
  148.5 14.3 %collective-permute-start.19 = (f32[256,256]{1,0:T(8,128)}, f32[256,256]{1,0:T(8,128)}, u32[]{:S(2)}, u32[]{:S(2)}) collective-permute-start(f32[256,256]{1,0:T(8,128)} %get-tuple-element.55), channel_id=1, source_target_pairs={{0,2},{2,0},{16,18},{18,16},{1,3},{3,1},{17,19},{19,17},{4,6},{6,4... | collective-permute-start | bytes 786440 | tf_op jit(solution)/shard_map/ppermute | solution.py:44
  149.8 13.0 %collective-permute-start.20 = (f32[256,256]{1,0:T(8,128)}, f32[256,256]{1,0:T(8,128)}, u32[]{:S(2)}, u32[]{:S(2)}) collective-permute-start(f32[256,256]{1,0:T(8,128)} %get-tuple-element.56), channel_id=1, source_target_pairs={{0,16},{2,18},{16,0},{18,2},{1,17},{3,19},{17,1},{19,3},{4,20},{6,... | collective-permute-start | bytes 786440 | tf_op jit(solution)/shard_map/ppermute | solution.py:44
  151.3 13.4 %collective-permute-start.21 = (f32[256,256]{1,0:T(8,128)}, f32[256,256]{1,0:T(8,128)}, u32[]{:S(2)}, u32[]{:S(2)}) collective-permute-start(f32[256,256]{1,0:T(8,128)} %get-tuple-element.57), channel_id=1, source_target_pairs={{0,18},{2,16},{16,2},{18,0},{1,19},{3,17},{17,3},{19,1},{4,22},{6,... | collective-permute-start | bytes 786440 | tf_op jit(solution)/shard_map/ppermute | solution.py:44
  162.7 5.8 %collective-permute-start.22 = (bf16[128,256]{1,0:T(8,128)(2,1)S(1)}, bf16[128,256]{1,0:T(8,128)(2,1)S(1)}, u32[]{:S(2)}, u32[]{:S(2)}) collective-permute-start(bf16[128,256]{1,0:T(8,128)(2,1)S(1)} %get-tuple-element.59), channel_id=1, source_target_pairs={{0,1},{1,0},{2,3},{3,2},{4,5},{5,4},{6,7},{7,6},{8,9},{9,8},{10,11... | collective-permute-start | bytes 196616 | tf_op jit(solution)/shard_map/ppermute | solution.py:48
  (24 other events, 251.6 us)

commit v4 on v3

--- a/solution.py
+++ b/solution.py
@@ -174,7 +174,7 @@
     )(*operands)
 
 
-def finish_kernel(ys, groups, cuts, mine, others, last, sums, *outs):
+def finish_kernel(ys, groups, layout, mine, others, last, sums, *outs):
     side = lax.axis_index("dp")
     peers, count = mine.shape[:2]
     index = peer_order(ys, groups, peers)
@@ -182,21 +182,20 @@
     total = sums[...] + jnp.dot(rows, last[...], preferred_element_type=jnp.float32)
     here = pl.multiple_of(side * count, count)
     there = pl.multiple_of((1 - side) * count, count)
-    for at, out in enumerate(outs):
-        first, size = cuts[at // peers]
-        peer = at % peers
+    for (first, size, which), out in zip(layout, outs):
         part = total[:, first : first + size]
-        out[pl.ds(here, count), :] = part[peer * count : (peer + 1) * count]
-        out[pl.ds(there, count), :] = part[(peers + peer) * count : (peers + peer + 1) * count]
-
-
-def finish(mine, others, last, sums, cuts, ys, groups):
+        for at, peer in enumerate(which):
+            out[at, pl.ds(here, count), :] = part[peer * count : (peer + 1) * count]
+            out[at, pl.ds(there, count), :] = part[(peers + peer) * count : (peers + peer + 1) * count]
+
+
+def finish(mine, others, last, sums, layout, ys, groups):
     peers, count, columns = mine.shape
     width = last.shape[0]
     tokens = pl.BlockSpec((peers, count, width), lambda i: (0, 0, columns // width - 1))
-    sizes = [size for _, size in cuts for _ in range(peers)]
-    outs = pl.pallas_call(
-        functools.partial(finish_kernel, ys, groups, cuts),
+    shapes = [(len(which), 2 * count, size) for _, size, which in layout]
+    return pl.pallas_call(
+        functools.partial(finish_kernel, ys, groups, layout),
         grid=(1,),
         in_specs=[
             tokens,
@@ -204,13 +203,12 @@
             pl.BlockSpec(last.shape, lambda i: (0, 0)),
             pl.BlockSpec(sums.shape, lambda i: (0, 0)),
         ],
-        out_specs=[pl.BlockSpec((2 * count, size), lambda i: (0, 0)) for size in sizes],
-        out_shape=[jax.ShapeDtypeStruct((2 * count, size), jnp.float32) for size in sizes],
+        out_specs=[pl.BlockSpec(shape, lambda i: (0, 0, 0)) for shape in shapes],
+        out_shape=[jax.ShapeDtypeStruct(shape, jnp.float32) for shape in shapes],
         compiler_params=pltpu.CompilerParams(vmem_limit_bytes=32 * MIB),
         cost_estimate=COST,
         name="finish",
     )(mine, others, last, sums)
-    return [outs[at * peers : (at + 1) * peers] for at in range(len(cuts))]
 
 
 def attend_kernel(peers, window, place, *refs):
@@ -279,7 +277,7 @@
     window = min(tokens_all // 2 + pair, tokens_all)
     first_key = jnp.maximum(pair_base - tokens_all // 2, 0)
     key_blk = first_key // pair + jnp.arange(window // pair, dtype=jnp.int32)
-    spot = (blk % ys + ys - key_blk % ys) % ys * zs + (z + zs - key_blk // ys) % zs
+    spot = (blk % ys + ys - key_blk % ys) % ys + (z + zs - key_blk // ys) % zs * ys
     place = jnp.concatenate(
         [jnp.stack([side, own_slot, other_slot, first_key]).astype(jnp.int32), spot * pair]
     )
@@ -292,36 +290,6 @@
         axis=1,
     )
     normed = norm_pieces(tokens, gain, zs, ys, groups, width)
-    mine = lax.all_to_all(normed, ("groups", "y"), 0, 0, tiled=True)
-    pieces = {("own", 0): own}
-    came = [after(own, normed), after(own, normed)]
-    for step in range(1, zs - 1):
-        came = [hop_down(came[0], step, zs), hop_up(came[1], step, zs)]
-        pieces["down", step], pieces["up", step] = came
-    done = (mine, *came)
-    others = swap_core(after(mine, *done))
-    came = [after(came[0], *done), after(came[1], *done)]
-    cuts, first = [(0, HEAD)], HEAD
-    for heads in CHUNK_HEADS:
-        cuts.append((first, heads * HEAD))
-        first += heads * HEAD
-    last = [
-        hop_ends(jnp.where(z == 1, came[0][:, a : a + n], came[1][:, a : a + n]), zs)
-        for a, n in cuts
-    ]
-    sums = [
-        *collect(mine, others, pieces, cuts[:1], zs, ys, groups),
-        *collect(mine, others, pieces, cuts[1:], zs, ys, groups),
-    ]
-
-    def partial_sums(part):
-        inner = [(0, cuts[part][1])]
-        (parts,) = finish(mine, others, last[part], sums[part], inner, ys, groups)
-        return [
-            shift_square(part_of, -dx, -dy, groups, ys) if dx or dy else part_of
-            for (dx, dy), part_of in zip(peers, parts)
-        ]
-
     pair_rows = pair_base + jnp.arange(pair, dtype=jnp.int32)
     which, offset, masked = rollout_info(pair_rows, lengths, overlong)
     cosine, sine = rotation(offset)
@@ -329,24 +297,63 @@
     key_place = first_key + jnp.arange(window, dtype=jnp.int32)
     ends = jnp.cumsum(lengths)
     which_key = jnp.sum((ends[:, None] <= key_place[None, :]).astype(jnp.int32), axis=0)[None, :]
-
-    proj = sum(partial_sums(0))
+    tables = (cosine, sine, query_info, which_key, place)
+
+    mine = lax.all_to_all(normed, ("groups", "y"), 0, 0, tiled=True)
+    pieces = {("own", 0): own}
+    came = [after(own, normed), after(own, normed)]
+    for step in range(1, zs - 1):
+        came = [hop_down(came[0], step, zs), hop_up(came[1], step, zs)]
+        pieces["down", step], pieces["up", step] = came
+    done = (mine, *came, *tables)
+    others = swap_core(after(mine, *done))
+    came = [after(came[0], *done), after(came[1], *done)]
+    cosine, sine, query_info, which_key, place = lax.optimization_barrier((*tables, mine))[:5]
+    cuts, first = [(0, HEAD)], HEAD
+    for heads in CHUNK_HEADS:
+        cuts.append((first, heads * HEAD))
+        first += heads * HEAD
+    parts = [cuts[0], (HEAD, own.shape[1] - HEAD)]
+    last = [
+        hop_ends(jnp.where(z == 1, came[0][:, a : a + n], came[1][:, a : a + n]), zs)
+        for a, n in parts
+    ]
+    sums = [collect(mine, others, pieces, [part], zs, ys, groups)[0] for part in parts]
+
+    def to_owner(part, dx, dy):
+        return shift_square(part, -dx, -dy, groups, ys) if dx or dy else part
+
+    layout = [(0, HEAD, [at]) for at in range(len(peers))]
+    kv_parts = finish(mine, others, last[0], sums[0], layout, ys, groups)
+    proj = sum(to_owner(part[0], *peer) for part, peer in zip(kv_parts, peers))
     turned = proj * cosine + jnp.roll(proj, HEAD // 2, axis=1) * sine
     kept_kv = jnp.where(side == 0, turned, proj).astype(jnp.bfloat16)
     kept_kv, last[1] = lax.optimization_barrier((kept_kv, last[1]))
-    along = [
-        lax.ppermute(kept_kv, "z", [(i, (i + n) % zs) for i in range(zs)]) for n in range(1, zs)
-    ]
-    along, last[2] = lax.optimization_barrier((along, last[2]))
-    along = jnp.concatenate([kept_kv, *along], axis=0)
-    beside = lax.ppermute(along, "y", [(i, (i + 1) % ys) for i in range(ys)])
-    here = jnp.concatenate([along, beside], axis=0)
+    beside = lax.ppermute(kept_kv, "y", [(i, (i + 1) % ys) for i in range(ys)])
+
+    split = CHUNK_HEADS[0] * HEAD
+    rest = CHUNK_HEADS[1] * HEAD
+    layout = [(0, split, [dx * ys + dy for dy in range(ys)]) for dx in range(groups)]
+    layout += [(split, rest, [dx * ys + dy for dx in range(groups)]) for dy in range(ys)]
+    parts = finish(mine, others, last[1], sums[1], layout, ys, groups)
+    beside, *parts = lax.optimization_barrier((beside, *parts))
+    by_group = sum(to_owner(part, dx, 0) for dx, part in enumerate(parts[:groups]))
+    by_y = sum(to_owner(part, 0, dy) for dy, part in enumerate(parts[groups:]))
+    partials = [
+        [to_owner(by_group[dy], 0, dy) for dy in range(ys)],
+        [to_owner(by_y[dx], dx, 0) for dx in range(groups)],
+    ]
+
+    both = jnp.concatenate([kept_kv, beside], axis=0)
+    along = [both] + [
+        lax.ppermute(both, "z", [(i, (i + n) % zs) for i in range(zs)]) for n in range(1, zs)
+    ]
+    here = jnp.concatenate(along, axis=0)
     there = swap_core(here)
 
     kept, got = [], []
-    for part in range(1, len(cuts)):
-        partials = partial_sums(part)
-        owned, other = attend(partials, cosine, sine, query_info, which_key, here, there, place)
+    for part in partials:
+        owned, other = attend(part, cosine, sine, query_info, which_key, here, there, place)
         kept.append(owned)
         got.append(swap_core(other))
     kept = jnp.concatenate(kept, axis=1)

time: 171 us -> 155 us (0.906)
  waiting for transfers between devices: 75.2 us -> 66.7 us
  local copies, waits for them, and re-layouts: 16.3 us -> 10 us
    unnamed x50 -> x29, local copies, waits for them, and re-layouts: 14 us -> 5.9 us
    ppermute x3 -> x2, waiting for transfers between devices: 10.7 us -> 2.99 us  [hop_ends(): return lax.ppermute(block, 'z', [(1, 0), (zs - 2, zs - 1)])]
    ppermute x9 -> x7, waiting for transfers between devices: 1.92 us -> 6.27 us  [shift_square(): return lax.ppermute(block, ('groups', 'y'), route)]
    ppermute x9 -> x7, starting transfers between devices: 11.9 us -> 8.89 us  [shift_square(): return lax.ppermute(block, ('groups', 'y'), route)]
    ppermute x2, waiting for transfers between devices: 53.6 us -> 50.9 us  [hop_down(): lax.ppermute(block, 'z', [(i, i - 1) for i in range(1, zs - step + 1)])]
    pallas_call x3 -> x2, Pallas kernels: 8.32 us -> 6.02 us  [finish(): pl.pallas_call(functools.partial(finish_kernel, ys, groups, layout), grid...]
    ppermute x4, waiting for transfers between devices: 4.04 us -> 2.07 us  [swap_core(): return lax.ppermute(block, 'dp', [(0, 1), (1, 0)])]
    ppermute x4, starting transfers between devices: 6.95 us -> 8.69 us  [the longest x3 7.34 us: on_device(): lax.ppermute(both, 'z', [(i, (i + n) % zs) for i in range(zs)])]
  transfers between devices with their start and end apart: 25 -> 22, of which waited for: 8 -> 10; matrix products, arithmetic and copies ran while one was open for 5% -> 7% of each run, Pallas kernels for 17% -> 19%
where the time goes in v4:
time: 155 us
  waiting for transfers between devices  66.7 us (43%)
  starting transfers between devices  36.8 us (24%)
  Pallas kernels  31.9 us (21%)
  local copies, waits for them, and re-layouts  10 us (6%)
  other arithmetic  8.74 us (6%)
    ppermute x2, waiting for transfers between devices, hop_down(): lax.ppermute(block, 'z', [(i, i - 1) for i in range(1, zs - step + 1)])  50.9 us
    pallas_call x2, Pallas kernels, collect(): pl.pallas_call(functools.partial(collect_kernel, zs, ys, groups, list(pie...  16.7 us
    ppermute x7, starting transfers between devices, shift_square(): return lax.ppermute(block, ('groups', 'y'), route)  8.89 us
    ppermute x2, starting transfers between devices, hop_up(): lax.ppermute(block, 'z', [(i, i + 1) for i in range(step - 1, zs - 1)])  8.14 us
    ppermute x3, starting transfers between devices, on_device(): lax.ppermute(both, 'z', [(i, (i + n) % zs) for i in range(zs)])  7.34 us
    pallas_call x2, Pallas kernels, attend(): pl.pallas_call(functools.partial(attend_kernel, len(partials), window), g...  7.1 us
    ppermute x7, waiting for transfers between devices, shift_square(): return lax.ppermute(block, ('groups', 'y'), route)  6.27 us
    pallas_call x2, Pallas kernels, finish(): pl.pallas_call(functools.partial(finish_kernel, ys, groups, layout), grid...  6.02 us
  transfers between devices with their start and end apart: 22, of which 10 were waited for; matrix products, arithmetic and copies ran while one was open for 7% of the time, Pallas kernels for 19%

profile of v4, /device:TPU:0, one launch (start us, length us, event | category | flops | bytes accessed | tf_op | source)
XLA Modules:
  0.0 154.6 jit_solution(3059876645694525598)
XLA Ops:
  0.9 2.2 %copy-done.2 = bf16[128,16384]{1,0:T(8,128)(2,1)S(1)} copy-done((bf16[128,16384]{1,0:T(8,128)(2,1)S(1)}, bf16[128,16384]{1,0:T(8,128)(2,1)}, u32[]{:S(2)}) %copy-start.2) | copy-done | bytes 4194328
  3.1 2.1 %norm.1 = bf16[4,128,4096]{2,1,0:T(8,128)(2,1)S(1)} custom-call(bf16[128,16384]{1,0:T(8,128)(2,1)S(1)} %copy-done.2, f32[1,16384]{1,0:T(1,128)S(1)} %bitcast.23), custom_call_target="tpu_custom_call" | custom-call | flops 1 | bytes 1 | tf_op jit(solution)/shard_map/norm/pallas_call | solution.py:114
  5.2 2.0 %copy-done.1 = bf16[4,128,4096]{2,1,0:T(8,128)(2,1)} copy-done((bf16[4,128,4096]{2,1,0:T(8,128)(2,1)}, bf16[4,128,4096]{2,1,0:T(8,128)(2,1)S(1)}, u32[]{:S(2)}) %copy-start.1) | copy-done | bytes 4194328
  7.2 5.3 %all-to-all-start = ((bf16[4,128,4096]{2,1,0:T(8,128)(2,1)}), bf16[4,128,4096]{2,1,0:T(8,128)(2,1)}, u32[]{:S(2)}, u32[]{:S(2)}) async-start(bf16[4,128,4096]{2,1,0:T(8,128)(2,1)} %copy-done.1), calls=%async_computation | async-start | bytes 8388608 | tf_op jit(solution)/shard_map/all_to_all | solution.py:302
  14.1 6.4 %collective-permute-start.2 = (bf16[1024,640]{1,0:T(8,128)(2,1)S(1)}, bf16[1024,640]{1,0:T(8,128)(2,1)}, u32[]{:S(2)}, u32[]{:S(2)}) collective-permute-start(bf16[1024,640]{1,0:T(8,128)(2,1)S(1)} %pad_maximum_fusion.refs_2_), channel_id=1, source_target_pairs={{0,4},{4,8},{8,12},{1,5},{5,9},{9,13},{2,6},{6,10},{10,14},{3,7},{... | collective-permute-start | bytes 3932168 | tf_op jit(solution)/shard_map/hop1_up/ppermute | solution.py:62
  21.6 24.7 %collective-permute-done.refs_3_ = bf16[1024,640]{1,0:T(8,128)(2,1)} collective-permute-done((bf16[1024,640]{1,0:T(8,128)(2,1)S(1)}, bf16[1024,640]{1,0:T(8,128)(2,1)}, u32[]{:S(2)}, u32[]{:S(2)}) %collective-permute-start) | collective-permute-done | bytes 1310752 | tf_op jit(solution)/shard_map/hop1_down/ppermute | solution.py:57
  47.6 1.7 %collective-permute-start.3 = (bf16[1024,640]{1,0:T(8,128)(2,1)}, bf16[1024,640]{1,0:T(8,128)(2,1)}, u32[]{:S(2)}, u32[]{:S(2)}) collective-permute-start(bf16[1024,640]{1,0:T(8,128)(2,1)} %collective-permute-done.2.refs_4_), channel_id=1, source_target_pairs={{4,8},{8,12},{5,9},{9,13},{6,10},{10,14},{7,11},{11,15},{20,24},{2... | collective-permute-start | bytes 3932168 | tf_op jit(solution)/shard_map/hop2_up/ppermute | solution.py:62
  52.3 26.2 %collective-permute-done.1.refs_5_ = bf16[1024,640]{1,0:T(8,128)(2,1)} collective-permute-done((bf16[1024,640]{1,0:T(8,128)(2,1)}, bf16[1024,640]{1,0:T(8,128)(2,1)}, u32[]{:S(2)}, u32[]{:S(2)}) %collective-permute-start.1) | collective-permute-done | bytes 1310752 | tf_op jit(solution)/shard_map/hop2_down/ppermute | solution.py:57
  80.9 2.7 %slice_select_fusion = bf16[1024,512]{1,0:T(8,128)(2,1)} fusion(bf16[1024,640]{1,0:T(8,128)(2,1)} %collective-permute-done.3.refs_6_, bf16[1024,640]{1,0:T(8,128)(2,1)} %collective-permute-done.1.refs_5_, pred[]{:T(512)S(6)} %eq.31), kind=kLoop, calls=%fused_computation.1 | loop fusion | flops 524288 | bytes 3145729 | tf_op jit(solution)/shard_map/jit(_where)/select_n | solution.py:318
  86.0 7.2 %collect.2.sums = f32[1024,128]{1,0:T(8,128)S(1)} custom-call(bf16[4,128,4096]{2,1,0:T(8,128)(2,1)} %all-to-all-done.refs_0_.mine, bf16[4,128,4096]{2,1,0:T(8,128)(2,1)} %collective-permute-done.4.refs_1_.others, bf16[1024,640]{1,0:T(8,128)(2,1)S(1)} %pad_maximum_fusion.refs_2_, bf16[1024,640]{1,0:T(8,128)(2,1)} %collective-permute-done.refs_3_, ...), custom_call_target="tpu_custom_call" | custom-call | flops 1 | bytes 1 | tf_op jit(solution)/shard_map/collect/pallas_call | solution.py:166
  93.3 2.9 %finish.2 = (f32[1,256,128]{2,1,0:T(8,128)S(1)}, f32[1,256,128]{2,1,0:T(8,128)}, f32[1,256,128]{2,1,0:T(8,128)}, f32[1,256,128]{2,1,0:T(8,128)}) custom-call(bf16[4,128,4096]{2,1,0:T(8,128)(2,1)} %all-to-all-done.refs_0_.mine, bf16[4,128,4096]{2,1,0:T(8,128)(2,1)} %collective-permute-done.4.refs_1_.others, ...), custom_call_target="tpu_custom_call" | custom-call | flops 1 | bytes 1 | tf_op jit(solution)/shard_map/finish/pallas_call | solution.py:197
  96.8 2.3 %collective-permute-start.8 = (f32[256,128]{1,0:T(8,128)}, f32[256,128]{1,0:T(8,128)}, u32[]{:S(2)}, u32[]{:S(2)}) collective-permute-start(f32[256,128]{1,0:T(8,128)} %bitcast.9), channel_id=1, source_target_pairs={{0,18},{2,16},{16,2},{18,0},{1,19},{3,17},{17,3},{19,1},{4,22},{6,... | collective-permute-start | bytes 393224 | tf_op jit(solution)/shard_map/ppermute | solution.py:44
  100.3 9.4 %collect.3.sums = f32[1024,512]{1,0:T(8,128)S(1)} custom-call(bf16[4,128,4096]{2,1,0:T(8,128)(2,1)} %all-to-all-done.refs_0_.mine, bf16[4,128,4096]{2,1,0:T(8,128)(2,1)} %collective-permute-done.4.refs_1_.others, bf16[1024,640]{1,0:T(8,128)(2,1)S(1)} %pad_maximum_fusion.refs_2_, bf16[1024,640]{1,0:T(8,128)(2,1)} %collective-permute-done.refs_3_, ...), custom_call_target="tpu_custom_call" | custom-call | flops 1 | bytes 1 | tf_op jit(solution)/shard_map/collect/pallas_call | solution.py:166
  111.1 3.0 %collective-permute-done.9.last = bf16[1024,512]{1,0:T(8,128)(2,1)} collective-permute-done((bf16[1024,512]{1,0:T(8,128)(2,1)}, bf16[1024,512]{1,0:T(8,128)(2,1)}, u32[]{:S(2)}, u32[]{:S(2)}) %collective-permute-start.9) | collective-permute-done | bytes 1048608 | tf_op jit(solution)/shard_map/hop_ends/ppermute | solution.py:67
  115.4 3.1 %finish.3 = (f32[2,256,256]{2,1,0:T(8,128)S(1)}, f32[2,256,256]{2,1,0:T(8,128)S(1)}, f32[2,256,256]{2,1,0:T(8,128)S(1)}, f32[2,256,256]{2,1,0:T(8,128)S(1)}) custom-call(bf16[4,128,4096]{2,1,0:T(8,128)(2,1)} %all-to-all-done.refs_0_.mine, bf16[4,128,4096]{2,1,0:T(8,128)(2,1)} %collective-permute-done.4.refs_1_.others, ...), custom_call_target="tpu_custom_call" | custom-call | flops 1 | bytes 1 | tf_op jit(solution)/shard_map/finish/pallas_call | solution.py:197
  120.6 4.7 %collective-permute-start.14 = (bf16[512,128]{1,0:T(8,128)(2,1)S(1)}, bf16[512,128]{1,0:T(8,128)(2,1)S(1)}, u32[]{:S(2)}, u32[]{:S(2)}) collective-permute-start(bf16[512,128]{1,0:T(8,128)(2,1)S(1)} %get-tuple-element.69), channel_id=1, source_target_pairs={{0,8},{4,12},{8,0},{12,4},{1,9},{5,13},{9,1},{13,5},{2,10},{6,14},... | collective-permute-start | bytes 393224 | tf_op jit(solution)/shard_map/ppermute | solution.py:349
  125.3 1.8 %collective-permute-start.15 = (bf16[512,128]{1,0:T(8,128)(2,1)S(1)}, bf16[512,128]{1,0:T(8,128)(2,1)S(1)}, u32[]{:S(2)}, u32[]{:S(2)}) collective-permute-start(bf16[512,128]{1,0:T(8,128)(2,1)S(1)} %get-tuple-element.69), channel_id=1, source_target_pairs={{0,12},{4,0},{8,4},{12,8},{1,13},{5,1},{9,5},{13,9},{2,14},{6,2},{... | collective-permute-start | bytes 393224 | tf_op jit(solution)/shard_map/ppermute | solution.py:349
  127.1 1.5 collective-permute-start.11
  129.1 3.8 %collective-permute-done.14 = bf16[512,128]{1,0:T(8,128)(2,1)S(1)} collective-permute-done((bf16[512,128]{1,0:T(8,128)(2,1)S(1)}, bf16[512,128]{1,0:T(8,128)(2,1)S(1)}, u32[]{:S(2)}, u32[]{:S(2)}) %collective-permute-start.14) | collective-permute-done | bytes 131104 | tf_op jit(solution)/shard_map/ppermute | solution.py:349
  135.4 4.2 %collective-permute-done.11 = f32[2,256,256]{2,1,0:T(8,128)S(1)} collective-permute-done((f32[2,256,256]{2,1,0:T(8,128)S(1)}, f32[2,256,256]{2,1,0:T(8,128)S(1)}, u32[]{:S(2)}, u32[]{:S(2)}) %collective-permute-start.11) | collective-permute-done | bytes 524320 | tf_op jit(solution)/shard_map/ppermute | solution.py:44
  140.5 1.4 collective-permute-start.12
  142.1 2.1 %collective-permute-done.18.refs_1_ = f32[256,256]{1,0:T(8,128)} collective-permute-done((f32[256,256]{1,0:T(8,128)}, f32[256,256]{1,0:T(8,128)}, u32[]{:S(2)}, u32[]{:S(2)}) %collective-permute-start.18) | collective-permute-done | bytes 262176 | tf_op jit(solution)/shard_map/ppermute | solution.py:44
  145.2 3.5 %attend.3 = (bf16[128,256]{1,0:T(8,128)(2,1)S(1)}, bf16[128,256]{1,0:T(8,128)(2,1)S(1)}) custom-call(s32[9]{0:T(128)S(1)} %concatenate.35.place, f32[256,256]{1,0:T(8,128)S(1)} %copy-done.6, f32[256,256]{1,0:T(8,128)} %collective-permute-done.18.refs_1_, f32[256,128]{1,0:T(8,128)S(1)} %get-tuple-element.42.refs_2_, f32[256,128]{1,0:T(8,128)S(1)} %copy-done.4, ...), custom_call_target="tpu_custom_call" | custom-call | flops 1 | bytes 1 | tf_op jit(solution)/shard_map/attend/pallas_call | solution.py:250
  148.8 3.6 %attend.2 = (bf16[128,256]{1,0:T(8,128)(2,1)S(1)}, bf16[128,256]{1,0:T(8,128)(2,1)S(1)}) custom-call(s32[9]{0:T(128)S(1)} %concatenate.35.place, f32[256,256]{1,0:T(8,128)S(1)} %copy-done.5, f32[256,256]{1,0:T(8,128)} %collective-permute-done.12.refs_1_, f32[256,128]{1,0:T(8,128)S(1)} %get-tuple-element.42.refs_2_, f32[256,128]{1,0:T(8,128)S(1)} %copy-done.4, ...), custom_call_target="tpu_custom_call" | custom-call | flops 1 | bytes 1 | tf_op jit(solution)/shard_map/attend/pallas_call | solution.py:250
  (93 shorter events, 26.4 us)
Async XLA Ops:
  0.0 12.5 %copy-start = (bf16[2048,512]{1,0:T(8,128)(2,1)S(1)}, bf16[2048,512]{1,0:T(8,128)(2,1)}, u32[]{:S(2)}) copy-start(bf16[2048,512]{1,0:T(8,128)(2,1)} %param.9) | copy-start | bytes 6291460
  7.2 71.3 %all-to-all-start = ((bf16[4,128,4096]{2,1,0:T(8,128)(2,1)}), bf16[4,128,4096]{2,1,0:T(8,128)(2,1)}, u32[]{:S(2)}, u32[]{:S(2)}) async-start(bf16[4,128,4096]{2,1,0:T(8,128)(2,1)} %copy-done.1), calls=%async_computation | async-start | bytes 8388608 | tf_op jit(solution)/shard_map/all_to_all | solution.py:302
  12.7 38.2 %copy-start.12 = (s32[16]{0:T(128)S(1)}, s32[16]{0:T(128)}, u32[]{:S(2)}) copy-start(s32[16]{0:T(128)} %param.12) | copy-start | bytes 196
  12.8 33.5 %collective-permute-start = (bf16[1024,640]{1,0:T(8,128)(2,1)S(1)}, bf16[1024,640]{1,0:T(8,128)(2,1)}, u32[]{:S(2)}, u32[]{:S(2)}) collective-permute-start(bf16[1024,640]{1,0:T(8,128)(2,1)S(1)} %pad_maximum_fusion.refs_2_), channel_id=1, source_target_pairs={{4,0},{8,4},{12,8},{5,1},{9,5},{13,9},{6,2},{10,6},{14,10},{7,3},{... | collective-permute-start | bytes 3932168 | tf_op jit(solution)/shard_map/hop1_down/ppermute | solution.py:57
  14.1 33.5 %collective-permute-start.2 = (bf16[1024,640]{1,0:T(8,128)(2,1)S(1)}, bf16[1024,640]{1,0:T(8,128)(2,1)}, u32[]{:S(2)}, u32[]{:S(2)}) collective-permute-start(bf16[1024,640]{1,0:T(8,128)(2,1)S(1)} %pad_maximum_fusion.refs_2_), channel_id=1, source_target_pairs={{0,4},{4,8},{8,12},{1,5},{5,9},{9,13},{2,6},{6,10},{10,14},{3,7},{... | collective-permute-start | bytes 3932168 | tf_op jit(solution)/shard_map/hop1_up/ppermute | solution.py:62
  46.3 32.2 %collective-permute-start.1 = (bf16[1024,640]{1,0:T(8,128)(2,1)}, bf16[1024,640]{1,0:T(8,128)(2,1)}, u32[]{:S(2)}, u32[]{:S(2)}) collective-permute-start(bf16[1024,640]{1,0:T(8,128)(2,1)} %collective-permute-done.refs_3_), channel_id=1, source_target_pairs={{4,0},{8,4},{5,1},{9,5},{6,2},{10,6},{7,3},{11,7},{20,16},{24,20},... | collective-permute-start | bytes 3932168 | tf_op jit(solution)/shard_map/hop2_down/ppermute | solution.py:57
  47.6 30.9 %collective-permute-start.3 = (bf16[1024,640]{1,0:T(8,128)(2,1)}, bf16[1024,640]{1,0:T(8,128)(2,1)}, u32[]{:S(2)}, u32[]{:S(2)}) collective-permute-start(bf16[1024,640]{1,0:T(8,128)(2,1)} %collective-permute-done.2.refs_4_), channel_id=1, source_target_pairs={{4,8},{8,12},{5,9},{9,13},{6,10},{10,14},{7,11},{11,15},{20,24},{2... | collective-permute-start | bytes 3932168 | tf_op jit(solution)/shard_map/hop2_up/ppermute | solution.py:62
  78.5 7.5 %collective-permute-start.4 = (bf16[4,128,4096]{2,1,0:T(8,128)(2,1)}, bf16[4,128,4096]{2,1,0:T(8,128)(2,1)}, u32[]{:S(2)}, u32[]{:S(2)}) collective-permute-start(bf16[4,128,4096]{2,1,0:T(8,128)(2,1)} %all-to-all-done.refs_0_.mine), channel_id=1, source_target_pairs={{0,1},{1,0},{2,3},{3,2},{4,5},{5,4},{6,7},{7,6},{8,9},{9,8},{10,11... | collective-permute-start | bytes 12582920 | tf_op jit(solution)/shard_map/ppermute | solution.py:48
  79.6 13.7 %collective-permute-start.5 = (bf16[1024,128]{1,0:T(8,128)(2,1)S(1)}, bf16[1024,128]{1,0:T(8,128)(2,1)S(1)}, u32[]{:S(2)}, u32[]{:S(2)}) collective-permute-start(bf16[1024,128]{1,0:T(8,128)(2,1)S(1)} %slice_select_fusion.1), channel_id=1, source_target_pairs={{4,0},{8,12},{5,1},{9,13},{6,2},{10,14},{7,3},{11,15},{20,16},{24,... | collective-permute-start | bytes 786440 | tf_op jit(solution)/shard_map/hop_ends/ppermute | solution.py:67
  83.6 30.5 %collective-permute-start.9 = (bf16[1024,512]{1,0:T(8,128)(2,1)}, bf16[1024,512]{1,0:T(8,128)(2,1)}, u32[]{:S(2)}, u32[]{:S(2)}) collective-permute-start(bf16[1024,512]{1,0:T(8,128)(2,1)} %slice_select_fusion), channel_id=1, source_target_pairs={{4,0},{8,12},{5,1},{9,13},{6,2},{10,14},{7,3},{11,15},{20,16},{24,... | collective-permute-start | bytes 3145736 | tf_op jit(solution)/shard_map/hop_ends/ppermute | solution.py:67
  96.8 12.9 %collective-permute-start.8 = (f32[256,128]{1,0:T(8,128)}, f32[256,128]{1,0:T(8,128)}, u32[]{:S(2)}, u32[]{:S(2)}) collective-permute-start(f32[256,128]{1,0:T(8,128)} %bitcast.9), channel_id=1, source_target_pairs={{0,18},{2,16},{16,2},{18,0},{1,19},{3,17},{17,3},{19,1},{4,22},{6,... | collective-permute-start | bytes 393224 | tf_op jit(solution)/shard_map/ppermute | solution.py:44
  99.1 10.7 %collective-permute-start.7 = (f32[256,128]{1,0:T(8,128)}, f32[256,128]{1,0:T(8,128)}, u32[]{:S(2)}, u32[]{:S(2)}) collective-permute-start(f32[256,128]{1,0:T(8,128)} %bitcast.8), channel_id=1, source_target_pairs={{0,16},{2,18},{16,0},{18,2},{1,17},{3,19},{17,1},{19,3},{4,20},{6,... | collective-permute-start | bytes 393224 | tf_op jit(solution)/shard_map/ppermute | solution.py:44
  99.7 10.1 %collective-permute-start.6 = (f32[256,128]{1,0:T(8,128)}, f32[256,128]{1,0:T(8,128)}, u32[]{:S(2)}, u32[]{:S(2)}) collective-permute-start(f32[256,128]{1,0:T(8,128)} %bitcast.7), channel_id=1, source_target_pairs={{0,2},{2,0},{16,18},{18,16},{1,3},{3,1},{17,19},{19,17},{4,6},{6,4... | collective-permute-start | bytes 393224 | tf_op jit(solution)/shard_map/ppermute | solution.py:44
  114.1 4.5 %collective-permute-start.10 = (bf16[256,128]{1,0:T(8,128)(2,1)S(1)}, bf16[256,128]{1,0:T(8,128)(2,1)S(1)}, u32[]{:S(2)}, u32[]{:S(2)}) collective-permute-start(bf16[256,128]{1,0:T(8,128)(2,1)S(1)} %fusion.2), channel_id=1, source_target_pairs={{0,2},{2,0},{1,3},{3,1},{4,6},{6,4},{5,7},{7,5},{8,10},{10,8},{9,1... | collective-permute-start | bytes 196616 | tf_op jit(solution)/shard_map/ppermute | solution.py:332
  118.6 14.5 %collective-permute-start.17 = (f32[2,256,256]{2,1,0:T(8,128)S(1)}, f32[2,256,256]{2,1,0:T(8,128)S(1)}, u32[]{:S(2)}, u32[]{:S(2)}) collective-permute-start(f32[2,256,256]{2,1,0:T(8,128)S(1)} %get-tuple-element.57), channel_id=1, source_target_pairs={{0,2},{2,0},{16,18},{18,16},{1,3},{3,1},{17,19},{19,17},{4,6},{6,4... | collective-permute-start | bytes 1572872 | tf_op jit(solution)/shard_map/ppermute | solution.py:44
  119.7 9.3 %collective-permute-start.13 = (bf16[512,128]{1,0:T(8,128)(2,1)S(1)}, bf16[512,128]{1,0:T(8,128)(2,1)S(1)}, u32[]{:S(2)}, u32[]{:S(2)}) collective-permute-start(bf16[512,128]{1,0:T(8,128)(2,1)S(1)} %get-tuple-element.69), channel_id=1, source_target_pairs={{0,4},{4,8},{8,12},{12,0},{1,5},{5,9},{9,13},{13,1},{2,6},{6,10},{... | collective-permute-start | bytes 393224 | tf_op jit(solution)/shard_map/ppermute | solution.py:349
  120.6 12.3 %collective-permute-start.14 = (bf16[512,128]{1,0:T(8,128)(2,1)S(1)}, bf16[512,128]{1,0:T(8,128)(2,1)S(1)}, u32[]{:S(2)}, u32[]{:S(2)}) collective-permute-start(bf16[512,128]{1,0:T(8,128)(2,1)S(1)} %get-tuple-element.69), channel_id=1, source_target_pairs={{0,8},{4,12},{8,0},{12,4},{1,9},{5,13},{9,1},{13,5},{2,10},{6,14},... | collective-permute-start | bytes 393224 | tf_op jit(solution)/shard_map/ppermute | solution.py:349
  125.3 7.7 %collective-permute-start.15 = (bf16[512,128]{1,0:T(8,128)(2,1)S(1)}, bf16[512,128]{1,0:T(8,128)(2,1)S(1)}, u32[]{:S(2)}, u32[]{:S(2)}) collective-permute-start(bf16[512,128]{1,0:T(8,128)(2,1)S(1)} %get-tuple-element.69), channel_id=1, source_target_pairs={{0,12},{4,0},{8,4},{12,8},{1,13},{5,1},{9,5},{13,9},{2,14},{6,2},{... | collective-permute-start | bytes 393224 | tf_op jit(solution)/shard_map/ppermute | solution.py:349
  127.1 12.5 %collective-permute-start.11 = (f32[2,256,256]{2,1,0:T(8,128)S(1)}, f32[2,256,256]{2,1,0:T(8,128)S(1)}, u32[]{:S(2)}, u32[]{:S(2)}) collective-permute-start(f32[2,256,256]{2,1,0:T(8,128)S(1)} %get-tuple-element.51), channel_id=1, source_target_pairs={{0,16},{2,18},{16,0},{18,2},{1,17},{3,19},{17,1},{19,3},{4,20},{6,... | collective-permute-start | bytes 1572872 | tf_op jit(solution)/shard_map/ppermute | solution.py:44
  133.0 9.1 %collective-permute-start.16 = (bf16[2048,128]{1,0:T(8,128)(2,1)S(1)}, bf16[2048,128]{1,0:T(8,128)(2,1)S(1)}, u32[]{:S(2)}, u32[]{:S(2)}) collective-permute-start(bf16[2048,128]{1,0:T(8,128)(2,1)S(1)} %constant_dynamic-update-slice_fusion.2.refs_6_), channel_id=1, source_target_pairs={{0,1},{1,0},{2,3},{3,2},{4,5},{5,4},{6,7},{7,6},{8,9},{9,8},{10,11... | collective-permute-start | bytes 1572872 | tf_op jit(solution)/shard_map/ppermute | solution.py:48
  134.0 10.2 %collective-permute-start.18 = (f32[256,256]{1,0:T(8,128)}, f32[256,256]{1,0:T(8,128)}, u32[]{:S(2)}, u32[]{:S(2)}) collective-permute-start(f32[256,256]{1,0:T(8,128)} %get-tuple-element.65), channel_id=1, source_target_pairs={{0,16},{2,18},{16,0},{18,2},{1,17},{3,19},{17,1},{19,3},{4,20},{6,... | collective-permute-start | bytes 786440 | tf_op jit(solution)/shard_map/ppermute | solution.py:44
  140.5 8.3 %collective-permute-start.12 = (f32[256,256]{1,0:T(8,128)}, f32[256,256]{1,0:T(8,128)}, u32[]{:S(2)}, u32[]{:S(2)}) collective-permute-start(f32[256,256]{1,0:T(8,128)} %get-tuple-element.63), channel_id=1, source_target_pairs={{0,2},{2,0},{16,18},{18,16},{1,3},{3,1},{17,19},{19,17},{4,6},{6,4... | collective-permute-start | bytes 786440 | tf_op jit(solution)/shard_map/ppermute | solution.py:44
  148.7 4.2 %collective-permute-start.20 = (bf16[128,256]{1,0:T(8,128)(2,1)S(1)}, bf16[128,256]{1,0:T(8,128)(2,1)S(1)}, u32[]{:S(2)}, u32[]{:S(2)}) collective-permute-start(bf16[128,256]{1,0:T(8,128)(2,1)S(1)} %get-tuple-element.60), channel_id=1, source_target_pairs={{0,1},{1,0},{2,3},{3,2},{4,5},{5,4},{6,7},{7,6},{8,9},{9,8},{10,11... | collective-permute-start | bytes 196616 | tf_op jit(solution)/shard_map/ppermute | solution.py:48
  152.4 1.4 collective-permute-start.19
  (11 other events, 64.3 us)

commit v5 on v4

--- a/solution.py
+++ b/solution.py
@@ -87,8 +87,8 @@
     )
 
 
-def norm_kernel(zs, ys, groups, width, tokens, gain, out):
-    z = lax.axis_index("z")
+def norm_kernel(zs, ys, groups, width, tokens, gain, near, *far):
+    x, z, y = (lax.axis_index(name) for name in ("groups", "z", "y"))
     rows, columns = tokens.shape
     step = min(columns, 1024)
     squares = jnp.zeros((rows, step), jnp.float32)
@@ -96,21 +96,25 @@
         part = tokens[:, at : at + step].astype(jnp.float32)
         squares += part * part
     factor = lax.rsqrt(jnp.sum(squares, axis=1, keepdims=True) / columns + 1e-05)
+    half = zs // 2
     for s in range(zs):
-        into = slice(s * width, (s + 1) * width)
+        into = slice(s % half * width, (s % half + 1) * width)
         for peer in range(groups * ys):
-            x, y = peer // ys, peer % ys
-            blk = nearest(z, s, zs) * ys + y
-            start = pl.multiple_of((blk * groups + x) * width, width)
+            to_x, to_y = peer // ys, peer % ys
+            if s >= half:
+                to_x, to_y = lax.rem(x + to_x, groups), lax.rem(y + to_y, ys)
+            blk = nearest(z, s, zs) * ys + to_y
+            start = pl.multiple_of((blk * groups + to_x) * width, width)
             part = tokens[:, pl.ds(start, width)].astype(jnp.float32)
             scale = gain[:, pl.ds(start, width)]
-            out[peer, :, into] = (part * factor * scale).astype(jnp.bfloat16)
+            out = near.at[peer] if s < half else far[peer]
+            out[:, into] = (part * factor * scale).astype(jnp.bfloat16)
 
 
 def norm_pieces(tokens, gain, zs, ys, groups, width):
     count, columns = tokens.shape
     rows = min(count, 32)
-    shape = (groups * ys, count, zs * width)
+    shape = (groups * ys, count, zs // 2 * width)
     return pl.pallas_call(
         functools.partial(norm_kernel, zs, ys, groups, width),
         grid=(count // rows,),
@@ -118,8 +122,10 @@
             pl.BlockSpec((rows, columns), lambda i: (i, 0)),
             pl.BlockSpec((1, columns), lambda i: (0, 0)),
         ],
-        out_specs=pl.BlockSpec((shape[0], rows, shape[2]), lambda i: (0, i, 0)),
-        out_shape=jax.ShapeDtypeStruct(shape, jnp.bfloat16),
+        out_specs=[pl.BlockSpec((shape[0], rows, shape[2]), lambda i: (0, i, 0))]
+        + [pl.BlockSpec((rows, shape[2]), lambda i: (i, 0))] * shape[0],
+        out_shape=[jax.ShapeDtypeStruct(shape, jnp.bfloat16)]
+        + [jax.ShapeDtypeStruct(shape[1:], jnp.bfloat16)] * shape[0],
         compiler_params=pltpu.CompilerParams(vmem_limit_bytes=24 * MIB),
         cost_estimate=COST,
         name="norm",
@@ -135,17 +141,20 @@
 
 
 def collect_kernel(zs, ys, groups, names, cuts, *refs):
-    mine, others = refs[:2]
-    weights, outs = dict(zip(names, refs[2:])), refs[2 + len(names) :]
+    mine, others = refs[:2], refs[2:4]
+    weights, outs = dict(zip(names, refs[4:])), refs[4 + len(names) :]
     z = lax.axis_index("z")
     base, size = cuts[0][0], sum(size for _, size in cuts)
-    peers, _, columns = mine.shape
-    width = columns // zs
-    index = peer_order(ys, groups, peers)
+    peers, _, columns = mine[0].shape
+    half = zs // 2
+    width = columns // half
+    orders = peer_order(ys, groups, peers), range(peers)
     total = None
     for place in range(zs):
-        into = slice(place * width, (place + 1) * width)
-        rows = jnp.concatenate([ref[i, :, into] for ref in (mine, others) for i in index], axis=0)
+        part, at = place // half, place % half * width
+        rows = jnp.concatenate(
+            [ref[part][i, :, at : at + width] for ref in (mine, others) for i in orders[part]], axis=0
+        )
         weight = None
         for who, way, hops in ways(place, zs):
             if (way, hops) in weights:
@@ -161,8 +170,8 @@
 
 
 def collect(mine, others, pieces, cuts, zs, ys, groups):
-    rows = 2 * mine.shape[0] * mine.shape[1]
-    operands = [mine, others, *pieces.values()]
+    rows = 2 * mine[0].shape[0] * mine[0].shape[1]
+    operands = [*mine, *others, *pieces.values()]
     return pl.pallas_call(
         functools.partial(collect_kernel, zs, ys, groups, list(pieces), cuts),
         in_specs=[pl.BlockSpec(memory_space=pltpu.VMEM)] * len(operands),
@@ -174,11 +183,12 @@
     )(*operands)
 
 
-def finish_kernel(ys, groups, layout, mine, others, last, sums, *outs):
+def finish_kernel(layout, mine, others, last, sums, *outs):
     side = lax.axis_index("dp")
     peers, count = mine.shape[:2]
-    index = peer_order(ys, groups, peers)
-    rows = jnp.concatenate([ref[i] for ref in (mine, others) for i in index], axis=0)
+    rows = jnp.concatenate(
+        [ref[...].reshape(peers * count, ref.shape[2]) for ref in (mine, others)], axis=0
+    )
     total = sums[...] + jnp.dot(rows, last[...], preferred_element_type=jnp.float32)
     here = pl.multiple_of(side * count, count)
     there = pl.multiple_of((1 - side) * count, count)
@@ -189,13 +199,13 @@
             out[at, pl.ds(there, count), :] = part[(peers + peer) * count : (peers + peer + 1) * count]
 
 
-def finish(mine, others, last, sums, layout, ys, groups):
+def finish(mine, others, last, sums, layout):
     peers, count, columns = mine.shape
     width = last.shape[0]
     tokens = pl.BlockSpec((peers, count, width), lambda i: (0, 0, columns // width - 1))
     shapes = [(len(which), 2 * count, size) for _, size, which in layout]
     return pl.pallas_call(
-        functools.partial(finish_kernel, ys, groups, layout),
+        functools.partial(finish_kernel, layout),
         grid=(1,),
         in_specs=[
             tokens,
@@ -299,16 +309,23 @@
     which_key = jnp.sum((ends[:, None] <= key_place[None, :]).astype(jnp.int32), axis=0)[None, :]
     tables = (cosine, sine, query_info, which_key, place)
 
-    mine = lax.all_to_all(normed, ("groups", "y"), 0, 0, tiled=True)
+    near, *far = normed
+    near = lax.all_to_all(near, ("groups", "y"), 0, 0, tiled=True)
     pieces = {("own", 0): own}
-    came = [after(own, normed), after(own, normed)]
+    came = [own, own]
     for step in range(1, zs - 1):
         came = [hop_down(came[0], step, zs), hop_up(came[1], step, zs)]
         pieces["down", step], pieces["up", step] = came
-    done = (mine, *came, *tables)
-    others = swap_core(after(mine, *done))
+    far = lax.optimization_barrier((near, *far))[1:]
+    far = [
+        shift_square(part, dx, dy, groups, ys) if dx or dy else part
+        for (dx, dy), part in zip(peers, far)
+    ]
+    mine = [near, jnp.stack(far)]
+    done = (*mine, *came, *tables)
+    others = [swap_core(after(half, *done)) for half in mine]
     came = [after(came[0], *done), after(came[1], *done)]
-    cosine, sine, query_info, which_key, place = lax.optimization_barrier((*tables, mine))[:5]
+    cosine, sine, query_info, which_key, place = lax.optimization_barrier((*tables, near))[:5]
     cuts, first = [(0, HEAD)], HEAD
     for heads in CHUNK_HEADS:
         cuts.append((first, heads * HEAD))
@@ -324,7 +341,7 @@
         return shift_square(part, -dx, -dy, groups, ys) if dx or dy else part
 
     layout = [(0, HEAD, [at]) for at in range(len(peers))]
-    kv_parts = finish(mine, others, last[0], sums[0], layout, ys, groups)
+    kv_parts = finish(mine[1], others[1], last[0], sums[0], layout)
     proj = sum(to_owner(part[0], *peer) for part, peer in zip(kv_parts, peers))
     turned = proj * cosine + jnp.roll(proj, HEAD // 2, axis=1) * sine
     kept_kv = jnp.where(side == 0, turned, proj).astype(jnp.bfloat16)
@@ -335,7 +352,7 @@
     rest = CHUNK_HEADS[1] * HEAD
     layout = [(0, split, [dx * ys + dy for dy in range(ys)]) for dx in range(groups)]
     layout += [(split, rest, [dx * ys + dy for dx in range(groups)]) for dy in range(ys)]
-    parts = finish(mine, others, last[1], sums[1], layout, ys, groups)
+    parts = finish(mine[1], others[1], last[1], sums[1], layout)
     beside, *parts = lax.optimization_barrier((beside, *parts))
     by_group = sum(to_owner(part, dx, 0) for dx, part in enumerate(parts[:groups]))
     by_y = sum(to_owner(part, 0, dy) for dy, part in enumerate(parts[groups:]))

time: 155 us -> 148 us (0.955)
  waiting for transfers between devices: 66.7 us -> 52.9 us
  starting transfers between devices: 36.8 us -> 38.9 us
  local copies, waits for them, and re-layouts: 10 us -> 12 us
  other arithmetic: 8.74 us -> 10.5 us
    ppermute x2, waiting for transfers between devices: 50.9 us -> 14.2 us  [hop_down(): lax.ppermute(block, 'z', [(i, i - 1) for i in range(1, zs - step + 1)])]
    ppermute x7 -> x10, waiting for transfers between devices: 6.27 us -> 26.2 us  [shift_square(): return lax.ppermute(block, ('groups', 'y'), route)]
    all_to_all x1, waiting for transfers between devices: 0.01 us -> 4.89 us  [on_device(): near = lax.all_to_all(near, ('groups', 'y'), 0, 0, tiled=True)]
    ppermute x7 -> x10, starting transfers between devices: 8.89 us -> 13.4 us  [shift_square(): return lax.ppermute(block, ('groups', 'y'), route)]
    another operation x2 -> x3, other arithmetic: 0.16 us -> 2.79 us  [the longest x1 2.64 us: on_device(): mine = [near, jnp.stack(far)]]
    ppermute x3, starting transfers between devices: 7.34 us -> 4.75 us  [on_device(): lax.ppermute(both, 'z', [(i, (i + n) % zs) for i in range(zs)])]
    unnamed x29 -> x39, local copies, waits for them, and re-layouts: 5.9 us -> 7.82 us
    ppermute x2, waiting for transfers between devices: 2.99 us -> 1.35 us  [hop_ends(): return lax.ppermute(block, 'z', [(1, 0), (zs - 2, zs - 1)])]
  transfers between devices with their start and end apart: 22 -> 26, of which waited for: 10 -> 13; matrix products, arithmetic and copies ran while one was open for 7% -> 9% of each run, Pallas kernels for 19% -> 22%
where the time goes in v5:
time: 148 us; the launch traced here: 146 us
  waiting for transfers between devices  52.9 us (36%)
  starting transfers between devices  38.9 us (26%)
  Pallas kernels  31.8 us (21%)
  local copies, waits for them, and re-layouts  12 us (8%)
  other arithmetic  10.5 us (7%)
    ppermute x10, waiting for transfers between devices, shift_square(): return lax.ppermute(block, ('groups', 'y'), route)  26.2 us
    pallas_call x2, Pallas kernels, collect(): pl.pallas_call(functools.partial(collect_kernel, zs, ys, groups, list(pie...  16.7 us
    ppermute x2, waiting for transfers between devices, hop_down(): lax.ppermute(block, 'z', [(i, i - 1) for i in range(1, zs - step + 1)])  14.2 us
    ppermute x10, starting transfers between devices, shift_square(): return lax.ppermute(block, ('groups', 'y'), route)  13.4 us
    ppermute x2, starting transfers between devices, hop_up(): lax.ppermute(block, 'z', [(i, i + 1) for i in range(step - 1, zs - 1)])  8.4 us
    unnamed x39, local copies, waits for them, and re-layouts  7.82 us
    pallas_call x2, Pallas kernels, attend(): pl.pallas_call(functools.partial(attend_kernel, len(partials), window), g...  7.09 us
    pallas_call x2, Pallas kernels, finish(): pl.pallas_call(functools.partial(finish_kernel, layout), grid=(1,), in_sp...  6.02 us
  transfers between devices with their start and end apart: 26, of which 13 were waited for; matrix products, arithmetic and copies ran while one was open for 9% of the time, Pallas kernels for 22%

profile of v5, /device:TPU:0, one launch (start us, length us, event | category | flops | bytes accessed | tf_op | source)
XLA Modules:
  0.0 146.4 jit_solution(2767129111292760543)
XLA Ops:
  0.0 1.6 %copy-done = bf16[2048,512]{1,0:T(8,128)(2,1)S(1)} copy-done((bf16[2048,512]{1,0:T(8,128)(2,1)S(1)}, bf16[2048,512]{1,0:T(8,128)(2,1)}, u32[]{:S(2)}) %copy-start) | copy-done | bytes 2097176
  3.4 6.6 %collective-permute-start.5 = (bf16[1024,640]{1,0:T(8,128)(2,1)S(1)}, bf16[1024,640]{1,0:T(8,128)(2,1)}, u32[]{:S(2)}, u32[]{:S(2)}) collective-permute-start(bf16[1024,640]{1,0:T(8,128)(2,1)S(1)} %pad_maximum_fusion.1.refs_4_), channel_id=1, source_target_pairs={{0,4},{4,8},{8,12},{1,5},{5,9},{9,13},{2,6},{6,10},{10,14},{3,7},{... | collective-permute-start | bytes 3932168 | tf_op jit(solution)/shard_map/hop1_up/ppermute | solution.py:62
  10.1 2.0 %norm.1 = (bf16[4,128,2048]{2,1,0:T(8,128)(2,1)S(1)}, bf16[128,2048]{1,0:T(8,128)(2,1)S(1)}, bf16[128,2048]{1,0:T(8,128)(2,1)S(1)}, bf16[128,2048]{1,0:T(8,128)(2,1)S(1)}, bf16[128,2048]{1,0:T(8,128)(2,1)S(1)}) custom-call(bf16[128,16384]{1,0:T(8,128)(2,1)S(1)} %copy-done.1, f32[1,16384]{1,0:T(1,128)S(1)} %bitcast.28), custom_call_target="tpu_custom_call" | custom-call | flops 1 | bytes 1 | tf_op jit(solution)/shard_map/norm/pallas_call | solution.py:118
  16.6 4.6 %all-to-all-start = ((bf16[4,128,2048]{2,1,0:T(8,128)(2,1)}), bf16[4,128,2048]{2,1,0:T(8,128)(2,1)}, u32[]{:S(2)}, u32[]{:S(2)}) async-start(bf16[4,128,2048]{2,1,0:T(8,128)(2,1)} %copy-done.4), calls=%async_computation | async-start | bytes 4194304 | tf_op jit(solution)/shard_map/all_to_all | solution.py:313
  21.7 14.2 %collective-permute-done.3.refs_5_ = bf16[1024,640]{1,0:T(8,128)(2,1)} collective-permute-done((bf16[1024,640]{1,0:T(8,128)(2,1)S(1)}, bf16[1024,640]{1,0:T(8,128)(2,1)}, u32[]{:S(2)}, u32[]{:S(2)}) %collective-permute-start.3) | collective-permute-done | bytes 1310752 | tf_op jit(solution)/shard_map/hop1_down/ppermute | solution.py:57
  37.2 1.8 %collective-permute-start.6 = (bf16[1024,640]{1,0:T(8,128)(2,1)}, bf16[1024,640]{1,0:T(8,128)(2,1)}, u32[]{:S(2)}, u32[]{:S(2)}) collective-permute-start(bf16[1024,640]{1,0:T(8,128)(2,1)} %collective-permute-done.5.refs_6_), channel_id=1, source_target_pairs={{4,8},{8,12},{5,9},{9,13},{6,10},{10,14},{7,11},{11,15},{20,24},{2... | collective-permute-start | bytes 3932168 | tf_op jit(solution)/shard_map/hop2_up/ppermute | solution.py:62
  41.3 4.9 %all-to-all-done.refs_0_ = bf16[4,128,2048]{2,1,0:T(8,128)(2,1)} async-done(((bf16[4,128,2048]{2,1,0:T(8,128)(2,1)}), bf16[4,128,2048]{2,1,0:T(8,128)(2,1)}, u32[]{:S(2)}, u32[]{:S(2)}) %all-to-all-start) | async-done | bytes 2097184 | tf_op jit(solution)/shard_map/all_to_all | solution.py:313
  51.0 11.2 %collective-permute-done.2 = bf16[128,2048]{1,0:T(8,128)(2,1)S(1)} collective-permute-done((bf16[128,2048]{1,0:T(8,128)(2,1)}, bf16[128,2048]{1,0:T(8,128)(2,1)S(1)}, u32[]{:S(2)}, u32[]{:S(2)}) %collective-permute-start.2) | collective-permute-done | bytes 524320 | tf_op jit(solution)/shard_map/ppermute | solution.py:44
  62.2 9.0 %collective-permute-done.1 = bf16[128,2048]{1,0:T(8,128)(2,1)S(1)} collective-permute-done((bf16[128,2048]{1,0:T(8,128)(2,1)}, bf16[128,2048]{1,0:T(8,128)(2,1)S(1)}, u32[]{:S(2)}, u32[]{:S(2)}) %collective-permute-start.1) | collective-permute-done | bytes 524320 | tf_op jit(solution)/shard_map/ppermute | solution.py:44
  71.3 2.6 %pad_maximum_fusion.refs_1_.mine = bf16[4,128,2048]{2,1,0:T(8,128)(2,1)} fusion(bf16[1,128,2048]{2,1,0:T(8,128)(2,1)S(1)} %bitcast.29, bf16[1,128,2048]{2,1,0:T(8,128)(2,1)S(1)} %bitcast.30, bf16[1,128,2048]{2,1,0:T(8,128)(2,1)S(1)} %bitcast.31, bf16[1,128,2048]{2,1,0:T(8,128)(2,1)} %bitcast.27), kind=kLoop, calls=%fused_computation | loop fusion | flops 3145728 | bytes 4194304 | tf_op jit(solution)/shard_map/stack | solution.py:324
  76.9 2.6 %slice_select_fusion = bf16[1024,512]{1,0:T(8,128)(2,1)} fusion(bf16[1024,640]{1,0:T(8,128)(2,1)} %collective-permute-done.6.refs_8_, bf16[1024,640]{1,0:T(8,128)(2,1)} %collective-permute-done.4.refs_7_, pred[]{:T(512)S(6)} %eq.31), kind=kLoop, calls=%fused_computation.2 | loop fusion | flops 524288 | bytes 3145729 | tf_op jit(solution)/shard_map/jit(_where)/select_n | solution.py:335
  81.5 7.2 %collect.2.sums = f32[1024,128]{1,0:T(8,128)S(1)} custom-call(bf16[4,128,2048]{2,1,0:T(8,128)(2,1)} %all-to-all-done.refs_0_, bf16[4,128,2048]{2,1,0:T(8,128)(2,1)} %pad_maximum_fusion.refs_1_.mine, bf16[4,128,2048]{2,1,0:T(8,128)(2,1)} %collective-permute-done.9.refs_2_, bf16[4,128,2048]{2,1,0:T(8,128)(2,1)} %collective-permute-done.7.refs_3_.others, ...), custom_call_target="tpu_custom_call" | custom-call | flops 1 | bytes 1 | tf_op jit(solution)/shard_map/collect/pallas_call | solution.py:175
  88.7 2.9 %finish.2 = (f32[1,256,128]{2,1,0:T(8,128)S(1)}, f32[1,256,128]{2,1,0:T(8,128)}, f32[1,256,128]{2,1,0:T(8,128)}, f32[1,256,128]{2,1,0:T(8,128)}) custom-call(bf16[4,128,2048]{2,1,0:T(8,128)(2,1)} %pad_maximum_fusion.refs_1_.mine, bf16[4,128,2048]{2,1,0:T(8,128)(2,1)} %collective-permute-done.7.refs_3_.others, ...), custom_call_target="tpu_custom_call" | custom-call | flops 1 | bytes 1 | tf_op jit(solution)/shard_map/finish/pallas_call | solution.py:207
  92.3 2.5 %collective-permute-start.12 = (f32[256,128]{1,0:T(8,128)}, f32[256,128]{1,0:T(8,128)}, u32[]{:S(2)}, u32[]{:S(2)}) collective-permute-start(f32[256,128]{1,0:T(8,128)} %bitcast.13), channel_id=1, source_target_pairs={{0,18},{2,16},{16,2},{18,0},{1,19},{3,17},{17,3},{19,1},{4,22},{6,... | collective-permute-start | bytes 393224 | tf_op jit(solution)/shard_map/ppermute | solution.py:44
  96.2 9.4 %collect.3.sums = f32[1024,512]{1,0:T(8,128)S(1)} custom-call(bf16[4,128,2048]{2,1,0:T(8,128)(2,1)} %all-to-all-done.refs_0_, bf16[4,128,2048]{2,1,0:T(8,128)(2,1)} %pad_maximum_fusion.refs_1_.mine, bf16[4,128,2048]{2,1,0:T(8,128)(2,1)} %collective-permute-done.9.refs_2_, bf16[4,128,2048]{2,1,0:T(8,128)(2,1)} %collective-permute-done.7.refs_3_.others, ...), custom_call_target="tpu_custom_call" | custom-call | flops 1 | bytes 1 | tf_op jit(solution)/shard_map/collect/pallas_call | solution.py:175
  109.6 3.1 %finish.3 = (f32[2,256,256]{2,1,0:T(8,128)S(1)}, f32[2,256,256]{2,1,0:T(8,128)S(1)}, f32[2,256,256]{2,1,0:T(8,128)S(1)}, f32[2,256,256]{2,1,0:T(8,128)S(1)}) custom-call(bf16[4,128,2048]{2,1,0:T(8,128)(2,1)} %pad_maximum_fusion.refs_1_.mine, bf16[4,128,2048]{2,1,0:T(8,128)(2,1)} %collective-permute-done.7.refs_3_.others, ...), custom_call_target="tpu_custom_call" | custom-call | flops 1 | bytes 1 | tf_op jit(solution)/shard_map/finish/pallas_call | solution.py:207
  116.3 2.2 %collective-permute-start.19 = (bf16[512,128]{1,0:T(8,128)(2,1)S(1)}, bf16[512,128]{1,0:T(8,128)(2,1)S(1)}, u32[]{:S(2)}, u32[]{:S(2)}) collective-permute-start(bf16[512,128]{1,0:T(8,128)(2,1)S(1)} %get-tuple-element.87), channel_id=1, source_target_pairs={{0,12},{4,0},{8,4},{12,8},{1,13},{5,1},{9,5},{13,9},{2,14},{6,2},{... | collective-permute-start | bytes 393224 | tf_op jit(solution)/shard_map/ppermute | solution.py:366
  118.6 2.0 %collective-permute-start.15 = (f32[2,256,256]{2,1,0:T(8,128)S(1)}, f32[2,256,256]{2,1,0:T(8,128)S(1)}, u32[]{:S(2)}, u32[]{:S(2)}) collective-permute-start(f32[2,256,256]{2,1,0:T(8,128)S(1)} %get-tuple-element.69), channel_id=1, source_target_pairs={{0,16},{2,18},{16,0},{18,2},{1,17},{3,19},{17,1},{19,3},{4,20},{6,... | collective-permute-start | bytes 1572872 | tf_op jit(solution)/shard_map/ppermute | solution.py:44
  122.2 3.0 %collective-permute-done.18 = bf16[512,128]{1,0:T(8,128)(2,1)S(1)} collective-permute-done((bf16[512,128]{1,0:T(8,128)(2,1)S(1)}, bf16[512,128]{1,0:T(8,128)(2,1)S(1)}, u32[]{:S(2)}, u32[]{:S(2)}) %collective-permute-start.18) | collective-permute-done | bytes 131104 | tf_op jit(solution)/shard_map/ppermute | solution.py:366
  126.4 2.3 %collective-permute-start.22 = (f32[256,256]{1,0:T(8,128)}, f32[256,256]{1,0:T(8,128)}, u32[]{:S(2)}, u32[]{:S(2)}) collective-permute-start(f32[256,256]{1,0:T(8,128)} %get-tuple-element.83), channel_id=1, source_target_pairs={{0,16},{2,18},{16,0},{18,2},{1,17},{3,19},{17,1},{19,3},{4,20},{6,... | collective-permute-start | bytes 786440 | tf_op jit(solution)/shard_map/ppermute | solution.py:44
  128.7 1.6 %collective-permute-done.15 = f32[2,256,256]{2,1,0:T(8,128)S(1)} collective-permute-done((f32[2,256,256]{2,1,0:T(8,128)S(1)}, f32[2,256,256]{2,1,0:T(8,128)S(1)}, u32[]{:S(2)}, u32[]{:S(2)}) %collective-permute-start.15) | collective-permute-done | bytes 524320 | tf_op jit(solution)/shard_map/ppermute | solution.py:44
  132.0 4.1 %collective-permute-done.22.refs_1_ = f32[256,256]{1,0:T(8,128)} collective-permute-done((f32[256,256]{1,0:T(8,128)}, f32[256,256]{1,0:T(8,128)}, u32[]{:S(2)}, u32[]{:S(2)}) %collective-permute-start.22) | collective-permute-done | bytes 262176 | tf_op jit(solution)/shard_map/ppermute | solution.py:44
  137.0 3.5 %attend.3 = (bf16[128,256]{1,0:T(8,128)(2,1)S(1)}, bf16[128,256]{1,0:T(8,128)(2,1)S(1)}) custom-call(s32[9]{0:T(128)S(1)} %concatenate.35.place, f32[256,256]{1,0:T(8,128)S(1)} %copy-done.6, f32[256,256]{1,0:T(8,128)} %collective-permute-done.22.refs_1_, f32[256,128]{1,0:T(8,128)S(1)} %get-tuple-element.60.refs_2_, f32[256,128]{1,0:T(8,128)S(1)} %copy-done.3, ...), custom_call_target="tpu_custom_call" | custom-call | flops 1 | bytes 1 | tf_op jit(solution)/shard_map/attend/pallas_call | solution.py:260
  140.6 3.6 %attend.2 = (bf16[128,256]{1,0:T(8,128)(2,1)S(1)}, bf16[128,256]{1,0:T(8,128)(2,1)S(1)}) custom-call(s32[9]{0:T(128)S(1)} %concatenate.35.place, f32[256,256]{1,0:T(8,128)S(1)} %copy-done.5, f32[256,256]{1,0:T(8,128)} %collective-permute-done.16.refs_1_, f32[256,128]{1,0:T(8,128)S(1)} %get-tuple-element.60.refs_2_, f32[256,128]{1,0:T(8,128)S(1)} %copy-done.3, ...), custom_call_target="tpu_custom_call" | custom-call | flops 1 | bytes 1 | tf_op jit(solution)/shard_map/attend/pallas_call | solution.py:260
  (112 shorter events, 37.4 us)
Async XLA Ops:
  1.9 34.1 %collective-permute-start.3 = (bf16[1024,640]{1,0:T(8,128)(2,1)S(1)}, bf16[1024,640]{1,0:T(8,128)(2,1)}, u32[]{:S(2)}, u32[]{:S(2)}) collective-permute-start(bf16[1024,640]{1,0:T(8,128)(2,1)S(1)} %pad_maximum_fusion.1.refs_4_), channel_id=1, source_target_pairs={{4,0},{8,4},{12,8},{5,1},{9,5},{13,9},{6,2},{10,6},{14,10},{7,3},{... | collective-permute-start | bytes 3932168 | tf_op jit(solution)/shard_map/hop1_down/ppermute | solution.py:57
  3.4 33.8 %collective-permute-start.5 = (bf16[1024,640]{1,0:T(8,128)(2,1)S(1)}, bf16[1024,640]{1,0:T(8,128)(2,1)}, u32[]{:S(2)}, u32[]{:S(2)}) collective-permute-start(bf16[1024,640]{1,0:T(8,128)(2,1)S(1)} %pad_maximum_fusion.1.refs_4_), channel_id=1, source_target_pairs={{0,4},{4,8},{8,12},{1,5},{5,9},{9,13},{2,6},{6,10},{10,14},{3,7},{... | collective-permute-start | bytes 3932168 | tf_op jit(solution)/shard_map/hop1_up/ppermute | solution.py:62
  16.6 29.5 %all-to-all-start = ((bf16[4,128,2048]{2,1,0:T(8,128)(2,1)}), bf16[4,128,2048]{2,1,0:T(8,128)(2,1)}, u32[]{:S(2)}, u32[]{:S(2)}) async-start(bf16[4,128,2048]{2,1,0:T(8,128)(2,1)} %copy-done.4), calls=%async_computation | async-start | bytes 4194304 | tf_op jit(solution)/shard_map/all_to_all | solution.py:313
  35.9 38.0 %collective-permute-start.4 = (bf16[1024,640]{1,0:T(8,128)(2,1)}, bf16[1024,640]{1,0:T(8,128)(2,1)}, u32[]{:S(2)}, u32[]{:S(2)}) collective-permute-start(bf16[1024,640]{1,0:T(8,128)(2,1)} %collective-permute-done.3.refs_5_), channel_id=1, source_target_pairs={{4,0},{8,4},{5,1},{9,5},{6,2},{10,6},{7,3},{11,7},{20,16},{24,20},... | collective-permute-start | bytes 3932168 | tf_op jit(solution)/shard_map/hop2_down/ppermute | solution.py:57
  37.2 36.7 %collective-permute-start.6 = (bf16[1024,640]{1,0:T(8,128)(2,1)}, bf16[1024,640]{1,0:T(8,128)(2,1)}, u32[]{:S(2)}, u32[]{:S(2)}) collective-permute-start(bf16[1024,640]{1,0:T(8,128)(2,1)} %collective-permute-done.5.refs_6_), channel_id=1, source_target_pairs={{4,8},{8,12},{5,9},{9,13},{6,10},{10,14},{7,11},{11,15},{20,24},{2... | collective-permute-start | bytes 3932168 | tf_op jit(solution)/shard_map/hop2_up/ppermute | solution.py:62
  46.1 16.0 %collective-permute-start.2 = (bf16[128,2048]{1,0:T(8,128)(2,1)}, bf16[128,2048]{1,0:T(8,128)(2,1)S(1)}, u32[]{:S(2)}, u32[]{:S(2)}) collective-permute-start(bf16[128,2048]{1,0:T(8,128)(2,1)} %copy-done.12), channel_id=1, source_target_pairs={{0,18},{2,16},{16,2},{18,0},{1,19},{3,17},{17,3},{19,1},{4,22},{6,... | collective-permute-start | bytes 1572872 | tf_op jit(solution)/shard_map/ppermute | solution.py:44
  47.6 23.5 %collective-permute-start.1 = (bf16[128,2048]{1,0:T(8,128)(2,1)}, bf16[128,2048]{1,0:T(8,128)(2,1)S(1)}, u32[]{:S(2)}, u32[]{:S(2)}) collective-permute-start(bf16[128,2048]{1,0:T(8,128)(2,1)} %copy-done.11), channel_id=1, source_target_pairs={{0,16},{2,18},{16,0},{18,2},{1,17},{3,19},{17,1},{19,3},{4,20},{6,... | collective-permute-start | bytes 1572872 | tf_op jit(solution)/shard_map/ppermute | solution.py:44
  49.1 22.3 %collective-permute-start = (bf16[128,2048]{1,0:T(8,128)(2,1)}, bf16[128,2048]{1,0:T(8,128)(2,1)S(1)}, u32[]{:S(2)}, u32[]{:S(2)}) collective-permute-start(bf16[128,2048]{1,0:T(8,128)(2,1)} %copy-done.10), channel_id=1, source_target_pairs={{0,2},{2,0},{16,18},{18,16},{1,3},{3,1},{17,19},{19,17},{4,6},{6,4... | collective-permute-start | bytes 1572872 | tf_op jit(solution)/shard_map/ppermute | solution.py:44
  74.0 6.8 %collective-permute-start.7 = (bf16[4,128,2048]{2,1,0:T(8,128)(2,1)}, bf16[4,128,2048]{2,1,0:T(8,128)(2,1)}, u32[]{:S(2)}, u32[]{:S(2)}) collective-permute-start(bf16[4,128,2048]{2,1,0:T(8,128)(2,1)} %pad_maximum_fusion.refs_1_.mine), channel_id=1, source_target_pairs={{0,1},{1,0},{2,3},{3,2},{4,5},{5,4},{6,7},{7,6},{8,9},{9,8},{10,11... | collective-permute-start | bytes 6291464 | tf_op jit(solution)/shard_map/ppermute | solution.py:48
  74.0 7.5 %collective-permute-start.9 = (bf16[4,128,2048]{2,1,0:T(8,128)(2,1)}, bf16[4,128,2048]{2,1,0:T(8,128)(2,1)}, u32[]{:S(2)}, u32[]{:S(2)}) collective-permute-start(bf16[4,128,2048]{2,1,0:T(8,128)(2,1)} %all-to-all-done.refs_0_), channel_id=1, source_target_pairs={{0,1},{1,0},{2,3},{3,2},{4,5},{5,4},{6,7},{7,6},{8,9},{9,8},{10,11... | collective-permute-start | bytes 6291464 | tf_op jit(solution)/shard_map/ppermute | solution.py:48
  75.6 13.2 %collective-permute-start.8 = (bf16[1024,128]{1,0:T(8,128)(2,1)S(1)}, bf16[1024,128]{1,0:T(8,128)(2,1)S(1)}, u32[]{:S(2)}, u32[]{:S(2)}) collective-permute-start(bf16[1024,128]{1,0:T(8,128)(2,1)S(1)} %slice_select_fusion.1), channel_id=1, source_target_pairs={{4,0},{8,12},{5,1},{9,13},{6,2},{10,14},{7,3},{11,15},{20,16},{24,... | collective-permute-start | bytes 786440 | tf_op jit(solution)/shard_map/hop_ends/ppermute | solution.py:67
  79.5 28.8 %collective-permute-start.13 = (bf16[1024,512]{1,0:T(8,128)(2,1)}, bf16[1024,512]{1,0:T(8,128)(2,1)}, u32[]{:S(2)}, u32[]{:S(2)}) collective-permute-start(bf16[1024,512]{1,0:T(8,128)(2,1)} %slice_select_fusion), channel_id=1, source_target_pairs={{4,0},{8,12},{5,1},{9,13},{6,2},{10,14},{7,3},{11,15},{20,16},{24,... | collective-permute-start | bytes 3145736 | tf_op jit(solution)/shard_map/hop_ends/ppermute | solution.py:67
  92.3 13.3 %collective-permute-start.12 = (f32[256,128]{1,0:T(8,128)}, f32[256,128]{1,0:T(8,128)}, u32[]{:S(2)}, u32[]{:S(2)}) collective-permute-start(f32[256,128]{1,0:T(8,128)} %bitcast.13), channel_id=1, source_target_pairs={{0,18},{2,16},{16,2},{18,0},{1,19},{3,17},{17,3},{19,1},{4,22},{6,... | collective-permute-start | bytes 393224 | tf_op jit(solution)/shard_map/ppermute | solution.py:44
  94.8 10.9 %collective-permute-start.11 = (f32[256,128]{1,0:T(8,128)}, f32[256,128]{1,0:T(8,128)}, u32[]{:S(2)}, u32[]{:S(2)}) collective-permute-start(f32[256,128]{1,0:T(8,128)} %bitcast.12), channel_id=1, source_target_pairs={{0,16},{2,18},{16,0},{18,2},{1,17},{3,19},{17,1},{19,3},{4,20},{6,... | collective-permute-start | bytes 393224 | tf_op jit(solution)/shard_map/ppermute | solution.py:44
  95.0 10.6 %collective-permute-start.10 = (f32[256,128]{1,0:T(8,128)}, f32[256,128]{1,0:T(8,128)}, u32[]{:S(2)}, u32[]{:S(2)}) collective-permute-start(f32[256,128]{1,0:T(8,128)} %bitcast.11), channel_id=1, source_target_pairs={{0,2},{2,0},{16,18},{18,16},{1,3},{3,1},{17,19},{19,17},{4,6},{6,4... | collective-permute-start | bytes 393224 | tf_op jit(solution)/shard_map/ppermute | solution.py:44
  108.3 4.4 %collective-permute-start.14 = (bf16[256,128]{1,0:T(8,128)(2,1)S(1)}, bf16[256,128]{1,0:T(8,128)(2,1)S(1)}, u32[]{:S(2)}, u32[]{:S(2)}) collective-permute-start(bf16[256,128]{1,0:T(8,128)(2,1)S(1)} %fusion.2), channel_id=1, source_target_pairs={{0,2},{2,0},{1,3},{3,1},{4,6},{6,4},{5,7},{7,5},{8,10},{10,8},{9,1... | collective-permute-start | bytes 196616 | tf_op jit(solution)/shard_map/ppermute | solution.py:349
  112.7 12.8 %collective-permute-start.21 = (f32[2,256,256]{2,1,0:T(8,128)S(1)}, f32[2,256,256]{2,1,0:T(8,128)S(1)}, u32[]{:S(2)}, u32[]{:S(2)}) collective-permute-start(f32[2,256,256]{2,1,0:T(8,128)S(1)} %get-tuple-element.75), channel_id=1, source_target_pairs={{0,2},{2,0},{16,18},{18,16},{1,3},{3,1},{17,19},{19,17},{4,6},{6,4... | collective-permute-start | bytes 1572872 | tf_op jit(solution)/shard_map/ppermute | solution.py:44
  113.8 8.3 %collective-permute-start.17 = (bf16[512,128]{1,0:T(8,128)(2,1)S(1)}, bf16[512,128]{1,0:T(8,128)(2,1)S(1)}, u32[]{:S(2)}, u32[]{:S(2)}) collective-permute-start(bf16[512,128]{1,0:T(8,128)(2,1)S(1)} %get-tuple-element.87), channel_id=1, source_target_pairs={{0,4},{4,8},{8,12},{12,0},{1,5},{5,9},{9,13},{13,1},{2,6},{6,10},{... | collective-permute-start | bytes 393224 | tf_op jit(solution)/shard_map/ppermute | solution.py:366
  115.3 9.9 %collective-permute-start.18 = (bf16[512,128]{1,0:T(8,128)(2,1)S(1)}, bf16[512,128]{1,0:T(8,128)(2,1)S(1)}, u32[]{:S(2)}, u32[]{:S(2)}) collective-permute-start(bf16[512,128]{1,0:T(8,128)(2,1)S(1)} %get-tuple-element.87), channel_id=1, source_target_pairs={{0,8},{4,12},{8,0},{12,4},{1,9},{5,13},{9,1},{13,5},{2,10},{6,14},... | collective-permute-start | bytes 393224 | tf_op jit(solution)/shard_map/ppermute | solution.py:366
  116.3 8.9 %collective-permute-start.19 = (bf16[512,128]{1,0:T(8,128)(2,1)S(1)}, bf16[512,128]{1,0:T(8,128)(2,1)S(1)}, u32[]{:S(2)}, u32[]{:S(2)}) collective-permute-start(bf16[512,128]{1,0:T(8,128)(2,1)S(1)} %get-tuple-element.87), channel_id=1, source_target_pairs={{0,12},{4,0},{8,4},{12,8},{1,13},{5,1},{9,5},{13,9},{2,14},{6,2},{... | collective-permute-start | bytes 393224 | tf_op jit(solution)/shard_map/ppermute | solution.py:366
  118.6 11.7 %collective-permute-start.15 = (f32[2,256,256]{2,1,0:T(8,128)S(1)}, f32[2,256,256]{2,1,0:T(8,128)S(1)}, u32[]{:S(2)}, u32[]{:S(2)}) collective-permute-start(f32[2,256,256]{2,1,0:T(8,128)S(1)} %get-tuple-element.69), channel_id=1, source_target_pairs={{0,16},{2,18},{16,0},{18,2},{1,17},{3,19},{17,1},{19,3},{4,20},{6,... | collective-permute-start | bytes 1572872 | tf_op jit(solution)/shard_map/ppermute | solution.py:44
  125.3 6.7 %collective-permute-start.20 = (bf16[2048,128]{1,0:T(8,128)(2,1)S(1)}, bf16[2048,128]{1,0:T(8,128)(2,1)S(1)}, u32[]{:S(2)}, u32[]{:S(2)}) collective-permute-start(bf16[2048,128]{1,0:T(8,128)(2,1)S(1)} %constant_dynamic-update-slice_fusion.2.refs_6_), channel_id=1, source_target_pairs={{0,1},{1,0},{2,3},{3,2},{4,5},{5,4},{6,7},{7,6},{8,9},{9,8},{10,11... | collective-permute-start | bytes 1572872 | tf_op jit(solution)/shard_map/ppermute | solution.py:48
  126.4 9.6 %collective-permute-start.22 = (f32[256,256]{1,0:T(8,128)}, f32[256,256]{1,0:T(8,128)}, u32[]{:S(2)}, u32[]{:S(2)}) collective-permute-start(f32[256,256]{1,0:T(8,128)} %get-tuple-element.83), channel_id=1, source_target_pairs={{0,16},{2,18},{16,0},{18,2},{1,17},{3,19},{17,1},{19,3},{4,20},{6,... | collective-permute-start | bytes 786440 | tf_op jit(solution)/shard_map/ppermute | solution.py:44
  131.2 9.4 %collective-permute-start.16 = (f32[256,256]{1,0:T(8,128)}, f32[256,256]{1,0:T(8,128)}, u32[]{:S(2)}, u32[]{:S(2)}) collective-permute-start(f32[256,256]{1,0:T(8,128)} %get-tuple-element.81), channel_id=1, source_target_pairs={{0,2},{2,0},{16,18},{18,16},{1,3},{3,1},{17,19},{19,17},{4,6},{6,4... | collective-permute-start | bytes 786440 | tf_op jit(solution)/shard_map/ppermute | solution.py:44
  (20 other events, 105.2 us)

commit v6 on v5

--- a/solution.py
+++ b/solution.py
@@ -77,6 +77,12 @@
 def ways(place, zs):
     if place == 0:
         return [(None, "own", 0)]
+    if zs == 4:
+        return [
+            [(None, "pair", 1), (2, "pair", 2)],
+            [(None, "pair", 4), (1, "pair", 2), (2, "pair", 1)],
+            [(0, "last", 0), (1, "pair", 3), (2, "pair", 3), (3, "last", 0)],
+        ][place - 1]
     step = (place + 1) // 2
     inner = [(None, "up" if place % 2 else "down", step)] if place <= zs - 2 else []
     ends = [z for z in range(zs // 2) if 2 * z < place]
@@ -126,7 +132,7 @@
         + [pl.BlockSpec((rows, shape[2]), lambda i: (i, 0))] * shape[0],
         out_shape=[jax.ShapeDtypeStruct(shape, jnp.bfloat16)]
         + [jax.ShapeDtypeStruct(shape[1:], jnp.bfloat16)] * shape[0],
-        compiler_params=pltpu.CompilerParams(vmem_limit_bytes=24 * MIB),
+        compiler_params=pltpu.CompilerParams(vmem_limit_bytes=56 * MIB),
         cost_estimate=COST,
         name="norm",
     )(tokens, gain.astype(jnp.float32)[None, :])
@@ -312,10 +318,16 @@
     near, *far = normed
     near = lax.all_to_all(near, ("groups", "y"), 0, 0, tiled=True)
     pieces = {("own", 0): own}
-    came = [own, own]
-    for step in range(1, zs - 1):
-        came = [hop_down(came[0], step, zs), hop_up(came[1], step, zs)]
-        pieces["down", step], pieces["up", step] = came
+    if zs == 4:
+        ends, middle = [(0, 1), (1, 0), (2, 3), (3, 2)], [(1, 2), (2, 1)]
+        first = [lax.ppermute(own, "z", ends), lax.ppermute(own, "z", middle)]
+        came = [lax.ppermute(first[0], "z", middle), lax.ppermute(first[1], "z", [(1, 0), (2, 3)])]
+        pieces.update({("pair", 1 + at): block for at, block in enumerate(first + came)})
+    else:
+        came = [own, own]
+        for step in range(1, zs - 1):
+            came = [hop_down(came[0], step, zs), hop_up(came[1], step, zs)]
+            pieces["down", step], pieces["up", step] = came
     far = lax.optimization_barrier((near, *far))[1:]
     far = [
         shift_square(part, dx, dy, groups, ys) if dx or dy else part
@@ -331,10 +343,12 @@
         cuts.append((first, heads * HEAD))
         first += heads * HEAD
     parts = [cuts[0], (HEAD, own.shape[1] - HEAD)]
-    last = [
-        hop_ends(jnp.where(z == 1, came[0][:, a : a + n], came[1][:, a : a + n]), zs)
-        for a, n in parts
-    ]
+    last = []
+    for a, n in parts:
+        block = came[0][:, a : a + n]
+        if zs != 4:
+            block = jnp.where(z == 1, block, came[1][:, a : a + n])
+        last.append(hop_ends(block, zs))
     sums = [collect(mine, others, pieces, [part], zs, ys, groups)[0] for part in parts]
 
     def to_owner(part, dx, dy):

time: 148 us -> 145 us (0.980)
  starting transfers between devices: 38.9 us -> 33.8 us
  local copies, waits for them, and re-layouts: 12 us -> 16.6 us
  other arithmetic: 10.5 us -> 6.05 us
  waiting for transfers between devices: 52.9 us -> 55.9 us
    select_n x2 -> x0, other arithmetic: 3.7 us -> none  [on_device(): jnp.where(z == 1, came[0][:, a:a + n], came[1][:, a:a + n])]
    pallas_call x1, Pallas kernels: 1.99 us -> 5.52 us  [norm_pieces(): pl.pallas_call(functools.partial(norm_kernel, zs, ys, groups, width), gri...]
    ppermute x4, starting transfers between devices: 11.2 us -> 7.84 us  [the longest x2 4.8 us: on_device(): first = [lax.ppermute(own, 'z', ends), lax.ppermute(own, 'z', middle)]]
    slice x0 -> x2, local copies, waits for them, and re-layouts: none -> 3.36 us  [on_device(): block = came[0][:, a:a + n]]
    ppermute x10, starting transfers between devices: 13.4 us -> 10.1 us  [shift_square(): return lax.ppermute(block, ('groups', 'y'), route)]
    ppermute x10, waiting for transfers between devices: 26.2 us -> 29 us  [shift_square(): return lax.ppermute(block, ('groups', 'y'), route)]
    ppermute x3, starting transfers between devices: 4.75 us -> 6.94 us  [on_device(): lax.ppermute(both, 'z', [(i, (i + n) % zs) for i in range(zs)])]
    pallas_call x2, Pallas kernels: 6.02 us -> 3.98 us  [finish(): pl.pallas_call(functools.partial(finish_kernel, layout), grid=(1,), in_sp...]
where the time goes in v6:
time: 145 us; the launch traced here: 144 us
  waiting for transfers between devices  55.9 us (39%)
  starting transfers between devices  33.8 us (23%)
  Pallas kernels  31.6 us (22%)
  local copies, waits for them, and re-layouts  16.6 us (11%)
  other arithmetic  6.05 us (4%)
    ppermute x10, waiting for transfers between devices, shift_square(): return lax.ppermute(block, ('groups', 'y'), route)  29 us
    ppermute x2, waiting for transfers between devices, on_device(): first = [lax.ppermute(own, 'z', ends), lax.ppermute(own, 'z', middle)]  15.9 us
    pallas_call x2, Pallas kernels, collect(): pl.pallas_call(functools.partial(collect_kernel, zs, ys, groups, list(pie...  15 us
    ppermute x10, starting transfers between devices, shift_square(): return lax.ppermute(block, ('groups', 'y'), route)  10.1 us
    unnamed x39, local copies, waits for them, and re-layouts  9.17 us
    pallas_call x2, Pallas kernels, attend(): pl.pallas_call(functools.partial(attend_kernel, len(partials), window), g...  7.09 us
    ppermute x3, starting transfers between devices, on_device(): lax.ppermute(both, 'z', [(i, (i + n) % zs) for i in range(zs)])  6.94 us
    pallas_call x1, Pallas kernels, norm_pieces(): pl.pallas_call(functools.partial(norm_kernel, zs, ys, groups, width), gri...  5.52 us
  transfers between devices with their start and end apart: 26, of which 13 were waited for; matrix products, arithmetic and copies ran while one was open for 9% of the time, Pallas kernels for 22%

profile of v6, /device:TPU:0, one launch (start us, length us, event | category | flops | bytes accessed | tf_op | source)
XLA Modules:
  0.0 144.4 jit_solution(15945654053141490212)
XLA Ops:
  1.9 3.1 %collective-permute-start.3 = (bf16[1024,640]{1,0:T(8,128)(2,1)S(1)}, bf16[1024,640]{1,0:T(8,128)(2,1)}, u32[]{:S(2)}, u32[]{:S(2)}) collective-permute-start(bf16[1024,640]{1,0:T(8,128)(2,1)S(1)} %pad_maximum_fusion.1.refs_4_), channel_id=1, source_target_pairs={{0,4},{4,0},{8,12},{12,8},{1,5},{5,1},{9,13},{13,9},{2,6},{6,2},{1... | collective-permute-start | bytes 3932168 | tf_op jit(solution)/shard_map/ppermute | solution.py:323
  5.0 1.7 %collective-permute-start.5 = (bf16[1024,640]{1,0:T(8,128)(2,1)S(1)}, bf16[1024,640]{1,0:T(8,128)(2,1)}, u32[]{:S(2)}, u32[]{:S(2)}) collective-permute-start(bf16[1024,640]{1,0:T(8,128)(2,1)S(1)} %pad_maximum_fusion.1.refs_4_), channel_id=1, source_target_pairs={{4,8},{8,4},{5,9},{9,5},{6,10},{10,6},{7,11},{11,7},{20,24},{24,20... | collective-permute-start | bytes 3932168 | tf_op jit(solution)/shard_map/ppermute | solution.py:323
  7.3 5.5 %norm.1 = (bf16[4,128,2048]{2,1,0:T(8,128)(2,1)}, bf16[128,2048]{1,0:T(8,128)(2,1)}, bf16[128,2048]{1,0:T(8,128)(2,1)}, bf16[128,2048]{1,0:T(8,128)(2,1)}, bf16[128,2048]{1,0:T(8,128)(2,1)}) custom-call(bf16[128,16384]{1,0:T(8,128)(2,1)} %tokens.1, f32[1,16384]{1,0:T(1,128)} %bitcast.31), custom_call_target="tpu_custom_call" | custom-call | flops 1 | bytes 1 | tf_op jit(solution)/shard_map/norm/pallas_call | solution.py:124
  12.9 4.6 %all-to-all-start = ((bf16[4,128,2048]{2,1,0:T(8,128)(2,1)}), bf16[4,128,2048]{2,1,0:T(8,128)(2,1)}, u32[]{:S(2)}, u32[]{:S(2)}) async-start(bf16[4,128,2048]{2,1,0:T(8,128)(2,1)} %get-tuple-element.41), calls=%async_computation | async-start | bytes 4194304 | tf_op jit(solution)/shard_map/all_to_all | solution.py:319
  17.9 15.9 %collective-permute-done.3.refs_5_ = bf16[1024,640]{1,0:T(8,128)(2,1)} collective-permute-done((bf16[1024,640]{1,0:T(8,128)(2,1)S(1)}, bf16[1024,640]{1,0:T(8,128)(2,1)}, u32[]{:S(2)}, u32[]{:S(2)}) %collective-permute-start.3) | collective-permute-done | bytes 1310752 | tf_op jit(solution)/shard_map/ppermute | solution.py:323
  33.8 1.8 %collective-permute-start.4 = (bf16[1024,640]{1,0:T(8,128)(2,1)}, bf16[1024,640]{1,0:T(8,128)(2,1)}, u32[]{:S(2)}, u32[]{:S(2)}) collective-permute-start(bf16[1024,640]{1,0:T(8,128)(2,1)} %collective-permute-done.3.refs_5_), channel_id=1, source_target_pairs={{4,8},{8,4},{5,9},{9,5},{6,10},{10,6},{7,11},{11,7},{20,24},{24,20... | collective-permute-start | bytes 3932168 | tf_op jit(solution)/shard_map/ppermute | solution.py:324
  39.1 3.2 %all-to-all-done.refs_0_ = bf16[4,128,2048]{2,1,0:T(8,128)(2,1)} async-done(((bf16[4,128,2048]{2,1,0:T(8,128)(2,1)}), bf16[4,128,2048]{2,1,0:T(8,128)(2,1)}, u32[]{:S(2)}, u32[]{:S(2)}) %all-to-all-start) | async-done | bytes 2097184 | tf_op jit(solution)/shard_map/all_to_all | solution.py:319
  47.2 8.3 %collective-permute-done = bf16[128,2048]{1,0:T(8,128)(2,1)S(1)} collective-permute-done((bf16[128,2048]{1,0:T(8,128)(2,1)}, bf16[128,2048]{1,0:T(8,128)(2,1)S(1)}, u32[]{:S(2)}, u32[]{:S(2)}) %collective-permute-start) | collective-permute-done | bytes 524320 | tf_op jit(solution)/shard_map/ppermute | solution.py:44
  55.5 3.4 %collective-permute-done.1 = bf16[128,2048]{1,0:T(8,128)(2,1)S(1)} collective-permute-done((bf16[128,2048]{1,0:T(8,128)(2,1)}, bf16[128,2048]{1,0:T(8,128)(2,1)S(1)}, u32[]{:S(2)}, u32[]{:S(2)}) %collective-permute-start.1) | collective-permute-done | bytes 524320 | tf_op jit(solution)/shard_map/ppermute | solution.py:44
  58.9 9.6 %collective-permute-done.2 = bf16[128,2048]{1,0:T(8,128)(2,1)S(1)} collective-permute-done((bf16[128,2048]{1,0:T(8,128)(2,1)}, bf16[128,2048]{1,0:T(8,128)(2,1)S(1)}, u32[]{:S(2)}, u32[]{:S(2)}) %collective-permute-start.2) | collective-permute-done | bytes 524320 | tf_op jit(solution)/shard_map/ppermute | solution.py:44
  72.8 2.3 %slice.29 = bf16[1024,512]{1,0:T(8,128)(2,1)} slice(bf16[1024,640]{1,0:T(8,128)(2,1)} %collective-permute-done.4.refs_7_), slice={[0:1024], [128:640]} | slice | bytes 2097152 | tf_op jit(solution)/shard_map/slice | solution.py:348
  78.4 6.0 %collect.2.sums = f32[1024,128]{1,0:T(8,128)S(1)} custom-call(bf16[4,128,2048]{2,1,0:T(8,128)(2,1)} %all-to-all-done.refs_0_, bf16[4,128,2048]{2,1,0:T(8,128)(2,1)S(1)} %pad_maximum_fusion.refs_1_.mine, bf16[4,128,2048]{2,1,0:T(8,128)(2,1)S(1)} %collective-permute-done.9.refs_2_, bf16[4,128,2048]{2,1,0:T(8,128)(2,1)} %copy-done.3, ...), custom_call_target="tpu_custom_call" | custom-call | flops 1 | bytes 1 | tf_op jit(solution)/shard_map/collect/pallas_call | solution.py:181
  85.8 1.6 %copy-done.4 = bf16[4,128,2048]{2,1,0:T(8,128)(2,1)S(1)} copy-done((bf16[4,128,2048]{2,1,0:T(8,128)(2,1)S(1)}, bf16[4,128,2048]{2,1,0:T(8,128)(2,1)}, u32[]{:S(2)}) %copy-start.4) | copy-done | bytes 2097176
  89.9 1.6 %collective-permute-start.11 = (f32[256,128]{1,0:T(8,128)}, f32[256,128]{1,0:T(8,128)}, u32[]{:S(2)}, u32[]{:S(2)}) collective-permute-start(f32[256,128]{1,0:T(8,128)} %bitcast.12), channel_id=1, source_target_pairs={{0,16},{2,18},{16,0},{18,2},{1,17},{3,19},{17,1},{19,3},{4,20},{6,... | collective-permute-start | bytes 393224 | tf_op jit(solution)/shard_map/ppermute | solution.py:44
  94.5 8.9 %collect.3.sums = f32[1024,512]{1,0:T(8,128)S(1)} custom-call(bf16[4,128,2048]{2,1,0:T(8,128)(2,1)} %all-to-all-done.refs_0_, bf16[4,128,2048]{2,1,0:T(8,128)(2,1)S(1)} %copy-done.2, bf16[4,128,2048]{2,1,0:T(8,128)(2,1)} %copy-done.6, bf16[4,128,2048]{2,1,0:T(8,128)(2,1)} %copy-done.3, bf16[1024,640]{1,0:T(8,128)(2,1)S(1)} %pad_maximum_fusion.1.refs_4_, ...), custom_call_target="tpu_custom_call" | custom-call | flops 1 | bytes 1 | tf_op jit(solution)/shard_map/collect/pallas_call | solution.py:181
  105.4 2.6 %finish.3 = (f32[2,256,256]{2,1,0:T(8,128)S(1)}, f32[2,256,256]{2,1,0:T(8,128)S(1)}, f32[2,256,256]{2,1,0:T(8,128)S(1)}, f32[2,256,256]{2,1,0:T(8,128)S(1)}) custom-call(bf16[4,128,2048]{2,1,0:T(8,128)(2,1)S(1)} %copy-done.2, bf16[4,128,2048]{2,1,0:T(8,128)(2,1)S(1)} %copy-done.5, bf16[1024,512]{1,0:T(8,128)(2,1)} %collective-permute-done.13.last, ...), custom_call_target="tpu_custom_call" | custom-call | flops 1 | bytes 1 | tf_op jit(solution)/shard_map/finish/pallas_call | solution.py:213
  109.2 1.7 %collective-permute-start.15 = (f32[2,256,256]{2,1,0:T(8,128)S(1)}, f32[2,256,256]{2,1,0:T(8,128)S(1)}, u32[]{:S(2)}, u32[]{:S(2)}) collective-permute-start(f32[2,256,256]{2,1,0:T(8,128)S(1)} %get-tuple-element.67), channel_id=1, source_target_pairs={{0,16},{2,18},{16,0},{18,2},{1,17},{3,19},{17,1},{19,3},{4,20},{6,... | collective-permute-start | bytes 1572872 | tf_op jit(solution)/shard_map/ppermute | solution.py:44
  110.9 3.4 %collective-permute-start.17 = (bf16[512,128]{1,0:T(8,128)(2,1)S(1)}, bf16[512,128]{1,0:T(8,128)(2,1)S(1)}, u32[]{:S(2)}, u32[]{:S(2)}) collective-permute-start(bf16[512,128]{1,0:T(8,128)(2,1)S(1)} %get-tuple-element.85), channel_id=1, source_target_pairs={{0,4},{4,8},{8,12},{12,0},{1,5},{5,9},{9,13},{13,1},{2,6},{6,10},{... | collective-permute-start | bytes 393224 | tf_op jit(solution)/shard_map/ppermute | solution.py:380
  115.0 2.8 %collective-permute-start.19 = (bf16[512,128]{1,0:T(8,128)(2,1)S(1)}, bf16[512,128]{1,0:T(8,128)(2,1)S(1)}, u32[]{:S(2)}, u32[]{:S(2)}) collective-permute-start(bf16[512,128]{1,0:T(8,128)(2,1)S(1)} %get-tuple-element.85), channel_id=1, source_target_pairs={{0,12},{4,0},{8,4},{12,8},{1,13},{5,1},{9,5},{13,9},{2,14},{6,2},{... | collective-permute-start | bytes 393224 | tf_op jit(solution)/shard_map/ppermute | solution.py:380
  119.2 4.0 %collective-permute-done.18 = bf16[512,128]{1,0:T(8,128)(2,1)S(1)} collective-permute-done((bf16[512,128]{1,0:T(8,128)(2,1)S(1)}, bf16[512,128]{1,0:T(8,128)(2,1)S(1)}, u32[]{:S(2)}, u32[]{:S(2)}) %collective-permute-start.18) | collective-permute-done | bytes 131104 | tf_op jit(solution)/shard_map/ppermute | solution.py:380
  125.0 3.9 %collective-permute-done.21 = f32[2,256,256]{2,1,0:T(8,128)S(1)} collective-permute-done((f32[2,256,256]{2,1,0:T(8,128)S(1)}, f32[2,256,256]{2,1,0:T(8,128)S(1)}, u32[]{:S(2)}, u32[]{:S(2)}) %collective-permute-start.21) | collective-permute-done | bytes 524320 | tf_op jit(solution)/shard_map/ppermute | solution.py:44
  130.2 3.8 %collective-permute-done.16.refs_1_ = f32[256,256]{1,0:T(8,128)} collective-permute-done((f32[256,256]{1,0:T(8,128)}, f32[256,256]{1,0:T(8,128)}, u32[]{:S(2)}, u32[]{:S(2)}) %collective-permute-start.16) | collective-permute-done | bytes 262176 | tf_op jit(solution)/shard_map/ppermute | solution.py:44
  135.0 3.5 %attend.2 = (bf16[128,256]{1,0:T(8,128)(2,1)S(1)}, bf16[128,256]{1,0:T(8,128)(2,1)S(1)}) custom-call(s32[9]{0:T(128)S(1)} %concatenate.35.place, f32[256,256]{1,0:T(8,128)S(1)} %copy-done.10, f32[256,256]{1,0:T(8,128)} %collective-permute-done.16.refs_1_, f32[256,128]{1,0:T(8,128)S(1)} %get-tuple-element.58.refs_2_, f32[256,128]{1,0:T(8,128)S(1)} %copy-done.8, ...), custom_call_target="tpu_custom_call" | custom-call | flops 1 | bytes 1 | tf_op jit(solution)/shard_map/attend/pallas_call | solution.py:266
  138.6 3.6 %attend.3 = (bf16[128,256]{1,0:T(8,128)(2,1)S(1)}, bf16[128,256]{1,0:T(8,128)(2,1)S(1)}) custom-call(s32[9]{0:T(128)S(1)} %concatenate.35.place, f32[256,256]{1,0:T(8,128)S(1)} %copy-done.9, f32[256,256]{1,0:T(8,128)} %collective-permute-done.22.refs_1_, f32[256,128]{1,0:T(8,128)S(1)} %get-tuple-element.58.refs_2_, f32[256,128]{1,0:T(8,128)S(1)} %copy-done.8, ...), custom_call_target="tpu_custom_call" | custom-call | flops 1 | bytes 1 | tf_op jit(solution)/shard_map/attend/pallas_call | solution.py:266
  (112 shorter events, 37.0 us)
Async XLA Ops:
  1.9 32.0 %collective-permute-start.3 = (bf16[1024,640]{1,0:T(8,128)(2,1)S(1)}, bf16[1024,640]{1,0:T(8,128)(2,1)}, u32[]{:S(2)}, u32[]{:S(2)}) collective-permute-start(bf16[1024,640]{1,0:T(8,128)(2,1)S(1)} %pad_maximum_fusion.1.refs_4_), channel_id=1, source_target_pairs={{0,4},{4,0},{8,12},{12,8},{1,5},{5,1},{9,13},{13,9},{2,6},{6,2},{1... | collective-permute-start | bytes 3932168 | tf_op jit(solution)/shard_map/ppermute | solution.py:323
  5.0 30.6 %collective-permute-start.5 = (bf16[1024,640]{1,0:T(8,128)(2,1)S(1)}, bf16[1024,640]{1,0:T(8,128)(2,1)}, u32[]{:S(2)}, u32[]{:S(2)}) collective-permute-start(bf16[1024,640]{1,0:T(8,128)(2,1)S(1)} %pad_maximum_fusion.1.refs_4_), channel_id=1, source_target_pairs={{4,8},{8,4},{5,9},{9,5},{6,10},{10,6},{7,11},{11,7},{20,24},{24,20... | collective-permute-start | bytes 3932168 | tf_op jit(solution)/shard_map/ppermute | solution.py:323
  12.9 29.5 %all-to-all-start = ((bf16[4,128,2048]{2,1,0:T(8,128)(2,1)}), bf16[4,128,2048]{2,1,0:T(8,128)(2,1)}, u32[]{:S(2)}, u32[]{:S(2)}) async-start(bf16[4,128,2048]{2,1,0:T(8,128)(2,1)} %get-tuple-element.41), calls=%async_computation | async-start | bytes 4194304 | tf_op jit(solution)/shard_map/all_to_all | solution.py:319
  33.8 36.0 %collective-permute-start.4 = (bf16[1024,640]{1,0:T(8,128)(2,1)}, bf16[1024,640]{1,0:T(8,128)(2,1)}, u32[]{:S(2)}, u32[]{:S(2)}) collective-permute-start(bf16[1024,640]{1,0:T(8,128)(2,1)} %collective-permute-done.3.refs_5_), channel_id=1, source_target_pairs={{4,8},{8,4},{5,9},{9,5},{6,10},{10,6},{7,11},{11,7},{20,24},{24,20... | collective-permute-start | bytes 3932168 | tf_op jit(solution)/shard_map/ppermute | solution.py:324
  35.6 34.2 %collective-permute-start.6 = (bf16[1024,640]{1,0:T(8,128)(2,1)}, bf16[1024,640]{1,0:T(8,128)(2,1)}, u32[]{:S(2)}, u32[]{:S(2)}) collective-permute-start(bf16[1024,640]{1,0:T(8,128)(2,1)} %collective-permute-done.5.refs_6_), channel_id=1, source_target_pairs={{4,0},{8,12},{5,1},{9,13},{6,2},{10,14},{7,3},{11,15},{20,16},{24,... | collective-permute-start | bytes 3932168 | tf_op jit(solution)/shard_map/ppermute | solution.py:324
  42.4 13.1 %collective-permute-start = (bf16[128,2048]{1,0:T(8,128)(2,1)}, bf16[128,2048]{1,0:T(8,128)(2,1)S(1)}, u32[]{:S(2)}, u32[]{:S(2)}) collective-permute-start(bf16[128,2048]{1,0:T(8,128)(2,1)} %get-tuple-element.48), channel_id=1, source_target_pairs={{0,2},{2,0},{16,18},{18,16},{1,3},{3,1},{17,19},{19,17},{4,6},{6,4... | collective-permute-start | bytes 1572872 | tf_op jit(solution)/shard_map/ppermute | solution.py:44
  43.8 15.1 %collective-permute-start.1 = (bf16[128,2048]{1,0:T(8,128)(2,1)}, bf16[128,2048]{1,0:T(8,128)(2,1)S(1)}, u32[]{:S(2)}, u32[]{:S(2)}) collective-permute-start(bf16[128,2048]{1,0:T(8,128)(2,1)} %get-tuple-element.49), channel_id=1, source_target_pairs={{0,16},{2,18},{16,0},{18,2},{1,17},{3,19},{17,1},{19,3},{4,20},{6,... | collective-permute-start | bytes 1572872 | tf_op jit(solution)/shard_map/ppermute | solution.py:44
  44.4 24.1 %collective-permute-start.2 = (bf16[128,2048]{1,0:T(8,128)(2,1)}, bf16[128,2048]{1,0:T(8,128)(2,1)S(1)}, u32[]{:S(2)}, u32[]{:S(2)}) collective-permute-start(bf16[128,2048]{1,0:T(8,128)(2,1)} %get-tuple-element.50), channel_id=1, source_target_pairs={{0,18},{2,16},{16,2},{18,0},{1,19},{3,17},{17,3},{19,1},{4,22},{6,... | collective-permute-start | bytes 1572872 | tf_op jit(solution)/shard_map/ppermute | solution.py:44
  69.8 6.7 %collective-permute-start.9 = (bf16[4,128,2048]{2,1,0:T(8,128)(2,1)}, bf16[4,128,2048]{2,1,0:T(8,128)(2,1)S(1)}, u32[]{:S(2)}, u32[]{:S(2)}) collective-permute-start(bf16[4,128,2048]{2,1,0:T(8,128)(2,1)} %all-to-all-done.refs_0_), channel_id=1, source_target_pairs={{0,1},{1,0},{2,3},{3,2},{4,5},{5,4},{6,7},{7,6},{8,9},{9,8},{10,11... | collective-permute-start | bytes 6291464 | tf_op jit(solution)/shard_map/ppermute | solution.py:48
  69.9 7.1 %collective-permute-start.7 = (bf16[4,128,2048]{2,1,0:T(8,128)(2,1)S(1)}, bf16[4,128,2048]{2,1,0:T(8,128)(2,1)S(1)}, u32[]{:S(2)}, u32[]{:S(2)}) collective-permute-start(bf16[4,128,2048]{2,1,0:T(8,128)(2,1)S(1)} %pad_maximum_fusion.refs_1_.mine), channel_id=1, source_target_pairs={{0,1},{1,0},{2,3},{3,2},{4,5},{5,4},{6,7},{7,6},{8,9},{9,8},{10,11... | collective-permute-start | bytes 6291464 | tf_op jit(solution)/shard_map/ppermute | solution.py:48
  71.5 14.3 %collective-permute-start.8 = (bf16[1024,128]{1,0:T(8,128)(2,1)S(1)}, bf16[1024,128]{1,0:T(8,128)(2,1)S(1)}, u32[]{:S(2)}, u32[]{:S(2)}) collective-permute-start(bf16[1024,128]{1,0:T(8,128)(2,1)S(1)} %slice.26), channel_id=1, source_target_pairs={{4,0},{8,12},{5,1},{9,13},{6,2},{10,14},{7,3},{11,15},{20,16},{24,... | collective-permute-start | bytes 786440 | tf_op jit(solution)/shard_map/hop_ends/ppermute | solution.py:67
  75.1 29.8 %collective-permute-start.13 = (bf16[1024,512]{1,0:T(8,128)(2,1)}, bf16[1024,512]{1,0:T(8,128)(2,1)}, u32[]{:S(2)}, u32[]{:S(2)}) collective-permute-start(bf16[1024,512]{1,0:T(8,128)(2,1)} %slice.29), channel_id=1, source_target_pairs={{4,0},{8,12},{5,1},{9,13},{6,2},{10,14},{7,3},{11,15},{20,16},{24,... | collective-permute-start | bytes 3145736 | tf_op jit(solution)/shard_map/hop_ends/ppermute | solution.py:67
  89.5 14.0 %collective-permute-start.10 = (f32[256,128]{1,0:T(8,128)}, f32[256,128]{1,0:T(8,128)}, u32[]{:S(2)}, u32[]{:S(2)}) collective-permute-start(f32[256,128]{1,0:T(8,128)} %bitcast.11), channel_id=1, source_target_pairs={{0,2},{2,0},{16,18},{18,16},{1,3},{3,1},{17,19},{19,17},{4,6},{6,4... | collective-permute-start | bytes 393224 | tf_op jit(solution)/shard_map/ppermute | solution.py:44
  89.9 13.6 %collective-permute-start.11 = (f32[256,128]{1,0:T(8,128)}, f32[256,128]{1,0:T(8,128)}, u32[]{:S(2)}, u32[]{:S(2)}) collective-permute-start(f32[256,128]{1,0:T(8,128)} %bitcast.12), channel_id=1, source_target_pairs={{0,16},{2,18},{16,0},{18,2},{1,17},{3,19},{17,1},{19,3},{4,20},{6,... | collective-permute-start | bytes 393224 | tf_op jit(solution)/shard_map/ppermute | solution.py:44
  91.5 12.0 %collective-permute-start.12 = (f32[256,128]{1,0:T(8,128)}, f32[256,128]{1,0:T(8,128)}, u32[]{:S(2)}, u32[]{:S(2)}) collective-permute-start(f32[256,128]{1,0:T(8,128)} %bitcast.13), channel_id=1, source_target_pairs={{0,18},{2,16},{16,2},{18,0},{1,19},{3,17},{17,3},{19,1},{4,22},{6,... | collective-permute-start | bytes 393224 | tf_op jit(solution)/shard_map/ppermute | solution.py:44
  104.9 4.3 %collective-permute-start.14 = (bf16[256,128]{1,0:T(8,128)(2,1)S(1)}, bf16[256,128]{1,0:T(8,128)(2,1)S(1)}, u32[]{:S(2)}, u32[]{:S(2)}) collective-permute-start(bf16[256,128]{1,0:T(8,128)(2,1)S(1)} %fusion.2), channel_id=1, source_target_pairs={{0,2},{2,0},{1,3},{3,1},{4,6},{6,4},{5,7},{7,5},{8,10},{10,8},{9,1... | collective-permute-start | bytes 196616 | tf_op jit(solution)/shard_map/ppermute | solution.py:363
  109.2 14.3 %collective-permute-start.15 = (f32[2,256,256]{2,1,0:T(8,128)S(1)}, f32[2,256,256]{2,1,0:T(8,128)S(1)}, u32[]{:S(2)}, u32[]{:S(2)}) collective-permute-start(f32[2,256,256]{2,1,0:T(8,128)S(1)} %get-tuple-element.67), channel_id=1, source_target_pairs={{0,16},{2,18},{16,0},{18,2},{1,17},{3,19},{17,1},{19,3},{4,20},{6,... | collective-permute-start | bytes 1572872 | tf_op jit(solution)/shard_map/ppermute | solution.py:44
  110.9 8.3 %collective-permute-start.17 = (bf16[512,128]{1,0:T(8,128)(2,1)S(1)}, bf16[512,128]{1,0:T(8,128)(2,1)S(1)}, u32[]{:S(2)}, u32[]{:S(2)}) collective-permute-start(bf16[512,128]{1,0:T(8,128)(2,1)S(1)} %get-tuple-element.85), channel_id=1, source_target_pairs={{0,4},{4,8},{8,12},{12,0},{1,5},{5,9},{9,13},{13,1},{2,6},{6,10},{... | collective-permute-start | bytes 393224 | tf_op jit(solution)/shard_map/ppermute | solution.py:380
  114.4 8.9 %collective-permute-start.18 = (bf16[512,128]{1,0:T(8,128)(2,1)S(1)}, bf16[512,128]{1,0:T(8,128)(2,1)S(1)}, u32[]{:S(2)}, u32[]{:S(2)}) collective-permute-start(bf16[512,128]{1,0:T(8,128)(2,1)S(1)} %get-tuple-element.85), channel_id=1, source_target_pairs={{0,8},{4,12},{8,0},{12,4},{1,9},{5,13},{9,1},{13,5},{2,10},{6,14},... | collective-permute-start | bytes 393224 | tf_op jit(solution)/shard_map/ppermute | solution.py:380
  115.0 8.3 %collective-permute-start.19 = (bf16[512,128]{1,0:T(8,128)(2,1)S(1)}, bf16[512,128]{1,0:T(8,128)(2,1)S(1)}, u32[]{:S(2)}, u32[]{:S(2)}) collective-permute-start(bf16[512,128]{1,0:T(8,128)(2,1)S(1)} %get-tuple-element.85), channel_id=1, source_target_pairs={{0,12},{4,0},{8,4},{12,8},{1,13},{5,1},{9,5},{13,9},{2,14},{6,2},{... | collective-permute-start | bytes 393224 | tf_op jit(solution)/shard_map/ppermute | solution.py:380
  117.9 11.0 %collective-permute-start.21 = (f32[2,256,256]{2,1,0:T(8,128)S(1)}, f32[2,256,256]{2,1,0:T(8,128)S(1)}, u32[]{:S(2)}, u32[]{:S(2)}) collective-permute-start(f32[2,256,256]{2,1,0:T(8,128)S(1)} %get-tuple-element.73), channel_id=1, source_target_pairs={{0,2},{2,0},{16,18},{18,16},{1,3},{3,1},{17,19},{19,17},{4,6},{6,4... | collective-permute-start | bytes 1572872 | tf_op jit(solution)/shard_map/ppermute | solution.py:44
  123.3 6.9 %collective-permute-start.20 = (bf16[2048,128]{1,0:T(8,128)(2,1)S(1)}, bf16[2048,128]{1,0:T(8,128)(2,1)S(1)}, u32[]{:S(2)}, u32[]{:S(2)}) collective-permute-start(bf16[2048,128]{1,0:T(8,128)(2,1)S(1)} %constant_dynamic-update-slice_fusion.2.refs_6_), channel_id=1, source_target_pairs={{0,1},{1,0},{2,3},{3,2},{4,5},{5,4},{6,7},{7,6},{8,9},{9,8},{10,11... | collective-permute-start | bytes 1572872 | tf_op jit(solution)/shard_map/ppermute | solution.py:48
  124.3 9.7 %collective-permute-start.16 = (f32[256,256]{1,0:T(8,128)}, f32[256,256]{1,0:T(8,128)}, u32[]{:S(2)}, u32[]{:S(2)}) collective-permute-start(f32[256,256]{1,0:T(8,128)} %get-tuple-element.79), channel_id=1, source_target_pairs={{0,2},{2,0},{16,18},{18,16},{1,3},{3,1},{17,19},{19,17},{4,6},{6,4... | collective-permute-start | bytes 786440 | tf_op jit(solution)/shard_map/ppermute | solution.py:44
  129.8 8.8 %collective-permute-start.22 = (f32[256,256]{1,0:T(8,128)}, f32[256,256]{1,0:T(8,128)}, u32[]{:S(2)}, u32[]{:S(2)}) collective-permute-start(f32[256,256]{1,0:T(8,128)} %get-tuple-element.81), channel_id=1, source_target_pairs={{0,16},{2,18},{16,0},{18,2},{1,17},{3,19},{17,1},{19,3},{4,20},{6,... | collective-permute-start | bytes 786440 | tf_op jit(solution)/shard_map/ppermute | solution.py:44
  (20 other events, 122.0 us)

commit v7 on v6

--- a/solution.py
+++ b/solution.py
@@ -335,7 +335,7 @@
     ]
     mine = [near, jnp.stack(far)]
     done = (*mine, *came, *tables)
-    others = [swap_core(after(half, *done)) for half in mine]
+    others = [swap_core(mine[0]), swap_core(after(mine[1], *done))]
     came = [after(came[0], *done), after(came[1], *done)]
     cosine, sine, query_info, which_key, place = lax.optimization_barrier((*tables, near))[:5]
     cuts, first = [(0, HEAD)], HEAD

time: 145 us -> 145 us (level)
  transfers between devices with their start and end apart: 26 -> 26, of which waited for: 13 -> 12; matrix products, arithmetic and copies ran while one was open for 9% -> 9% of each run, Pallas kernels for 22% -> 22%
where the time goes in v7:
time: 145 us; the launch traced here: 144 us
  waiting for transfers between devices  56.5 us (39%)
  starting transfers between devices  33 us (23%)
  Pallas kernels  31.6 us (22%)
  local copies, waits for them, and re-layouts  16.8 us (12%)
  other arithmetic  6.05 us (4%)
    ppermute x10, waiting for transfers between devices, shift_square(): return lax.ppermute(block, ('groups', 'y'), route)  29 us
    ppermute x2, waiting for transfers between devices, on_device(): first = [lax.ppermute(own, 'z', ends), lax.ppermute(own, 'z', middle)]  15.9 us
    pallas_call x2, Pallas kernels, collect(): pl.pallas_call(functools.partial(collect_kernel, zs, ys, groups, list(pie...  15 us
    ppermute x10, starting transfers between devices, shift_square(): return lax.ppermute(block, ('groups', 'y'), route)  10.3 us
    unnamed x39, local copies, waits for them, and re-layouts  9.16 us
    pallas_call x2, Pallas kernels, attend(): pl.pallas_call(functools.partial(attend_kernel, len(partials), window), g...  7.09 us
    ppermute x3, starting transfers between devices, on_device(): lax.ppermute(both, 'z', [(i, (i + n) % zs) for i in range(zs)])  6.67 us
    pallas_call x1, Pallas kernels, norm_pieces(): pl.pallas_call(functools.partial(norm_kernel, zs, ys, groups, width), gri...  5.52 us
  transfers between devices with their start and end apart: 26, of which 12 were waited for; matrix products, arithmetic and copies ran while one was open for 9% of the time, Pallas kernels for 22%

profile of v7, /device:TPU:0, one launch (start us, length us, event | category | flops | bytes accessed | tf_op | source)
XLA Modules:
  0.0 144.3 jit_solution(10779282390317044443)
XLA Ops:
  1.9 3.1 %collective-permute-start.3 = (bf16[1024,640]{1,0:T(8,128)(2,1)S(1)}, bf16[1024,640]{1,0:T(8,128)(2,1)}, u32[]{:S(2)}, u32[]{:S(2)}) collective-permute-start(bf16[1024,640]{1,0:T(8,128)(2,1)S(1)} %pad_maximum_fusion.1.refs_4_), channel_id=1, source_target_pairs={{0,4},{4,0},{8,12},{12,8},{1,5},{5,1},{9,13},{13,9},{2,6},{6,2},{1... | collective-permute-start | bytes 3932168 | tf_op jit(solution)/shard_map/ppermute | solution.py:323
  5.0 1.7 %collective-permute-start.5 = (bf16[1024,640]{1,0:T(8,128)(2,1)S(1)}, bf16[1024,640]{1,0:T(8,128)(2,1)}, u32[]{:S(2)}, u32[]{:S(2)}) collective-permute-start(bf16[1024,640]{1,0:T(8,128)(2,1)S(1)} %pad_maximum_fusion.1.refs_4_), channel_id=1, source_target_pairs={{4,8},{8,4},{5,9},{9,5},{6,10},{10,6},{7,11},{11,7},{20,24},{24,20... | collective-permute-start | bytes 3932168 | tf_op jit(solution)/shard_map/ppermute | solution.py:323
  7.3 5.5 %norm.1 = (bf16[4,128,2048]{2,1,0:T(8,128)(2,1)}, bf16[128,2048]{1,0:T(8,128)(2,1)}, bf16[128,2048]{1,0:T(8,128)(2,1)}, bf16[128,2048]{1,0:T(8,128)(2,1)}, bf16[128,2048]{1,0:T(8,128)(2,1)}) custom-call(bf16[128,16384]{1,0:T(8,128)(2,1)} %tokens.1, f32[1,16384]{1,0:T(1,128)} %bitcast.31), custom_call_target="tpu_custom_call" | custom-call | flops 1 | bytes 1 | tf_op jit(solution)/shard_map/norm/pallas_call | solution.py:124
  12.9 4.6 %all-to-all-start = ((bf16[4,128,2048]{2,1,0:T(8,128)(2,1)}), bf16[4,128,2048]{2,1,0:T(8,128)(2,1)}, u32[]{:S(2)}, u32[]{:S(2)}) async-start(bf16[4,128,2048]{2,1,0:T(8,128)(2,1)} %get-tuple-element.40), calls=%async_computation | async-start | bytes 4194304 | tf_op jit(solution)/shard_map/all_to_all | solution.py:319
  17.9 15.9 %collective-permute-done.3.refs_5_ = bf16[1024,640]{1,0:T(8,128)(2,1)} collective-permute-done((bf16[1024,640]{1,0:T(8,128)(2,1)S(1)}, bf16[1024,640]{1,0:T(8,128)(2,1)}, u32[]{:S(2)}, u32[]{:S(2)}) %collective-permute-start.3) | collective-permute-done | bytes 1310752 | tf_op jit(solution)/shard_map/ppermute | solution.py:323
  33.8 1.8 %collective-permute-start.4 = (bf16[1024,640]{1,0:T(8,128)(2,1)}, bf16[1024,640]{1,0:T(8,128)(2,1)}, u32[]{:S(2)}, u32[]{:S(2)}) collective-permute-start(bf16[1024,640]{1,0:T(8,128)(2,1)} %collective-permute-done.3.refs_5_), channel_id=1, source_target_pairs={{4,8},{8,4},{5,9},{9,5},{6,10},{10,6},{7,11},{11,7},{20,24},{24,20... | collective-permute-start | bytes 3932168 | tf_op jit(solution)/shard_map/ppermute | solution.py:324
  39.1 3.2 %all-to-all-done.refs_0_ = bf16[4,128,2048]{2,1,0:T(8,128)(2,1)} async-done(((bf16[4,128,2048]{2,1,0:T(8,128)(2,1)}), bf16[4,128,2048]{2,1,0:T(8,128)(2,1)}, u32[]{:S(2)}, u32[]{:S(2)}) %all-to-all-start) | async-done | bytes 2097184 | tf_op jit(solution)/shard_map/all_to_all | solution.py:319
  47.2 8.3 %collective-permute-done = bf16[128,2048]{1,0:T(8,128)(2,1)S(1)} collective-permute-done((bf16[128,2048]{1,0:T(8,128)(2,1)}, bf16[128,2048]{1,0:T(8,128)(2,1)S(1)}, u32[]{:S(2)}, u32[]{:S(2)}) %collective-permute-start) | collective-permute-done | bytes 524320 | tf_op jit(solution)/shard_map/ppermute | solution.py:44
  55.5 3.4 %collective-permute-done.1 = bf16[128,2048]{1,0:T(8,128)(2,1)S(1)} collective-permute-done((bf16[128,2048]{1,0:T(8,128)(2,1)}, bf16[128,2048]{1,0:T(8,128)(2,1)S(1)}, u32[]{:S(2)}, u32[]{:S(2)}) %collective-permute-start.1) | collective-permute-done | bytes 524320 | tf_op jit(solution)/shard_map/ppermute | solution.py:44
  58.9 9.6 %collective-permute-done.2 = bf16[128,2048]{1,0:T(8,128)(2,1)S(1)} collective-permute-done((bf16[128,2048]{1,0:T(8,128)(2,1)}, bf16[128,2048]{1,0:T(8,128)(2,1)S(1)}, u32[]{:S(2)}, u32[]{:S(2)}) %collective-permute-start.2) | collective-permute-done | bytes 524320 | tf_op jit(solution)/shard_map/ppermute | solution.py:44
  72.4 2.3 %slice.29 = bf16[1024,512]{1,0:T(8,128)(2,1)} slice(bf16[1024,640]{1,0:T(8,128)(2,1)} %collective-permute-done.4.refs_7_), slice={[0:1024], [128:640]} | slice | bytes 2097152 | tf_op jit(solution)/shard_map/slice | solution.py:348
  77.4 6.0 %collect.2.sums = f32[1024,128]{1,0:T(8,128)S(1)} custom-call(bf16[4,128,2048]{2,1,0:T(8,128)(2,1)} %all-to-all-done.refs_0_, bf16[4,128,2048]{2,1,0:T(8,128)(2,1)S(1)} %pad_maximum_fusion.refs_1_.mine, bf16[4,128,2048]{2,1,0:T(8,128)(2,1)S(1)} %collective-permute-done.9.refs_2_, bf16[4,128,2048]{2,1,0:T(8,128)(2,1)} %copy-done.3, ...), custom_call_target="tpu_custom_call" | custom-call | flops 1 | bytes 1 | tf_op jit(solution)/shard_map/collect/pallas_call | solution.py:181
  84.8 1.6 %copy-done.4 = bf16[4,128,2048]{2,1,0:T(8,128)(2,1)S(1)} copy-done((bf16[4,128,2048]{2,1,0:T(8,128)(2,1)S(1)}, bf16[4,128,2048]{2,1,0:T(8,128)(2,1)}, u32[]{:S(2)}) %copy-start.4) | copy-done | bytes 2097176
  88.9 1.6 %collective-permute-start.11 = (f32[256,128]{1,0:T(8,128)}, f32[256,128]{1,0:T(8,128)}, u32[]{:S(2)}, u32[]{:S(2)}) collective-permute-start(f32[256,128]{1,0:T(8,128)} %bitcast.12), channel_id=1, source_target_pairs={{0,16},{2,18},{16,0},{18,2},{1,17},{3,19},{17,1},{19,3},{4,20},{6,... | collective-permute-start | bytes 393224 | tf_op jit(solution)/shard_map/ppermute | solution.py:44
  93.5 8.9 %collect.3.sums = f32[1024,512]{1,0:T(8,128)S(1)} custom-call(bf16[4,128,2048]{2,1,0:T(8,128)(2,1)} %all-to-all-done.refs_0_, bf16[4,128,2048]{2,1,0:T(8,128)(2,1)S(1)} %copy-done.2, bf16[4,128,2048]{2,1,0:T(8,128)(2,1)} %copy-done.6, bf16[4,128,2048]{2,1,0:T(8,128)(2,1)} %copy-done.3, bf16[1024,640]{1,0:T(8,128)(2,1)S(1)} %pad_maximum_fusion.1.refs_4_, ...), custom_call_target="tpu_custom_call" | custom-call | flops 1 | bytes 1 | tf_op jit(solution)/shard_map/collect/pallas_call | solution.py:181
  105.1 2.6 %finish.3 = (f32[2,256,256]{2,1,0:T(8,128)S(1)}, f32[2,256,256]{2,1,0:T(8,128)S(1)}, f32[2,256,256]{2,1,0:T(8,128)S(1)}, f32[2,256,256]{2,1,0:T(8,128)S(1)}) custom-call(bf16[4,128,2048]{2,1,0:T(8,128)(2,1)S(1)} %copy-done.2, bf16[4,128,2048]{2,1,0:T(8,128)(2,1)S(1)} %copy-done.5, bf16[1024,512]{1,0:T(8,128)(2,1)} %collective-permute-done.13.last, ...), custom_call_target="tpu_custom_call" | custom-call | flops 1 | bytes 1 | tf_op jit(solution)/shard_map/finish/pallas_call | solution.py:213
  109.1 1.7 %collective-permute-start.15 = (f32[2,256,256]{2,1,0:T(8,128)S(1)}, f32[2,256,256]{2,1,0:T(8,128)S(1)}, u32[]{:S(2)}, u32[]{:S(2)}) collective-permute-start(f32[2,256,256]{2,1,0:T(8,128)S(1)} %get-tuple-element.65), channel_id=1, source_target_pairs={{0,16},{2,18},{16,0},{18,2},{1,17},{3,19},{17,1},{19,3},{4,20},{6,... | collective-permute-start | bytes 1572872 | tf_op jit(solution)/shard_map/ppermute | solution.py:44
  110.8 3.2 %collective-permute-start.17 = (bf16[512,128]{1,0:T(8,128)(2,1)S(1)}, bf16[512,128]{1,0:T(8,128)(2,1)S(1)}, u32[]{:S(2)}, u32[]{:S(2)}) collective-permute-start(bf16[512,128]{1,0:T(8,128)(2,1)S(1)} %get-tuple-element.83), channel_id=1, source_target_pairs={{0,4},{4,8},{8,12},{12,0},{1,5},{5,9},{9,13},{13,1},{2,6},{6,10},{... | collective-permute-start | bytes 393224 | tf_op jit(solution)/shard_map/ppermute | solution.py:380
  114.7 2.8 %collective-permute-start.19 = (bf16[512,128]{1,0:T(8,128)(2,1)S(1)}, bf16[512,128]{1,0:T(8,128)(2,1)S(1)}, u32[]{:S(2)}, u32[]{:S(2)}) collective-permute-start(bf16[512,128]{1,0:T(8,128)(2,1)S(1)} %get-tuple-element.83), channel_id=1, source_target_pairs={{0,12},{4,0},{8,4},{12,8},{1,13},{5,1},{9,5},{13,9},{2,14},{6,2},{... | collective-permute-start | bytes 393224 | tf_op jit(solution)/shard_map/ppermute | solution.py:380
  119.1 3.9 %collective-permute-done.18 = bf16[512,128]{1,0:T(8,128)(2,1)S(1)} collective-permute-done((bf16[512,128]{1,0:T(8,128)(2,1)S(1)}, bf16[512,128]{1,0:T(8,128)(2,1)S(1)}, u32[]{:S(2)}, u32[]{:S(2)}) %collective-permute-start.18) | collective-permute-done | bytes 131104 | tf_op jit(solution)/shard_map/ppermute | solution.py:380
  124.9 4.1 %collective-permute-done.21 = f32[2,256,256]{2,1,0:T(8,128)S(1)} collective-permute-done((f32[2,256,256]{2,1,0:T(8,128)S(1)}, f32[2,256,256]{2,1,0:T(8,128)S(1)}, u32[]{:S(2)}, u32[]{:S(2)}) %collective-permute-start.21) | collective-permute-done | bytes 524320 | tf_op jit(solution)/shard_map/ppermute | solution.py:44
  130.3 3.6 %collective-permute-done.16.refs_1_ = f32[256,256]{1,0:T(8,128)} collective-permute-done((f32[256,256]{1,0:T(8,128)}, f32[256,256]{1,0:T(8,128)}, u32[]{:S(2)}, u32[]{:S(2)}) %collective-permute-start.16) | collective-permute-done | bytes 262176 | tf_op jit(solution)/shard_map/ppermute | solution.py:44
  134.9 3.5 %attend.2 = (bf16[128,256]{1,0:T(8,128)(2,1)S(1)}, bf16[128,256]{1,0:T(8,128)(2,1)S(1)}) custom-call(s32[9]{0:T(128)S(1)} %concatenate.35.place, f32[256,256]{1,0:T(8,128)S(1)} %copy-done.10, f32[256,256]{1,0:T(8,128)} %collective-permute-done.16.refs_1_, f32[256,128]{1,0:T(8,128)S(1)} %get-tuple-element.56.refs_2_, f32[256,128]{1,0:T(8,128)S(1)} %copy-done.8, ...), custom_call_target="tpu_custom_call" | custom-call | flops 1 | bytes 1 | tf_op jit(solution)/shard_map/attend/pallas_call | solution.py:266
  138.5 3.6 %attend.3 = (bf16[128,256]{1,0:T(8,128)(2,1)S(1)}, bf16[128,256]{1,0:T(8,128)(2,1)S(1)}) custom-call(s32[9]{0:T(128)S(1)} %concatenate.35.place, f32[256,256]{1,0:T(8,128)S(1)} %copy-done.9, f32[256,256]{1,0:T(8,128)} %collective-permute-done.22.refs_1_, f32[256,128]{1,0:T(8,128)S(1)} %get-tuple-element.56.refs_2_, f32[256,128]{1,0:T(8,128)S(1)} %copy-done.8, ...), custom_call_target="tpu_custom_call" | custom-call | flops 1 | bytes 1 | tf_op jit(solution)/shard_map/attend/pallas_call | solution.py:266
  (112 shorter events, 37.3 us)
Async XLA Ops:
  1.9 32.0 %collective-permute-start.3 = (bf16[1024,640]{1,0:T(8,128)(2,1)S(1)}, bf16[1024,640]{1,0:T(8,128)(2,1)}, u32[]{:S(2)}, u32[]{:S(2)}) collective-permute-start(bf16[1024,640]{1,0:T(8,128)(2,1)S(1)} %pad_maximum_fusion.1.refs_4_), channel_id=1, source_target_pairs={{0,4},{4,0},{8,12},{12,8},{1,5},{5,1},{9,13},{13,9},{2,6},{6,2},{1... | collective-permute-start | bytes 3932168 | tf_op jit(solution)/shard_map/ppermute | solution.py:323
  5.0 30.6 %collective-permute-start.5 = (bf16[1024,640]{1,0:T(8,128)(2,1)S(1)}, bf16[1024,640]{1,0:T(8,128)(2,1)}, u32[]{:S(2)}, u32[]{:S(2)}) collective-permute-start(bf16[1024,640]{1,0:T(8,128)(2,1)S(1)} %pad_maximum_fusion.1.refs_4_), channel_id=1, source_target_pairs={{4,8},{8,4},{5,9},{9,5},{6,10},{10,6},{7,11},{11,7},{20,24},{24,20... | collective-permute-start | bytes 3932168 | tf_op jit(solution)/shard_map/ppermute | solution.py:323
  12.9 29.5 %all-to-all-start = ((bf16[4,128,2048]{2,1,0:T(8,128)(2,1)}), bf16[4,128,2048]{2,1,0:T(8,128)(2,1)}, u32[]{:S(2)}, u32[]{:S(2)}) async-start(bf16[4,128,2048]{2,1,0:T(8,128)(2,1)} %get-tuple-element.40), calls=%async_computation | async-start | bytes 4194304 | tf_op jit(solution)/shard_map/all_to_all | solution.py:319
  33.8 36.0 %collective-permute-start.4 = (bf16[1024,640]{1,0:T(8,128)(2,1)}, bf16[1024,640]{1,0:T(8,128)(2,1)}, u32[]{:S(2)}, u32[]{:S(2)}) collective-permute-start(bf16[1024,640]{1,0:T(8,128)(2,1)} %collective-permute-done.3.refs_5_), channel_id=1, source_target_pairs={{4,8},{8,4},{5,9},{9,5},{6,10},{10,6},{7,11},{11,7},{20,24},{24,20... | collective-permute-start | bytes 3932168 | tf_op jit(solution)/shard_map/ppermute | solution.py:324
  35.6 34.2 %collective-permute-start.6 = (bf16[1024,640]{1,0:T(8,128)(2,1)}, bf16[1024,640]{1,0:T(8,128)(2,1)}, u32[]{:S(2)}, u32[]{:S(2)}) collective-permute-start(bf16[1024,640]{1,0:T(8,128)(2,1)} %collective-permute-done.5.refs_6_), channel_id=1, source_target_pairs={{4,0},{8,12},{5,1},{9,13},{6,2},{10,14},{7,3},{11,15},{20,16},{24,... | collective-permute-start | bytes 3932168 | tf_op jit(solution)/shard_map/ppermute | solution.py:324
  42.4 13.1 %collective-permute-start = (bf16[128,2048]{1,0:T(8,128)(2,1)}, bf16[128,2048]{1,0:T(8,128)(2,1)S(1)}, u32[]{:S(2)}, u32[]{:S(2)}) collective-permute-start(bf16[128,2048]{1,0:T(8,128)(2,1)} %get-tuple-element.47), channel_id=1, source_target_pairs={{0,2},{2,0},{16,18},{18,16},{1,3},{3,1},{17,19},{19,17},{4,6},{6,4... | collective-permute-start | bytes 1572872 | tf_op jit(solution)/shard_map/ppermute | solution.py:44
  43.8 15.1 %collective-permute-start.1 = (bf16[128,2048]{1,0:T(8,128)(2,1)}, bf16[128,2048]{1,0:T(8,128)(2,1)S(1)}, u32[]{:S(2)}, u32[]{:S(2)}) collective-permute-start(bf16[128,2048]{1,0:T(8,128)(2,1)} %get-tuple-element.48), channel_id=1, source_target_pairs={{0,16},{2,18},{16,0},{18,2},{1,17},{3,19},{17,1},{19,3},{4,20},{6,... | collective-permute-start | bytes 1572872 | tf_op jit(solution)/shard_map/ppermute | solution.py:44
  44.4 24.1 %collective-permute-start.2 = (bf16[128,2048]{1,0:T(8,128)(2,1)}, bf16[128,2048]{1,0:T(8,128)(2,1)S(1)}, u32[]{:S(2)}, u32[]{:S(2)}) collective-permute-start(bf16[128,2048]{1,0:T(8,128)(2,1)} %get-tuple-element.49), channel_id=1, source_target_pairs={{0,18},{2,16},{16,2},{18,0},{1,19},{3,17},{17,3},{19,1},{4,22},{6,... | collective-permute-start | bytes 1572872 | tf_op jit(solution)/shard_map/ppermute | solution.py:44
  55.5 20.5 %collective-permute-start.9 = (bf16[4,128,2048]{2,1,0:T(8,128)(2,1)}, bf16[4,128,2048]{2,1,0:T(8,128)(2,1)S(1)}, u32[]{:S(2)}, u32[]{:S(2)}) collective-permute-start(bf16[4,128,2048]{2,1,0:T(8,128)(2,1)} %all-to-all-done.refs_0_), channel_id=1, source_target_pairs={{0,1},{1,0},{2,3},{3,2},{4,5},{5,4},{6,7},{7,6},{8,9},{9,8},{10,11... | collective-permute-start | bytes 6291464 | tf_op jit(solution)/shard_map/ppermute | solution.py:48
  69.8 6.2 %collective-permute-start.7 = (bf16[4,128,2048]{2,1,0:T(8,128)(2,1)S(1)}, bf16[4,128,2048]{2,1,0:T(8,128)(2,1)S(1)}, u32[]{:S(2)}, u32[]{:S(2)}) collective-permute-start(bf16[4,128,2048]{2,1,0:T(8,128)(2,1)S(1)} %pad_maximum_fusion.refs_1_.mine), channel_id=1, source_target_pairs={{0,1},{1,0},{2,3},{3,2},{4,5},{5,4},{6,7},{7,6},{8,9},{9,8},{10,11... | collective-permute-start | bytes 6291464 | tf_op jit(solution)/shard_map/ppermute | solution.py:48
  71.1 13.6 %collective-permute-start.8 = (bf16[1024,128]{1,0:T(8,128)(2,1)S(1)}, bf16[1024,128]{1,0:T(8,128)(2,1)S(1)}, u32[]{:S(2)}, u32[]{:S(2)}) collective-permute-start(bf16[1024,128]{1,0:T(8,128)(2,1)S(1)} %slice.26), channel_id=1, source_target_pairs={{4,0},{8,12},{5,1},{9,13},{6,2},{10,14},{7,3},{11,15},{20,16},{24,... | collective-permute-start | bytes 786440 | tf_op jit(solution)/shard_map/hop_ends/ppermute | solution.py:67
  74.7 30.1 %collective-permute-start.13 = (bf16[1024,512]{1,0:T(8,128)(2,1)}, bf16[1024,512]{1,0:T(8,128)(2,1)}, u32[]{:S(2)}, u32[]{:S(2)}) collective-permute-start(bf16[1024,512]{1,0:T(8,128)(2,1)} %slice.29), channel_id=1, source_target_pairs={{4,0},{8,12},{5,1},{9,13},{6,2},{10,14},{7,3},{11,15},{20,16},{24,... | collective-permute-start | bytes 3145736 | tf_op jit(solution)/shard_map/hop_ends/ppermute | solution.py:67
  88.4 14.0 %collective-permute-start.10 = (f32[256,128]{1,0:T(8,128)}, f32[256,128]{1,0:T(8,128)}, u32[]{:S(2)}, u32[]{:S(2)}) collective-permute-start(f32[256,128]{1,0:T(8,128)} %bitcast.11), channel_id=1, source_target_pairs={{0,2},{2,0},{16,18},{18,16},{1,3},{3,1},{17,19},{19,17},{4,6},{6,4... | collective-permute-start | bytes 393224 | tf_op jit(solution)/shard_map/ppermute | solution.py:44
  88.9 13.6 %collective-permute-start.11 = (f32[256,128]{1,0:T(8,128)}, f32[256,128]{1,0:T(8,128)}, u32[]{:S(2)}, u32[]{:S(2)}) collective-permute-start(f32[256,128]{1,0:T(8,128)} %bitcast.12), channel_id=1, source_target_pairs={{0,16},{2,18},{16,0},{18,2},{1,17},{3,19},{17,1},{19,3},{4,20},{6,... | collective-permute-start | bytes 393224 | tf_op jit(solution)/shard_map/ppermute | solution.py:44
  90.5 12.0 %collective-permute-start.12 = (f32[256,128]{1,0:T(8,128)}, f32[256,128]{1,0:T(8,128)}, u32[]{:S(2)}, u32[]{:S(2)}) collective-permute-start(f32[256,128]{1,0:T(8,128)} %bitcast.13), channel_id=1, source_target_pairs={{0,18},{2,16},{16,2},{18,0},{1,19},{3,17},{17,3},{19,1},{4,22},{6,... | collective-permute-start | bytes 393224 | tf_op jit(solution)/shard_map/ppermute | solution.py:44
  104.8 4.3 %collective-permute-start.14 = (bf16[256,128]{1,0:T(8,128)(2,1)S(1)}, bf16[256,128]{1,0:T(8,128)(2,1)S(1)}, u32[]{:S(2)}, u32[]{:S(2)}) collective-permute-start(bf16[256,128]{1,0:T(8,128)(2,1)S(1)} %fusion.2), channel_id=1, source_target_pairs={{0,2},{2,0},{1,3},{3,1},{4,6},{6,4},{5,7},{7,5},{8,10},{10,8},{9,1... | collective-permute-start | bytes 196616 | tf_op jit(solution)/shard_map/ppermute | solution.py:363
  109.1 14.1 %collective-permute-start.15 = (f32[2,256,256]{2,1,0:T(8,128)S(1)}, f32[2,256,256]{2,1,0:T(8,128)S(1)}, u32[]{:S(2)}, u32[]{:S(2)}) collective-permute-start(f32[2,256,256]{2,1,0:T(8,128)S(1)} %get-tuple-element.65), channel_id=1, source_target_pairs={{0,16},{2,18},{16,0},{18,2},{1,17},{3,19},{17,1},{19,3},{4,20},{6,... | collective-permute-start | bytes 1572872 | tf_op jit(solution)/shard_map/ppermute | solution.py:44
  110.8 8.3 %collective-permute-start.17 = (bf16[512,128]{1,0:T(8,128)(2,1)S(1)}, bf16[512,128]{1,0:T(8,128)(2,1)S(1)}, u32[]{:S(2)}, u32[]{:S(2)}) collective-permute-start(bf16[512,128]{1,0:T(8,128)(2,1)S(1)} %get-tuple-element.83), channel_id=1, source_target_pairs={{0,4},{4,8},{8,12},{12,0},{1,5},{5,9},{9,13},{13,1},{2,6},{6,10},{... | collective-permute-start | bytes 393224 | tf_op jit(solution)/shard_map/ppermute | solution.py:380
  114.0 9.0 %collective-permute-start.18 = (bf16[512,128]{1,0:T(8,128)(2,1)S(1)}, bf16[512,128]{1,0:T(8,128)(2,1)S(1)}, u32[]{:S(2)}, u32[]{:S(2)}) collective-permute-start(bf16[512,128]{1,0:T(8,128)(2,1)S(1)} %get-tuple-element.83), channel_id=1, source_target_pairs={{0,8},{4,12},{8,0},{12,4},{1,9},{5,13},{9,1},{13,5},{2,10},{6,14},... | collective-permute-start | bytes 393224 | tf_op jit(solution)/shard_map/ppermute | solution.py:380
  114.7 8.4 %collective-permute-start.19 = (bf16[512,128]{1,0:T(8,128)(2,1)S(1)}, bf16[512,128]{1,0:T(8,128)(2,1)S(1)}, u32[]{:S(2)}, u32[]{:S(2)}) collective-permute-start(bf16[512,128]{1,0:T(8,128)(2,1)S(1)} %get-tuple-element.83), channel_id=1, source_target_pairs={{0,12},{4,0},{8,4},{12,8},{1,13},{5,1},{9,5},{13,9},{2,14},{6,2},{... | collective-permute-start | bytes 393224 | tf_op jit(solution)/shard_map/ppermute | solution.py:380
  117.5 11.5 %collective-permute-start.21 = (f32[2,256,256]{2,1,0:T(8,128)S(1)}, f32[2,256,256]{2,1,0:T(8,128)S(1)}, u32[]{:S(2)}, u32[]{:S(2)}) collective-permute-start(f32[2,256,256]{2,1,0:T(8,128)S(1)} %get-tuple-element.71), channel_id=1, source_target_pairs={{0,2},{2,0},{16,18},{18,16},{1,3},{3,1},{17,19},{19,17},{4,6},{6,4... | collective-permute-start | bytes 1572872 | tf_op jit(solution)/shard_map/ppermute | solution.py:44
  123.1 7.2 %collective-permute-start.20 = (bf16[2048,128]{1,0:T(8,128)(2,1)S(1)}, bf16[2048,128]{1,0:T(8,128)(2,1)S(1)}, u32[]{:S(2)}, u32[]{:S(2)}) collective-permute-start(bf16[2048,128]{1,0:T(8,128)(2,1)S(1)} %constant_dynamic-update-slice_fusion.2.refs_6_), channel_id=1, source_target_pairs={{0,1},{1,0},{2,3},{3,2},{4,5},{5,4},{6,7},{7,6},{8,9},{9,8},{10,11... | collective-permute-start | bytes 1572872 | tf_op jit(solution)/shard_map/ppermute | solution.py:48
  124.1 9.8 %collective-permute-start.16 = (f32[256,256]{1,0:T(8,128)}, f32[256,256]{1,0:T(8,128)}, u32[]{:S(2)}, u32[]{:S(2)}) collective-permute-start(f32[256,256]{1,0:T(8,128)} %get-tuple-element.77), channel_id=1, source_target_pairs={{0,2},{2,0},{16,18},{18,16},{1,3},{3,1},{17,19},{19,17},{4,6},{6,4... | collective-permute-start | bytes 786440 | tf_op jit(solution)/shard_map/ppermute | solution.py:44
  129.8 8.7 %collective-permute-start.22 = (f32[256,256]{1,0:T(8,128)}, f32[256,256]{1,0:T(8,128)}, u32[]{:S(2)}, u32[]{:S(2)}) collective-permute-start(f32[256,256]{1,0:T(8,128)} %get-tuple-element.79), channel_id=1, source_target_pairs={{0,16},{2,18},{16,0},{18,2},{1,17},{3,19},{17,1},{19,3},{4,20},{6,... | collective-permute-start | bytes 786440 | tf_op jit(solution)/shard_map/ppermute | solution.py:44
  (20 other events, 121.8 us)
